TPU v7x, 32 devices: a whole 2x2x4 slice. The times are simulated.
32 devices in a mesh: dp: 8 (over y, x, core), shard: 4 (over z).
Axes of the slice: x: 2, y: 2, z: 4, core: 2. Of those that a mesh axis runs over, the one named last changes fastest.
Arguments:
- tokens: bfloat16 [32, 128, 2048], P(('dp', 'shard')), may hold values from -6 to 6
- segments: int32 [32, 128], P(('dp', 'shard')), may hold values from 0 to 5, never falling along the last dimension, each value on 1 to 64 neighbouring positions
- ln_gain: bfloat16 [2048], P('shard'), may hold values from 0.099609375 to 1.8984375
- ln_bias: bfloat16 [2048], P('shard'), may hold values from -1.75 to 1.75
- w_qkv: bfloat16 [2048, 6144], P('shard'), may hold values from -0.1875 to 0.1875
- b_qkv: bfloat16 [6144], P('shard'), may hold values from -1.75 to 1.75
- w_out: bfloat16 [2048, 2048], P('shard'), may hold values from -0.375 to 0.375
- b_out: bfloat16 [2048], P('shard'), may hold values from -1.75 to 1.75
- w_fc1: bfloat16 [2048, 8192], P('shard'), may hold values from -0.125 to 0.125
- b_fc1: bfloat16 [8192], P('shard'), may hold values from -1.75 to 1.75
- w_fc2: bfloat16 [8192, 2048], P('shard'), may hold values from -0.09375 to 0.09375
- b_fc2: bfloat16 [2048], P('shard'), may hold values from -1.75 to 1.75
- cotangent: bfloat16 [32, 128, 2048], P(('dp', 'shard')), may hold values from -6 to 6
Outputs:
- block_output: bfloat16 [32, 128, 2048], P(('dp', 'shard'))
- input_grad: float32 [32, 128, 2048], P(('dp', 'shard'))
- gain_grad: float32 [2048], P('shard')
- shift_grad: float32 [2048], P('shard')
- qkv_grad: float32 [2048, 6144], P('shard')
- qkv_bias_grad: float32 [6144], P('shard')
- out_grad: float32 [2048, 2048], P('shard')
- out_bias_grad: float32 [2048], P('shard')
- fc1_grad: float32 [2048, 8192], P('shard')
- fc1_bias_grad: float32 [8192], P('shard')
- fc2_grad: float32 [8192, 2048], P('shard')
- fc2_bias_grad: float32 [2048], P('shard')
Inputs may be any that keep to these rules, and one draw needn't show every extreme that they name: `segments`: within a sequence segment numbers never fall; each of the 6 documents has 1 to 64 tokens and one has exactly 64.
All inputs are finite; a program needn't handle non-finite values.
Results may differ from a plain program's by a relative error of at most 0.012.
The roundings to bfloat16 on the way count: a program that leaves them out, or rounds other values in their place, can miss the bound.
Values may be sent and summed in bfloat16 or wider, within the bound.
No kernel may reach another device: no remote copies, remote signals or barrier semaphores. Data moves between devices by JAX's collectives and lax.ppermute only.
A program may use at most 576 MiB of HBM per device.

v0:
```python
import math

import jax
import jax.numpy as jnp
from jax import lax
from jax.experimental import pallas as pl
from jax.experimental.pallas import tpu as pltpu
from jax.experimental.layout import Layout, with_layout_constraint
from jax.sharding import PartitionSpec as P

HEADS = 32
HEAD_DIM = 64
ROT = 32
CORES = 2
LANES = 128

epsilon = 1e-05
masked_value = -1e30
AXES = ("dp", "shard")
f32 = jnp.float32
bf16 = jnp.bfloat16
VMEM = 48 * 1024 * 1024


def rotary_tables(segments):
    seqs, length = segments.shape
    positions = jnp.broadcast_to(jnp.arange(length, dtype=jnp.int32), segments.shape)
    change = jnp.concatenate(
        [jnp.ones((seqs, 1), dtype=bool), segments[:, 1:] != segments[:, :-1]], axis=1
    )
    run_start = lax.cummax(jnp.where(change, positions, 0), axis=1)
    distance = (positions - run_start).astype(f32).reshape(-1, 1)
    lane = jnp.arange(LANES, dtype=jnp.int32) % HEAD_DIM
    half = ROT // 2
    frequency = jnp.exp((lane % half).astype(f32) * (-2.0 * math.log(10000.0) / ROT))
    angles = distance * frequency[None, :]
    sines = jnp.sin(angles)
    cos_table = jnp.where(lane < ROT, jnp.cos(angles), 1.0)
    low_table = jnp.where(lane < half, -sines, 0.0)
    high_table = jnp.where((lane >= half) & (lane < ROT), sines, 0.0)
    starts = jnp.broadcast_to(run_start.reshape(-1, 1), (seqs * length, LANES))
    return starts, cos_table, low_table, high_table


def attention_kernel(
    starts_ref, cos_ref, low_ref, high_ref, mixed_ref, outer_ref, context_ref, grad_ref
):
    length, width = outer_ref.shape
    half = ROT // 2
    scale = HEAD_DIM ** (-0.5)

    def wide(table):
        return jnp.concatenate([table[...]] * (width // LANES), axis=1)

    cos_table, low_table, high_table = wide(cos_ref), wide(low_ref), wide(high_ref)

    def rotate(v, sign):
        turned = pltpu.roll(v, width - half, 1) * low_table + pltpu.roll(v, half, 1) * high_table
        return v * cos_table + sign * turned

    queries = rotate(mixed_ref[:, :width], 1.0).astype(bf16)
    key_rows = rotate(mixed_ref[:, width : 2 * width], 1.0).astype(bf16)
    values = mixed_ref[:, 2 * width :].astype(bf16)
    outer = outer_ref[...]
    row = lax.broadcasted_iota(jnp.int32, (length, length), 0)
    column = lax.broadcasted_iota(jnp.int32, (length, length), 1)
    allowed = (column <= row) & (column >= starts_ref[...])
    spans = [slice(h * HEAD_DIM, (h + 1) * HEAD_DIM) for h in range(width // HEAD_DIM)]
    block = lambda x, h: x[h * length : (h + 1) * length]
    heads = range(len(spans))
    allowed = jnp.concatenate([allowed] * len(spans), axis=0)
    scores = jnp.concatenate([dot(queries[:, p], key_rows[:, p], ((1,), (1,))) for p in spans], axis=0)
    scores = jnp.where(allowed, scores * scale, masked_value)
    weights = jnp.exp(scores - jnp.max(scores, axis=1, keepdims=True))
    probs = weights / jnp.sum(weights, axis=1, keepdims=True)
    low = probs.astype(bf16)
    prob_grad = jnp.concatenate([dot(outer[:, p], values[:, p], ((1,), (1,))) for p in spans], axis=0)
    inner = jnp.sum(prob_grad * probs, axis=1, keepdims=True)
    score_grad = (probs * (prob_grad - inner)).astype(bf16)
    context = [dot(block(low, h), values[:, spans[h]], ((1,), (0,))) for h in heads]
    value_grad = [dot(block(low, h), outer[:, spans[h]], ((0,), (0,))) for h in heads]
    query_grad = [dot(block(score_grad, h), key_rows[:, spans[h]], ((1,), (0,))) for h in heads]
    key_grad = [dot(block(score_grad, h), queries[:, spans[h]], ((0,), (0,))) for h in heads]
    side = lambda x: jnp.concatenate(x, axis=1)
    context_ref[...] = side(context).astype(bf16)
    grad_ref[:, :width] = rotate(side(query_grad) * scale, -1.0).astype(bf16)
    grad_ref[:, width : 2 * width] = rotate(side(key_grad) * scale, -1.0).astype(bf16)
    grad_ref[:, 2 * width :] = side(value_grad).astype(bf16)


def attention(tables, mixed, outer, length):
    rows, width = outer.shape
    wide = lambda columns: pl.BlockSpec((length, columns), lambda i: (i, 0))
    return pl.pallas_call(
        attention_kernel,
        grid=(rows // length,),
        in_specs=[wide(LANES)] * 4 + [wide(3 * width), wide(width)],
        out_specs=[wide(width), wide(3 * width)],
        out_shape=[
            jax.ShapeDtypeStruct((rows, width), bf16),
            jax.ShapeDtypeStruct((rows, 3 * width), bf16),
        ],
        cost_estimate=pl.CostEstimate(flops=4 * 10**9, bytes_accessed=0, transcendentals=0),
        compiler_params=pltpu.CompilerParams(vmem_limit_bytes=VMEM),
    )(*tables, mixed, outer)


def call(kernel, grid, in_specs, out_specs, out_shape, scalars=0, us=0, **more):
    return pl.pallas_call(
        kernel,
        grid_spec=pltpu.PrefetchScalarGridSpec(
            num_scalar_prefetch=scalars, grid=grid, in_specs=in_specs, out_specs=out_specs
        ),
        out_shape=out_shape,
        cost_estimate=pl.CostEstimate(flops=us * 10**9 // 3, bytes_accessed=0, transcendentals=0),
        compiler_params=pltpu.CompilerParams(vmem_limit_bytes=VMEM),
        **more,
    )


def dot(a, b, dims):
    return lax.dot_general(a, b, (dims, ((), ())), preferred_element_type=f32)


def pack(w_fc1, w_qkv, row, core, planes, part, own, piece):
    third = w_qkv.shape[1] // 3 // piece
    cols = own + 3 * piece
    spots = jnp.stack([row, core]).astype(jnp.int32)

    def kernel(spots_ref, fc1_ref, q_ref, k_ref, v_ref, out_ref):
        out_ref[:, :own] = fc1_ref[...]
        for i, ref in enumerate((q_ref, k_ref, v_ref)):
            out_ref[:, own + i * piece : own + (i + 1) * piece] = ref[...]

    cut = lambda i: pl.BlockSpec(
        (part, piece), lambda p, spots: (spots[0], i * third + p * CORES + spots[1])
    )
    return call(
        kernel,
        (planes,),
        [
            pl.BlockSpec((part, own), lambda p, spots: (spots[0], p * CORES + spots[1])),
            cut(0),
            cut(1),
            cut(2),
        ],
        pl.BlockSpec((None, part, cols), lambda p, spots: (p, 0, 0)),
        jax.ShapeDtypeStruct((planes, part, cols), bf16),
        scalars=1,
    )(spots, w_fc1, w_qkv, w_qkv, w_qkv)


def assemble(w_fc1, w_qkv, arrays, order, spots, own, piece, blocks, before=None):
    others, rows, cols = arrays[0].shape
    planes = others + 1
    height = w_fc1.shape[0]
    third = w_qkv.shape[1] // 3 // piece

    def kernel(order_ref, spots_ref, fc1_ref, q_ref, k_ref, v_ref, *refs):
        fc1_out, qkv_out = refs[-2:]
        here = spots_ref[0]
        fc1_out[here] = fc1_ref[...]
        for i, ref in enumerate((q_ref, k_ref, v_ref)):
            qkv_out[here, :, i * piece : (i + 1) * piece] = ref[...]
        for n in range(len(arrays)):

            @pl.when(pl.program_id(0) == n)
            def _(ref=refs[n]):
                for k in range(1, planes):
                    there = spots_ref[k]
                    fc1_out[there] = ref[k - 1, :, :own]
                    qkv_out[there] = ref[k - 1, :, own:]

    cut = lambda i: pl.BlockSpec(
        (None, rows, piece), lambda n, order, spots: (order[n], 0, i * third + spots[planes])
    )
    result = lambda size: pl.BlockSpec(
        (planes, None, rows, size), lambda n, order, spots: (0, order[n], 0, 0)
    )
    more = {}
    if before is not None:
        first = 6 + len(arrays)
        more["input_output_aliases"] = {first: 0, first + 1: 1}
    return call(
        kernel,
        (len(arrays),),
        [
            pl.BlockSpec((None, rows, own), lambda n, order, spots: (order[n], 0, spots[planes])),
            cut(0),
            cut(1),
            cut(2),
        ]
        + [pl.BlockSpec(x.shape, lambda n, order, spots: (0, 0, 0)) for x in arrays]
        + [pl.BlockSpec(memory_space=pl.ANY)] * (0 if before is None else 2),
        [result(own), result(3 * piece)],
        [
            jax.ShapeDtypeStruct((planes, blocks, rows, own), bf16),
            jax.ShapeDtypeStruct((planes, blocks, rows, 3 * piece), bf16),
        ],
        scalars=2,
        **more,
    )(
        order,
        spots,
        w_fc1.reshape(blocks, rows, -1),
        *[w_qkv.reshape(blocks, rows, -1)] * 3,
        *arrays,
        *(before or ()),
    )


def norm(arrays, places, gain, shift, blocks, before=None):
    rows, width = arrays[0].shape[0] // 2, arrays[0].shape[1]

    def kernel(places_ref, gain_ref, shift_ref, *refs):
        out_ref, tokens_ref, cot_ref, mean_ref, inverse_ref = refs[-5:]
        for n in range(len(arrays)):

            @pl.when(pl.program_id(0) == n)
            def _(ref=refs[n]):
                tokens_ref[...] = ref[:rows]
                cot_ref[...] = ref[rows:]
                x = ref[:rows].astype(f32)
                mean = jnp.mean(x, axis=1, keepdims=True)
                centred = x - mean
                inverse = lax.rsqrt(jnp.mean(centred * centred, axis=1, keepdims=True) + epsilon)
                out_ref[...] = (centred * inverse * gain_ref[...] + shift_ref[...]).astype(bf16)
                mean_ref[...] = jnp.broadcast_to(mean, mean_ref.shape)
                inverse_ref[...] = jnp.broadcast_to(inverse, inverse_ref.shape)

    line = pl.BlockSpec((1, width), lambda i, places: (0, 0))
    wide = pl.BlockSpec((rows, width), lambda i, places: (places[i], 0))
    slim = pl.BlockSpec((rows, LANES), lambda i, places: (places[i], 0))
    more = {}
    if before is not None:
        more["input_output_aliases"] = {3 + len(arrays) + i: i for i in range(5)}
    return call(
        kernel,
        (len(arrays),),
        [line, line]
        + [pl.BlockSpec(x.shape, lambda i, places: (0, 0)) for x in arrays]
        + [pl.BlockSpec(memory_space=pl.ANY)] * (0 if before is None else 5),
        [wide, wide, wide, slim, slim],
        [jax.ShapeDtypeStruct((blocks * rows, width), bf16)] * 3
        + [jax.ShapeDtypeStruct((blocks * rows, LANES), f32)] * 2,
        scalars=1,
        **more,
    )(
        jnp.asarray(places, jnp.int32),
        gain.reshape(1, width),
        shift.reshape(1, width),
        *arrays,
        *(before or ()),
    )


def join(*lists):
    shape = lists[0][0].shape[1:]
    spans, arrays, total = [], [], 0
    for some in lists:
        start = total
        for x in some:
            arrays.append((total, x))
            total += x.shape[0]
        spans.append((start, total - start))

    def kernel(*refs):
        here = pl.program_id(0)
        for n, (start, x) in enumerate(arrays):
            for out, (first, count) in zip(refs[len(arrays) :], spans):
                if first <= start < first + count:

                    @pl.when((here >= start) & (here < start + x.shape[0]))
                    def _(ref=refs[n], out=out):
                        out[...] = ref[...]

    def spec(first, count):
        return pl.BlockSpec(
            (None,) + shape,
            lambda i: (jnp.clip(i - first, 0, count - 1),) + (0,) * len(shape),
        )

    results = call(
        kernel,
        (total,),
        [spec(start, x.shape[0]) for start, x in arrays],
        [spec(*span) for span in spans],
        [jax.ShapeDtypeStruct((count,) + shape, arrays[0][1].dtype) for _, count in spans],
        us=3,
    )(*[x for _, x in arrays])
    return results if len(lists) > 1 else results[0]


def add_in_order(mine, came, order):
    count = order.shape[0]
    rows, width = mine.shape[0] // count, mine.shape[1]

    def kernel(order_ref, mine_ref, came_ref, out_ref):
        out_ref[...] = (mine_ref[...] + came_ref[...].astype(f32)).astype(bf16)

    block = pl.BlockSpec((rows, width), lambda i, order: (i, 0))
    return call(
        kernel,
        (count,),
        [block, block],
        pl.BlockSpec((None, rows, width), lambda i, order: (order[i], 0, 0)),
        jax.ShapeDtypeStruct((count, rows, width), bf16),
        scalars=1,
        us=5,
    )(order, mine, came)


def branches(context, out_rows, active, fc2_rows):
    total, width = context.shape[0], out_rows.shape[1]
    half, block = total // 2, 256

    def kernel(context_ref, out_ref, active_ref, fc2_ref, mine_ref, other_ref):
        y = dot(context_ref[...], out_ref[...], ((1,), (0,)))
        y = y + dot(active_ref[...], fc2_ref[...], ((1,), (0,)))
        mine_ref[...] = y[:half]
        other_ref[...] = y[half:].astype(bf16)

    whole = lambda x: pl.BlockSpec(x.shape, lambda i: (0, 0))
    part = lambda rows: pl.BlockSpec((rows, block), lambda i: (0, i))
    return call(
        kernel,
        (width // block,),
        [whole(context), part(out_rows.shape[0]), whole(active), part(fc2_rows.shape[0])],
        [part(half), part(half)],
        [jax.ShapeDtypeStruct((half, width), f32), jax.ShapeDtypeStruct((half, width), bf16)],
        us=10,
    )(context, out_rows, active, fc2_rows)


def backs(hidden_grad, fc1_cols, mixed_grad, qkv_cols, tokens, mean, inverse):
    total, width = mean.shape[0], fc1_cols.shape[0]
    half, block = total // 2, 256

    def kernel(
        hidden_ref, fc1_ref, mixed_ref, qkv_ref, tokens_ref, mean_ref, inverse_ref,
        first_ref, second_ref, sums_ref,
    ):
        y = dot(hidden_ref[...], fc1_ref[...], ((1,), (1,)))
        y = y + dot(mixed_ref[...], qkv_ref[...], ((1,), (1,)))
        first_ref[...] = y[:half]
        second_ref[...] = y[half:].astype(bf16)
        normed = (tokens_ref[...].astype(f32) - mean_ref[:, :1]) * inverse_ref[:, :1]
        sums_ref[0:1, :] = jnp.sum(y * normed, axis=0, keepdims=True)
        sums_ref[1:2, :] = jnp.sum(y, axis=0, keepdims=True)
        sums_ref[2:8, :] = jnp.zeros((6, block), f32)

    whole = lambda x: pl.BlockSpec(x.shape, lambda i: (0, 0))
    part = lambda rows: pl.BlockSpec((rows, block), lambda i: (0, i))
    rhs = lambda x: pl.BlockSpec((block, x.shape[1]), lambda i: (i, 0))
    return call(
        kernel,
        (width // block,),
        [
            whole(hidden_grad),
            rhs(fc1_cols),
            whole(mixed_grad),
            rhs(qkv_cols),
            part(total),
            whole(mean),
            whole(inverse),
        ],
        [part(half), part(half), part(8)],
        [
            jax.ShapeDtypeStruct((half, width), f32),
            jax.ShapeDtypeStruct((half, width), bf16),
            jax.ShapeDtypeStruct((8, width), f32),
        ],
        us=14,
    )(hidden_grad, fc1_cols, mixed_grad, qkv_cols, tokens, mean, inverse)


def place_columns(net, mine, other, factor):
    J, planes = net.J, net.S
    _, rows, columns = mine[0].shape
    piece = columns // planes
    spots = jnp.concatenate([net.order(), jnp.stack([net.c, 1 - net.c])]).astype(jnp.int32)
    high = rows // 2

    def kernel(spots_ref, m0_ref, m1_ref, o0_ref, o1_ref, out_ref):
        here = pl.program_id(0)
        for e, (place, refs) in enumerate(
            ((net.mine, (m0_ref, m1_ref)), (net.theirs, (o0_ref, o1_ref)))
        ):
            last, _ = place(here)
            for ref, chosen in zip(refs, (jnp.logical_not(last), last)):

                @pl.when(chosen)
                def _(e=e, ref=ref):
                    for k in range(planes):
                        column = (k * CORES + spots_ref[J + e]) * piece
                        out_ref[:, pl.ds(pl.multiple_of(column, LANES), piece)] = (
                            ref[:, k * piece : (k + 1) * piece].astype(f32) * factor
                        )

    return call(
        kernel,
        (J, 2),
        [
            pl.BlockSpec(
                (None, high, columns), lambda i, h, spots, place=place, n=n: (place(i)[1][n], h, 0)
            )
            for place in (net.mine, net.theirs)
            for n in range(2)
        ],
        pl.BlockSpec((high, 2 * columns), lambda i, h, spots: (spots[i] * 2 + h, 0)),
        jax.ShapeDtypeStruct((J * rows, 2 * columns), f32),
        scalars=1,
        us=11,
    )(spots, *mine, *other)


def place_mixed(net, mine, other, factor):
    J, planes = net.J, net.S
    _, part, columns = mine[0].shape
    piece = columns // planes // 4
    width = planes * CORES * piece
    spots = jnp.concatenate([net.order(), jnp.stack([net.c, 1 - net.c])]).astype(jnp.int32)

    def kernel(spots_ref, m0_ref, m1_ref, o0_ref, o1_ref, qkv_ref, out_ref):
        here = pl.program_id(0)
        for e, (place, refs) in enumerate(
            ((net.mine, (m0_ref, m1_ref)), (net.theirs, (o0_ref, o1_ref)))
        ):
            last, _ = place(here)
            core = spots_ref[J + e]
            for ref, chosen in zip(refs, (jnp.logical_not(last), last)):
                for k in range(planes):

                    @pl.when(chosen & (pl.program_id(1) == k))
                    def _(k=k, core=core, ref=ref):
                        for i in range(3):
                            start = (4 * k + i) * piece
                            column = ((i * planes + k) * CORES + core) * piece
                            qkv_ref[:, pl.ds(pl.multiple_of(column, LANES), piece)] = (
                                ref[:, start : start + piece].astype(f32) * factor
                            )
                        block = ref[:, (4 * k + 3) * piece : (4 * k + 4) * piece].astype(f32)
                        out_ref[pl.ds(pl.multiple_of(core * piece, LANES), piece), :] = (
                            block * factor
                        ).T

    if part % LANES == 0:
        out_shape = (CORES * piece, planes * J * part)
        out_spec = pl.BlockSpec((CORES * piece, part), lambda i, k, spots: (0, k * J + spots[i]))
    else:
        out_shape = (planes, J, CORES * piece, part)
        out_spec = pl.BlockSpec(
            (None, None, CORES * piece, part), lambda i, k, spots: (k, spots[i], 0, 0)
        )
    return call(
        kernel,
        (J, planes),
        [
            pl.BlockSpec(
                (None, part, columns), lambda i, k, spots, place=place, n=n: (place(i)[1][n], 0, 0)
            )
            for place in (net.mine, net.theirs)
            for n in range(2)
        ],
        [pl.BlockSpec((part, 3 * width), lambda i, k, spots: (spots[i], 0)), out_spec],
        [
            jax.ShapeDtypeStruct((width // planes, 3 * width), f32),
            jax.ShapeDtypeStruct(out_shape, f32),
        ],
        scalars=1,
        us=16,
    )(spots, *mine, *other)


def place_rows(net, mine, other, factor):
    J = net.J
    _, rows, columns = mine[0].shape
    spots = jnp.concatenate([net.c * J + net.order(), (1 - net.c) * J + net.order(other=True)])
    arrays = (*mine, *other) if net.square else (mine[0], other[0])
    starts = [sum(x.shape[0] for x in arrays[:n]) for n in range(len(arrays))]

    def kernel(spots_ref, *refs):
        here = pl.program_id(0)
        for start, x, ref in zip(starts, arrays, refs):

            @pl.when((here >= start) & (here < start + x.shape[0]))
            def _(ref=ref):
                refs[-1][...] = ref[...].astype(f32) * factor

    def spec(start, count):
        return pl.BlockSpec(
            (None, rows, columns), lambda i, spots: (jnp.clip(i - start, 0, count - 1), 0, 0)
        )

    return call(
        kernel,
        (2 * J,),
        [spec(start, x.shape[0]) for start, x in zip(starts, arrays)],
        pl.BlockSpec((rows, columns), lambda i, spots: (spots[i], 0)),
        jax.ShapeDtypeStruct((2 * J * rows, columns), f32),
        scalars=1,
        us=12,
    )(spots.astype(jnp.int32), *arrays)


def tie(x, *after):
    return lax.optimization_barrier((x, after))[0]


class Links:
    def __init__(self, planes, replicas):
        self.S = planes
        self.J = replicas // CORES
        self.square = self.J == 4
        dp = lax.axis_index("dp")
        self.s = lax.axis_index("shard")
        self.c = dp % CORES
        self.j = dp // CORES
        self.first = jnp.where(self.c == 0, 2, 1)

    def move(self, x, ds=0, dc=0, steps=None):
        pairs = []
        for j in range(self.J):
            for c in range(CORES):
                for s in range(self.S):
                    turn = 0 if steps is None else (2, 1)[(c + steps) % 2]
                    to = ((j ^ turn) * CORES + (c + dc) % CORES) * self.S + (s + ds) % self.S
                    pairs.append(((j * CORES + c) * self.S + s, to))
        return lax.ppermute(x, AXES, pairs)

    def groups(self):
        return [[j * CORES + c for j in range(self.J)] for c in range(CORES)]

    def order(self, other=False):
        if not self.square:
            return jnp.arange(self.J)
        turn = 3 - self.first if other else self.first
        return jnp.stack([self.j, self.j ^ turn, self.j ^ 3 ^ turn, self.j ^ 3])

    def mine(self, i):
        return (i >= 2, (jnp.minimum(i, 1), jnp.maximum(i - 2, 0))) if self.square else (i < 0, (i, 0))

    def theirs(self, i):
        return (i % 2 == 1, (i // 2, i // 2)) if self.square else (i < 0, (i, 0))

    def gather(self, x):
        return self.move(x, steps=0) if self.square else None

    def gather_more(self, stack):
        return self.move(stack, steps=1) if self.square else None

    def spread(self, x):
        if not self.square:
            return x
        other = self.j ^ self.first
        return jnp.stack([pick(x, other, 1), pick(x, other ^ 3 ^ self.first, 1)])

    def spread_sum(self, x, got):
        if not self.square:
            return x, x
        mine = pick(x, self.j, 1), pick(x, self.j ^ 3 ^ self.first, 1)
        return [(m.astype(f32) + g.astype(f32)).astype(bf16) for m, g in zip(mine, got)]

    def spread_last(self, own, got):
        if not self.square:
            return lax.psum_scatter(
                own.astype(f32),
                "dp",
                scatter_dimension=1,
                axis_index_groups=self.groups(),
                tiled=False,
            ).astype(bf16)
        return (own.astype(f32) + got.astype(f32)).astype(bf16)

    def plane_sum(self, x, step):
        if not self.square:
            return lax.psum(x, "dp", axis_index_groups=self.groups()) if step else x
        return x + self.move(x, steps=step)


def swap(x, after=()):
    return lax.all_to_all(tie(x, *after), "shard", 0, 0, tiled=True)


def twofold(x, axis):
    high = lax.reduce_precision(x, 8, 7)
    return jnp.concatenate([high.astype(bf16), (x - high).astype(bf16)], axis=axis)


def as_rows(vector, width, multiple):
    count = -(-vector.shape[0] // (width * multiple)) * multiple
    return jnp.pad(vector, (0, count * width - vector.shape[0])).reshape(count, width)


def pick(x, index, axis):
    return lax.dynamic_index_in_dim(x, index, axis, keepdims=False)


def in_order(held, here):
    size = len(held)
    backwards = jnp.stack(held[::-1])
    return lax.dynamic_slice_in_dim(
        jnp.concatenate([backwards, backwards]), size - 1 - here, size, 0
    )


def local(
    tokens,
    segments,
    ln_gain,
    ln_bias,
    w_qkv,
    b_qkv,
    w_out,
    b_out,
    w_fc1,
    b_fc1,
    w_fc2,
    b_fc2,
    cotangent,
):
    planes = lax.axis_size("shard")
    replicas = lax.axis_size("dp")
    net = Links(planes, replicas)
    S, J, c, j, s = net.S, net.J, net.c, net.j, net.s
    seqs, length, width = tokens.shape
    rows = seqs * length
    ff = w_fc1.shape[1]
    ff_own = ff // (S * CORES)
    mix_own = width // (S * CORES)
    height = width // S
    part = height // J
    total = S * CORES * rows
    back_planes = (s - jnp.arange(S)) % S
    factor = 1.0 / math.sqrt(rows * planes * replicas)

    own_tokens = tokens.reshape(rows, width)
    own_cot = cotangent.reshape(rows, width)
    hops = [jnp.concatenate([own_tokens, own_cot])]
    hops.append(net.move(hops[0], ds=1))

    vectors = [ln_gain, ln_bias, b_qkv, b_out, b_fc1, b_fc2, segments.reshape(-1).astype(bf16)]
    small = jnp.concatenate(vectors)
    size = small.shape[0]
    held = [small] + [net.move(small, ds=k) for k in range(1, S)]

    got = swap(pack(w_fc1, w_qkv, j, c, S, part, ff_own, mix_own))
    others = [net.move(tie(hops[0], hops[1], held), dc=1), net.move(hops[1], dc=1)]
    fc2_rows = lax.dynamic_slice_in_dim(w_fc2, c * ff_own, ff_own, 0)
    out_rows = lax.dynamic_slice_in_dim(w_out, c * mix_own, mix_own, 0)
    marks = jnp.stack([v[size - rows :] for v in held])
    small_all = in_order(held, s)
    whole = []
    start = 0
    for vector in vectors[:-1]:
        whole.append(small_all[:, start : start + vector.shape[0]].reshape(-1).astype(f32))
        start += vector.shape[0]
    gain_full, shift_full, qkv_bias, out_bias, fc1_bias, fc2_bias = whole
    fc1_bias = lax.dynamic_slice_in_dim(fc1_bias, (s * CORES + c) * ff_own, ff_own, 0)
    qkv_bias = lax.dynamic_slice_in_dim(
        qkv_bias.reshape(3, width), (s * CORES + c) * mix_own, mix_own, 1
    ).reshape(-1)
    marks = jnp.stack([marks, net.move(tie(marks, hops[1], held), dc=1)])
    tables = rotary_tables(marks.reshape(-1, length).astype(jnp.int32))
    ready = tie((hops[1], others, fc2_rows, out_rows, tables, gain_full, fc1_bias, qkv_bias), hops[1])
    hop, others, fc2_rows, out_rows, tables, gain_full, fc1_bias, qkv_bias = ready

    got = tie(got, hop, others, fc2_rows, out_rows, tables, gain_full, fc1_bias, qkv_bias)
    block = jnp.concatenate([pick(got, back_planes[k], 0) for k in range(1, S)])[None]
    hops.append(net.move(tie(hop, got), ds=1))
    came = net.gather(block)
    if net.square:
        blocks = tie(join([block, came]))
    else:
        blocks = lax.all_gather(block[0], "dp", axis_index_groups=net.groups())
    came = net.gather_more(blocks)
    while len(hops) < S:
        hops.append(net.move(tie(hops[-1], blocks), ds=1))
        others.append(net.move(tie(hops[-2], blocks), dc=1))
    places = [e * S + k for k in range(S) for e in range(CORES)]
    early = [x for pair in zip(hops[: S - 1], others[: S - 1]) for x in pair]
    early = tie(early, blocks)
    normed_rows = norm(early, places[:-CORES], gain_full, shift_full, S * CORES)
    last = tie(hops[-1], normed_rows)
    others.append(net.move(last, dc=1))
    blocks = tie(blocks, normed_rows)
    spots_w = jnp.concatenate([back_planes, (s * CORES + c)[None]]).astype(jnp.int32)
    chips = net.order()
    weights = lambda x, order, *before: assemble(
        w_fc1,
        w_qkv,
        [y.reshape(S - 1, part, -1) for y in x],
        order.astype(jnp.int32),
        spots_w,
        ff_own,
        mix_own,
        J,
        *before,
    )
    weight_cols = weights(blocks, chips[: blocks.shape[0]])
    last, other = tie((last, others[-1]), weight_cols)
    hidden_in, tok_rows, cot_rows, mean, inverse = norm(
        [last, other], places[-CORES:], gain_full, shift_full, S * CORES, normed_rows
    )
    if net.square:
        weight_cols, came = tie((weight_cols, came), hidden_in)
        weight_cols = weights(came, chips[2:], weight_cols)
    fc1_cols = weight_cols[0].reshape(width, ff_own)
    qkv_cols = weight_cols[1].reshape(width, 3 * mix_own)

    hidden = jnp.dot(hidden_in, fc1_cols, preferred_element_type=f32) + fc1_bias
    active, gelu_back = jax.vjp(lambda v: jax.nn.gelu(v, approximate=True), hidden)
    active = active.astype(bf16)
    transposed = lambda x, y: jnp.einsum("td,te->de", x, y, preferred_element_type=f32).astype(bf16)
    fc2_term = transposed(active, cot_rows)

    mark = []

    def step(x, *made):
        nonlocal mark
        if not made:
            return tie(x, mark)
        mark = list(made)
        return x

    def first_sum(x):
        sent = tie(net.spread(x))
        step(None, sent)
        return x, net.gather(sent)

    def second_sum(x, got):
        x, got = step((x, got))
        own, sent = tie(net.spread_sum(x, got))
        step(None, own, sent)
        return own, net.gather_more(sent)

    def last_sum(own, got):
        part = tie(net.spread_last(*step((own, got))))
        step(None, part)
        return part

    def second_gather(part, came):
        part, came = step((part, came))
        if net.square:
            stack = join([part[None], came[None]])
        else:
            stack = lax.all_gather(part, "dp", axis_index_groups=net.groups())
        stack = tie(stack)
        step(None, stack)
        return stack, net.gather_more(stack)

    def to_other(x):
        return net.move(step(x), dc=1) if net.square else x

    fc2_own, fc2_got = first_sum(fc2_term.reshape(1, J, ff_own // J, width))
    late_cot = step(cot_rows)
    active_grad = jnp.einsum("td,fd->tf", late_cot, fc2_rows, preferred_element_type=f32)
    hidden_grad = gelu_back(active_grad)[0].astype(bf16)
    fc1_term = transposed(hidden_in, hidden_grad)
    fc1_own, fc1_got = first_sum(fc1_term.reshape(S, J, part, ff_own))
    fc2_own, fc2_got = second_sum(fc2_own, fc2_got)
    late_in, late_cot = step((hidden_in, cot_rows))
    mixed = jnp.dot(late_in, qkv_cols, preferred_element_type=f32) + qkv_bias
    context_grad = jnp.einsum("te,de->td", late_cot, out_rows, preferred_element_type=f32).astype(
        bf16
    )
    context, mixed_grad = attention(tables, mixed, context_grad, length)
    step(None, context, mixed_grad)
    fc1_own, fc1_got = second_sum(fc1_own, fc1_got)
    fc2_part = last_sum(fc2_own, fc2_got)[0]
    fc2_came = net.gather(fc2_part)
    late_in, late_cot, late_mixed, late_context = step((hidden_in, cot_rows, mixed_grad, context))
    mixed_term = with_layout_constraint(
        jnp.concatenate(
            [transposed(late_in, late_mixed), transposed(late_cot, late_context)], axis=1
        ),
        Layout((0, 1)),
    )
    mixed_own, mixed_got = first_sum(mixed_term.reshape(S, J, part, 4 * mix_own))
    fc1_part = last_sum(fc1_own, fc1_got)
    fc1_part = swap(fc1_part)
    fc2_part, fc2_came = second_gather(fc2_part, fc2_came)
    fc2_other = net.move(fc2_part, dc=1)
    late_context, late_active = step((context, active))
    branch, branch_other = branches(late_context, out_rows, late_active, fc2_rows)
    step(None, branch, branch_other)
    branch_came = net.move(branch_other, dc=1)
    late_mixed, late_grad = step((mixed_grad, hidden_grad))
    back, back_other, norm_sums = backs(
        late_grad, fc1_cols, late_mixed, qkv_cols, tok_rows, mean, inverse
    )
    step(None, back, back_other, norm_sums)
    back_came = net.move(back_other, dc=1)
    scatter = lambda x: lax.psum_scatter(x, "shard", scatter_dimension=0, tiled=True)[0]
    late_grad, late_mixed, late_cot, norm_sums = step((hidden_grad, mixed_grad, cot_rows, norm_sums))
    mixed_sums = jnp.sum(late_mixed, axis=0, dtype=f32)
    norm_sums = jnp.swapaxes(norm_sums[:2].reshape(2, S, height), 0, 1).reshape(S, -1)
    riders = jnp.concatenate([norm_sums, jnp.broadcast_to(mixed_sums, (S, 3 * mix_own))], axis=1)
    riding = riders.shape[1]
    riders = jnp.pad(riders, ((0, 0), (0, -riding % (24 * mix_own))))
    riders = twofold(riders.reshape(S, -1, 3 * mix_own), 1)
    column_sums = jnp.concatenate(
        [
            jnp.sum(late_grad, axis=0, dtype=f32),
            pick(jnp.sum(late_cot, axis=0, dtype=f32).reshape(S, height), s, 0),
        ]
    )
    riders, column_sums = tie((riders, column_sums))
    step(None, riders, column_sums)
    mixed_own, mixed_got = second_sum(mixed_own, mixed_got)
    fc1_part, fc2_came = step((fc1_part, fc2_came))
    fc1_part = tie(jnp.swapaxes(fc1_part, 0, 1).reshape(part, S * ff_own))
    step(None, fc1_part)
    fc1_came = net.gather(fc1_part)
    branch_acts = add_in_order(*step((branch, branch_came)), back_planes.astype(jnp.int32))
    back_acts = add_in_order(*step((back, back_came)), back_planes.astype(jnp.int32))
    mark += [branch_acts, back_acts]
    fc1_part, fc1_came = second_gather(fc1_part, fc1_came)
    branch_sum, back_sum = scatter(branch_acts), scatter(back_acts)
    mixed_part = last_sum(mixed_own, mixed_got)
    out_part = mixed_part[:, :, 3 * mix_own :]
    mixed_part = tie(jnp.concatenate([mixed_part[:, :, : 3 * mix_own], riders], axis=1))
    step(None, mixed_part)
    mixed_part = swap(mixed_part)
    fc1_other = net.move(step(fc1_part), dc=1)
    if net.square:
        fc2_last = net.move(step(fc2_came), dc=1)
        fc1_came = step(fc1_came)
        mark += [fc1_came]
    mixed_part = step(mixed_part)
    riders = mixed_part[:, part:].astype(f32)
    mixed_part = jnp.concatenate([mixed_part[:, :part], out_part], axis=2)
    mixed_part = tie(jnp.swapaxes(mixed_part, 0, 1).reshape(part, S * 4 * mix_own))
    step(None, mixed_part)
    mixed_came = net.gather(mixed_part)
    if net.square:
        fc1_last = net.move(step(fc1_came), dc=1)
        fc2_mine, fc2_other = (fc2_part, fc2_came), (fc2_other, fc2_last)
    else:
        fc2_mine, fc2_other = (fc2_part, fc2_part), (fc2_other, fc2_other)
    count = riders.shape[1] // 2
    riders = step(riders)
    riders = (riders[:, :count] + riders[:, count:]).reshape(S, -1)[:, :riding]
    sums = jnp.concatenate(
        [
            jnp.sum(riders[:, : 2 * height], axis=0),
            column_sums[:ff_own],
            riders[:, 2 * height :].reshape(-1),
            column_sums[ff_own:],
        ]
    )
    sums = tie(sums)
    step(None, sums)
    sums = net.plane_sum(sums, 0)
    fc2_own = place_rows(net, *step((fc2_mine, fc2_other)), factor)
    step(None, fc2_own)
    mixed_part, mixed_came = second_gather(mixed_part, mixed_came)
    mixed_other = net.move(mixed_part, dc=1)
    if net.square:
        fc1_mine, fc1_other = (fc1_part, fc1_came), (fc1_other, fc1_last)
    else:
        fc1_mine, fc1_other = (fc1_part, fc1_part), (fc1_other, fc1_other)
    fc1_own = place_columns(net, *step((fc1_mine, fc1_other)), factor)
    step(None, fc1_own)
    if net.square:
        mixed_came = tie(step(mixed_came))
        mixed_last = net.move(mixed_came, dc=1)
        mixed_mine, mixed_other = (mixed_part, mixed_came), (mixed_other, mixed_last)
    else:
        mixed_mine, mixed_other = (mixed_part, mixed_part), (mixed_other, mixed_other)
    sums = net.plane_sum(tie(sums, mixed_mine), 1)
    sums_came = net.move(sums, dc=1)
    qkv_own, out_own = place_mixed(net, mixed_mine, mixed_other, factor)
    if out_own.ndim == 4:
        out_own = jnp.transpose(out_own, (2, 0, 1, 3)).reshape(height, width)

    own_inputs = own_tokens.astype(f32)
    output = (own_inputs + branch_sum.astype(f32) + (out_bias + fc2_bias)).astype(bf16)
    normed = (own_inputs - mean[:rows, :1]) * inverse[:rows, :1]
    scaled = back_sum.astype(f32) * gain_full
    input_grad = own_cot.astype(f32) + inverse[:rows, :1] * (
        scaled
        - jnp.mean(scaled, axis=1, keepdims=True)
        - normed * jnp.mean(scaled * normed, axis=1, keepdims=True)
    )

    gain_own = (sums[:height] + sums_came[:height]) * factor
    shift_own = (sums[height : 2 * height] + sums_came[height : 2 * height]) * factor
    bias_own = sums[-height:] * factor
    pairs = jnp.where(c == 0, jnp.stack([sums, sums_came]), jnp.stack([sums_came, sums]))
    pairs = pairs[:, 2 * height : -height]
    fc1_bias_own = pairs[:, :ff_own].reshape(-1) * factor
    mixed_sums = jnp.transpose(pairs[:, ff_own:].reshape(CORES, S, 3, mix_own), (2, 1, 0, 3))
    qkv_bias_own = pick(mixed_sums.reshape(S, -1), s, 0) * factor
    return (
        output.reshape(tokens.shape),
        input_grad.reshape(tokens.shape),
        gain_own,
        shift_own,
        qkv_own,
        qkv_bias_own,
        out_own,
        bias_own,
        fc1_own,
        fc1_bias_own,
        fc2_own,
        bias_own,
    )


def solution(mesh):
    return jax.shard_map(
        local,
        mesh=mesh,
        in_specs=(
            P(("dp", "shard"), None, None),
            P(("dp", "shard"), None),
            P("shard"),
            P("shard"),
            P("shard", None),
            P("shard"),
            P("shard", None),
            P("shard"),
            P("shard", None),
            P("shard"),
            P("shard", None),
            P("shard"),
            P(("dp", "shard"), None, None),
        ),
        out_specs=(
            P(("dp", "shard"), None, None),
            P(("dp", "shard"), None, None),
            P("shard"),
            P("shard"),
            P("shard", None),
            P("shard"),
            P("shard", None),
            P("shard"),
            P("shard", None),
            P("shard"),
            P("shard", None),
            P("shard"),
        ),
        check_vma=False,
    )
```

profile of v0, /device:TPU:0, one launch (start us, length us, event | category | flops | bytes accessed | tf_op | source)
XLA Modules:
  0.0 460.4 jit_solution(633650231398407956)
XLA Ops:
  13.2 5.1 %collective-permute-start.3 = (bf16[5760]{0:T(1024)(128)(2,1)S(1)}, bf16[5760]{0:T(1024)(128)(2,1)S(1)}, u32[]{:S(2)}, u32[]{:S(2)}) collective-permute-start(bf16[5760]{0:T(1024)(128)(2,1)S(1)} %dynamic-update-slice.6), channel_id=1, source_target_pairs={{0,3},{1,0},{2,1},{3,2},{4,7},{5,4},{6,5},{7,6},{8,11},{9,8},{10,9... | collective-permute-start | bytes 34568 | tf_op jit(solution)/shard_map/ppermute | solution.py:529
  54.9 31.0 %all-to-all-done = bf16[4,128,1792]{2,1,0:T(8,128)(2,1)} async-done(((bf16[4,128,1792]{2,1,0:T(8,128)(2,1)}), bf16[4,128,1792]{2,1,0:T(8,128)(2,1)}, u32[]{:S(2)}, u32[]{:S(2)}) %all-to-all-start) | async-done | bytes 1835040 | tf_op jit(solution)/shard_map/all_to_all | solution.py:582
  89.0 16.8 %collective-permute-done.8.refs_1_ = bf16[1,384,1792]{2,1,0:T(8,128)(2,1)S(1)} collective-permute-done((bf16[1,384,1792]{2,1,0:T(8,128)(2,1)S(1)}, bf16[1,384,1792]{2,1,0:T(8,128)(2,1)S(1)}, u32[]{:S(2)}, u32[]{:S(2)}) %collective-permute-start.8) | collective-permute-done | bytes 1376288 | tf_op jit(solution)/shard_map/ppermute | solution.py:529
  107.5 8.2 %collective-permute-done.7.refs_4_ = bf16[256,2048]{1,0:T(8,128)(2,1)S(1)} collective-permute-done((bf16[256,2048]{1,0:T(8,128)(2,1)}, bf16[256,2048]{1,0:T(8,128)(2,1)S(1)}, u32[]{:S(2)}, u32[]{:S(2)}) %collective-permute-start.7) | collective-permute-done | bytes 1048608 | tf_op jit(solution)/shard_map/ppermute | solution.py:529
  119.4 7.8 %shard_map.240 = (bf16[1024,2048]{1,0:T(8,128)(2,1)}, bf16[1024,2048]{1,0:T(8,128)(2,1)}, bf16[1024,2048]{1,0:T(8,128)(2,1)}, f32[1024,128]{1,0:T(8,128)S(1)}, f32[1024,128]{1,0:T(8,128)S(1)}) custom-call(s32[6]{0:T(128)S(1)} %copy-done.29, f32[1,2048]{1,0:T(1,128)S(1)} %bitcast.172, f32[1,2048]{1,0:T(1,128)S(1)} %bitcast.176, ...), custom_call_target="tpu_custom_call" | custom-call | tf_op jit(solution)/shard_map/pallas_call | solution.py:237
  128.0 15.4 %collective-permute-done.9.refs_0_ = bf16[256,2048]{1,0:T(8,128)(2,1)} collective-permute-done((bf16[256,2048]{1,0:T(8,128)(2,1)S(1)}, bf16[256,2048]{1,0:T(8,128)(2,1)}, u32[]{:S(2)}, u32[]{:S(2)}) %collective-permute-start.9) | collective-permute-done | bytes 1048608 | tf_op jit(solution)/shard_map/ppermute | solution.py:529
  156.8 11.9 %multiply_convert_fusion = (bf16[1024,1024]{1,0:T(8,128)(2,1)S(1)}, f32[1024,1024]{1,0:T(8,128)}) fusion(f32[1024]{0:T(1024)S(1)} %dynamic_slice.74, bf16[1024,2048]{1,0:T(8,128)(2,1)} %get-tuple-element.184, bf16[2048,1024]{1,0:T(8,128)(2,1)} %bitcast.193), kind=kOutput, calls=%fused_computation.12 | convolution fusion | flops 4305453056 | bytes 14684160 | tf_op jit(solution)/shard_map/dot_general | solution.py:711
  175.9 9.3 %fusion.6.hidden_ref = bf16[1024,1024]{1,0:T(8,128)(2,1)S(1)} fusion(f32[1024,1024]{1,0:T(8,128)} %get-tuple-element.283, f32[1024]{0:T(1024)S(1)} %dynamic_slice.74, bf16[1024,2048]{1,0:T(8,128)(2,1)S(1)} %copy-done.37, bf16[1024,2048]{1,0:T(8,128)(2,1)S(1)} %copy-done.42), kind=kOutput, calls=%fused_computation.9 | convolution fusion | flops 4316987392 | bytes 14684160 | tf_op jit(solution)/shard_map/td,fd->tf/dot_general | solution.py:757
  185.3 4.9 %convolution_convert_fusion = bf16[2048,1024]{1,0:T(8,128)(2,1)S(1)} fusion(bf16[1024,2048]{1,0:T(8,128)(2,1)S(1)} %copy-done.44, bf16[1024,1024]{1,0:T(8,128)(2,1)S(1)} %fusion.6.hidden_ref), kind=kOutput, calls=%fused_computation.13 | convolution fusion | flops 4297064448 | bytes 10485760 | tf_op jit(solution)/shard_map/td,te->de/dot_general | solution.py:714
  194.5 5.6 %collective-permute-done.13 = bf16[2,1,256,2048]{3,2,1,0:T(8,128)(2,1)S(1)} collective-permute-done((bf16[2,1,256,2048]{3,2,1,0:T(8,128)(2,1)S(1)}, bf16[2,1,256,2048]{3,2,1,0:T(8,128)(2,1)S(1)}, u32[]{:S(2)}, u32[]{:S(2)}) %collective-permute-start.13) | collective-permute-done | bytes 2097184 | tf_op jit(solution)/shard_map/ppermute | solution.py:529
  201.5 5.1 %broadcast_add_fusion.mixed_ref = f32[1024,768]{1,0:T(8,128)} fusion(f32[768]{0:T(1024)S(1)} %reshape.336, bf16[1024,2048]{1,0:T(8,128)(2,1)S(1)} %copy-done.44, bf16[2048,768]{1,0:T(8,128)(2,1)S(1)} %bitcast.169), kind=kOutput, calls=%fused_computation.34 | convolution fusion | flops 3222011904 | bytes 10488832 | tf_op jit(solution)/shard_map/dot_general | solution.py:763
  208.1 12.1 %shard_map.244 = (bf16[1024,256]{1,0:T(8,128)(2,1)S(1)}, bf16[1024,768]{1,0:T(8,128)(2,1)S(1)}) custom-call(s32[1024,128]{1,0:T(8,128)S(1)} %copy-done.27, f32[1024,128]{1,0:T(8,128)S(1)} %copy-done.26, f32[1024,128]{1,0:T(8,128)S(1)} %copy-done.25, f32[1024,128]{1,0:T(8,128)S(1)} %copy-done.24, f32[1024,768]{1,0:T(8,128)} %broadcast_add_fusion.mixed_ref, ...), custom_call_target="tpu_custom_call" | custom-call | flops 4000000000 | tf_op jit(solution)/shard_map/pallas_call | solution.py:94
  220.2 13.7 %collective-permute-done.15 = bf16[2,4,128,1024]{3,2,1,0:T(8,128)(2,1)} collective-permute-done((bf16[2,4,128,1024]{3,2,1,0:T(8,128)(2,1)}, bf16[2,4,128,1024]{3,2,1,0:T(8,128)(2,1)}, u32[]{:S(2)}, u32[]{:S(2)}) %collective-permute-start.15) | collective-permute-done | bytes 2097184 | tf_op jit(solution)/shard_map/ppermute | solution.py:529
  248.2 14.2 %collective-permute-done.17 = bf16[4,128,1024]{2,1,0:T(8,128)(2,1)S(1)} collective-permute-done((bf16[4,128,1024]{2,1,0:T(8,128)(2,1)S(1)}, bf16[4,128,1024]{2,1,0:T(8,128)(2,1)S(1)}, u32[]{:S(2)}, u32[]{:S(2)}) %collective-permute-start.17) | collective-permute-done | bytes 1048608 | tf_op jit(solution)/shard_map/ppermute | solution.py:529
  274.2 9.5 %shard_map.246 = (f32[512,2048]{1,0:T(8,128)}, bf16[512,2048]{1,0:T(8,128)(2,1)S(1)}) custom-call(bf16[1024,256]{1,0:T(8,128)(2,1)S(1)} %copy-done.34, bf16[256,2048]{1,0:T(8,128)(2,1)S(1)} %copy-done.15, bf16[1024,1024]{1,0:T(8,128)(2,1)S(1)} %copy-done.32, bf16[1024,2048]{1,0:T(8,128)(2,1)} %constant_dynamic-slice_fusion.6.fc2_ref), custom_call_target="tpu_custom_call" | custom-call | flops 3333333248 | tf_op jit(solution)/shard_map/pallas_call | solution.py:325
  285.1 13.4 %shard_map.247 = (f32[512,2048]{1,0:T(8,128)}, bf16[512,2048]{1,0:T(8,128)(2,1)}, f32[8,2048]{1,0:T(8,128)S(1)}) custom-call(bf16[1024,1024]{1,0:T(8,128)(2,1)} %copy-done.47, bf16[2048,1024]{1,0:T(8,128)(2,1)} %bitcast.194, bf16[1024,768]{1,0:T(8,128)(2,1)S(1)} %copy-done.9, bf16[2048,768]{1,0:T(8,128)(2,1)} %bitcast.170, ...), custom_call_target="tpu_custom_call" | custom-call | flops 4666666496 | tf_op jit(solution)/shard_map/pallas_call | solution.py:355
  310.5 5.2 %shard_map.249 = bf16[4,128,2048]{2,1,0:T(8,128)(2,1)} custom-call(s32[4]{0:T(128)S(1)} %and_select_fusion.2.order_ref, f32[512,2048]{1,0:T(8,128)} %get-tuple-element.217.mine_ref, bf16[512,2048]{1,0:T(8,128)(2,1)} %collective-permute-done.21.came_ref), custom_call_target="tpu_custom_call" | custom-call | flops 1666666624 | tf_op jit(solution)/shard_map/pallas_call | solution.py:302
  325.1 17.0 %collective-permute-done.23 = bf16[128,4096]{1,0:T(8,128)(2,1)} collective-permute-done((bf16[128,4096]{1,0:T(8,128)(2,1)S(1)}, bf16[128,4096]{1,0:T(8,128)(2,1)}, u32[]{:S(2)}, u32[]{:S(2)}) %collective-permute-start.23) | collective-permute-done | bytes 1048608 | tf_op jit(solution)/shard_map/ppermute | solution.py:529
  348.1 5.0 %all-to-all-start.2 = ((bf16[4,144,768]{2,1,0:T(8,128)(2,1)}), bf16[4,144,768]{2,1,0:T(8,128)(2,1)}, u32[]{:S(2)}, u32[]{:S(2)}) async-start(bf16[4,144,768]{2,1,0:T(8,128)(2,1)} %pad_maximum_fusion.5), calls=%async_computation.4 | async-start | bytes 1769472 | tf_op jit(solution)/shard_map/all_to_all | solution.py:582
  354.2 16.9 %collective-permute-done.24.m1_ref = bf16[2,128,4096]{2,1,0:T(8,128)(2,1)} collective-permute-done((bf16[2,128,4096]{2,1,0:T(8,128)(2,1)}, bf16[2,128,4096]{2,1,0:T(8,128)(2,1)}, u32[]{:S(2)}, u32[]{:S(2)}) %collective-permute-start.24) | collective-permute-done | bytes 2097184 | tf_op jit(solution)/shard_map/ppermute | solution.py:529
  371.1 11.5 %all-to-all-done.2 = bf16[4,144,768]{2,1,0:T(8,128)(2,1)} async-done(((bf16[4,144,768]{2,1,0:T(8,128)(2,1)}), bf16[4,144,768]{2,1,0:T(8,128)(2,1)}, u32[]{:S(2)}, u32[]{:S(2)}) %all-to-all-start.2) | async-done | bytes 884768 | tf_op jit(solution)/shard_map/all_to_all | solution.py:582
  387.1 11.6 %shard_map.251 = f32[2048,2048]{1,0:T(8,128)} custom-call(s32[8]{0:T(128)S(1)} %pad_add_fusion.4.spots_ref, bf16[2,256,2048]{2,1,0:T(8,128)(2,1)S(1)} %shard_map.245.refs_0_, bf16[2,256,2048]{2,1,0:T(8,128)(2,1)} %collective-permute-done.19.refs_1_, bf16[2,256,2048]{2,1,0:T(8,128)(2,1)} %collective-permute-done.27.refs_2_, ...), custom_call_target="tpu_custom_call" | custom-call | flops 4000000000 | tf_op jit(solution)/shard_map/pallas_call | solution.py:495
  409.8 14.2 %shard_map.253 = f32[512,8192]{1,0:T(8,128)} custom-call(s32[6]{0:T(128)S(1)} %concatenate.63.spots_ref, bf16[2,128,4096]{2,1,0:T(8,128)(2,1)} %shard_map.250.m0_ref, bf16[2,128,4096]{2,1,0:T(8,128)(2,1)} %collective-permute-done.24.m1_ref, bf16[2,128,4096]{2,1,0:T(8,128)(2,1)} %collective-permute-done.30.o0_ref, ...), custom_call_target="tpu_custom_call" | custom-call | flops 3666666752 | tf_op jit(solution)/shard_map/pallas_call | solution.py:400
  437.4 15.4 %shard_map.254 = (f32[512,6144]{1,0:T(8,128)}, f32[512,2048]{1,0:T(8,128)}) custom-call(s32[6]{0:T(128)S(1)} %concatenate.63.spots_ref, bf16[2,128,4096]{2,1,0:T(8,128)(2,1)S(1)} %copy-done.7, bf16[2,128,4096]{2,1,0:T(8,128)(2,1)} %collective-permute-done.29.m1_ref, bf16[2,128,4096]{2,1,0:T(8,128)(2,1)} %collective-permute-done.34.o0_ref, ...), custom_call_target="tpu_custom_call" | custom-call | flops 5333333504 | tf_op jit(solution)/shard_map/pallas_call | solution.py:455
  (312 shorter events, 158.5 us)
Async XLA Ops:
  13.2 31.0 %collective-permute-start.3 = (bf16[5760]{0:T(1024)(128)(2,1)S(1)}, bf16[5760]{0:T(1024)(128)(2,1)S(1)}, u32[]{:S(2)}, u32[]{:S(2)}) collective-permute-start(bf16[5760]{0:T(1024)(128)(2,1)S(1)} %dynamic-update-slice.6), channel_id=1, source_target_pairs={{0,3},{1,0},{2,1},{3,2},{4,7},{5,4},{6,5},{7,6},{8,11},{9,8},{10,9... | collective-permute-start | bytes 34568 | tf_op jit(solution)/shard_map/ppermute | solution.py:529
  18.2 25.9 %collective-permute-start.2 = (bf16[5760]{0:T(1024)(128)(2,1)S(1)}, bf16[5760]{0:T(1024)(128)(2,1)S(1)}, u32[]{:S(2)}, u32[]{:S(2)}) collective-permute-start(bf16[5760]{0:T(1024)(128)(2,1)S(1)} %dynamic-update-slice.6), channel_id=1, source_target_pairs={{0,2},{1,3},{2,0},{3,1},{4,6},{5,7},{6,4},{7,5},{8,10},{9,11},{10,... | collective-permute-start | bytes 34568 | tf_op jit(solution)/shard_map/ppermute | solution.py:529
  20.5 28.2 %collective-permute-start = (bf16[256,2048]{1,0:T(8,128)(2,1)S(1)}, bf16[256,2048]{1,0:T(8,128)(2,1)}, u32[]{:S(2)}, u32[]{:S(2)}) collective-permute-start(bf16[256,2048]{1,0:T(8,128)(2,1)S(1)} %pad_maximum_fusion.4.refs_0_), channel_id=1, source_target_pairs={{0,1},{1,2},{2,3},{3,0},{4,5},{5,6},{6,7},{7,4},{8,9},{9,10},{10,1... | collective-permute-start | bytes 3145736 | tf_op jit(solution)/shard_map/ppermute | solution.py:529
  27.3 58.6 %all-to-all-start = ((bf16[4,128,1792]{2,1,0:T(8,128)(2,1)}), bf16[4,128,1792]{2,1,0:T(8,128)(2,1)}, u32[]{:S(2)}, u32[]{:S(2)}) async-start(bf16[4,128,1792]{2,1,0:T(8,128)(2,1)} %copy-done.2), calls=%async_computation | async-start | bytes 3670016 | tf_op jit(solution)/shard_map/all_to_all | solution.py:582
  89.0 26.8 %collective-permute-start.7 = (bf16[256,2048]{1,0:T(8,128)(2,1)}, bf16[256,2048]{1,0:T(8,128)(2,1)S(1)}, u32[]{:S(2)}, u32[]{:S(2)}) collective-permute-start(bf16[256,2048]{1,0:T(8,128)(2,1)} %collective-permute-done.refs_2_), channel_id=1, source_target_pairs={{0,1},{1,2},{2,3},{3,0},{4,5},{5,6},{6,7},{7,4},{8,9},{9,10},{10,1... | collective-permute-start | bytes 3145736 | tf_op jit(solution)/shard_map/ppermute | solution.py:529
  106.0 45.1 %collective-permute-start.12 = (bf16[2,384,1792]{2,1,0:T(8,128)(2,1)S(1)}, bf16[2,384,1792]{2,1,0:T(8,128)(2,1)}, u32[]{:S(2)}, u32[]{:S(2)}) collective-permute-start(bf16[2,384,1792]{2,1,0:T(8,128)(2,1)S(1)} %shard_map.239), channel_id=1, source_target_pairs={{0,8},{1,9},{2,10},{3,11},{4,20},{5,21},{6,22},{7,23},{8,0},{9,1},... | collective-permute-start | bytes 8257544 | tf_op jit(solution)/shard_map/ppermute | solution.py:529
  115.8 27.6 %collective-permute-start.9 = (bf16[256,2048]{1,0:T(8,128)(2,1)S(1)}, bf16[256,2048]{1,0:T(8,128)(2,1)}, u32[]{:S(2)}, u32[]{:S(2)}) collective-permute-start(bf16[256,2048]{1,0:T(8,128)(2,1)S(1)} %collective-permute-done.7.refs_4_), channel_id=1, source_target_pairs={{0,1},{1,2},{2,3},{3,0},{4,5},{5,6},{6,7},{7,4},{8,9},{9,10},{10,1... | collective-permute-start | bytes 3145736 | tf_op jit(solution)/shard_map/ppermute | solution.py:529
  174.0 26.1 %collective-permute-start.13 = (bf16[2,1,256,2048]{3,2,1,0:T(8,128)(2,1)S(1)}, bf16[2,1,256,2048]{3,2,1,0:T(8,128)(2,1)S(1)}, u32[]{:S(2)}, u32[]{:S(2)}) collective-permute-start(bf16[2,1,256,2048]{3,2,1,0:T(8,128)(2,1)S(1)} %pad_maximum_fusion.1), channel_id=1, source_target_pairs={{0,16},{1,17},{2,18},{3,19},{4,12},{5,13},{6,14},{7,15},{8,24},{9,... | collective-permute-start | bytes 6291464 | tf_op jit(solution)/shard_map/ppermute | solution.py:529
  193.0 40.9 %collective-permute-start.15 = (bf16[2,4,128,1024]{3,2,1,0:T(8,128)(2,1)}, bf16[2,4,128,1024]{3,2,1,0:T(8,128)(2,1)}, u32[]{:S(2)}, u32[]{:S(2)}) collective-permute-start(bf16[2,4,128,1024]{3,2,1,0:T(8,128)(2,1)} %pad_maximum_fusion.2), channel_id=1, source_target_pairs={{0,16},{1,17},{2,18},{3,19},{4,12},{5,13},{6,14},{7,15},{8,24},{9,... | collective-permute-start | bytes 6291464 | tf_op jit(solution)/shard_map/ppermute | solution.py:529
  200.9 36.3 %collective-permute-start.14 = (bf16[1,256,2048]{2,1,0:T(8,128)(2,1)S(1)}, bf16[1,256,2048]{2,1,0:T(8,128)(2,1)S(1)}, u32[]{:S(2)}, u32[]{:S(2)}) collective-permute-start(bf16[1,256,2048]{2,1,0:T(8,128)(2,1)S(1)} %get-tuple-element.172), channel_id=1, source_target_pairs={{0,8},{1,9},{2,10},{3,11},{4,20},{5,21},{6,22},{7,23},{8,0},{9,1},... | collective-permute-start | bytes 3145736 | tf_op jit(solution)/shard_map/ppermute | solution.py:529
  237.6 30.5 %collective-permute-start.16 = (bf16[256,2048]{1,0:T(8,128)(2,1)S(1)}, bf16[256,2048]{1,0:T(8,128)(2,1)S(1)}, u32[]{:S(2)}, u32[]{:S(2)}) collective-permute-start(bf16[256,2048]{1,0:T(8,128)(2,1)S(1)} %bitcast.164), channel_id=1, source_target_pairs={{0,16},{1,17},{2,18},{3,19},{4,12},{5,13},{6,14},{7,15},{8,24},{9,... | collective-permute-start | bytes 3145736 | tf_op jit(solution)/shard_map/ppermute | solution.py:529
  247.7 57.6 %collective-permute-start.20 = (bf16[2,4,128,1024]{3,2,1,0:T(8,128)(2,1)}, bf16[2,4,128,1024]{3,2,1,0:T(8,128)(2,1)}, u32[]{:S(2)}, u32[]{:S(2)}) collective-permute-start(bf16[2,4,128,1024]{3,2,1,0:T(8,128)(2,1)} %pad_maximum_fusion.3), channel_id=1, source_target_pairs={{0,16},{1,17},{2,18},{3,19},{4,12},{5,13},{6,14},{7,15},{8,24},{9,... | collective-permute-start | bytes 6291464 | tf_op jit(solution)/shard_map/ppermute | solution.py:529
  263.8 45.3 %all-to-all-start.1 = ((bf16[4,128,1024]{2,1,0:T(8,128)(2,1)}), bf16[4,128,1024]{2,1,0:T(8,128)(2,1)}, u32[]{:S(2)}, u32[]{:S(2)}) async-start(bf16[4,128,1024]{2,1,0:T(8,128)(2,1)} %add_convert_fusion.1), calls=%async_computation.1 | async-start | bytes 2097152 | tf_op jit(solution)/shard_map/all_to_all | solution.py:582
  268.1 140.1 %reduce-scatter.5.cloned.1.call-start = ((), (), s32[]{:S(2)}) async-start(), calls=%async_computation.6 | async-start | bytes 2621440 | tf_op jit(solution)/shard_map/reduce_scatter | solution.py:794
  270.5 38.6 %collective-permute-start.19 = (bf16[2,256,2048]{2,1,0:T(8,128)(2,1)S(1)}, bf16[2,256,2048]{2,1,0:T(8,128)(2,1)}, u32[]{:S(2)}, u32[]{:S(2)}) collective-permute-start(bf16[2,256,2048]{2,1,0:T(8,128)(2,1)S(1)} %shard_map.245.refs_0_), channel_id=1, source_target_pairs={{0,8},{1,9},{2,10},{3,11},{4,20},{5,21},{6,22},{7,23},{8,0},{9,1},... | collective-permute-start | bytes 6291464 | tf_op jit(solution)/shard_map/ppermute | solution.py:529
  318.0 27.4 %collective-permute-start.22 = (bf16[4,128,1024]{2,1,0:T(8,128)(2,1)}, bf16[4,128,1024]{2,1,0:T(8,128)(2,1)}, u32[]{:S(2)}, u32[]{:S(2)}) collective-permute-start(bf16[4,128,1024]{2,1,0:T(8,128)(2,1)} %get-tuple-element.213), channel_id=1, source_target_pairs={{0,8},{1,9},{2,10},{3,11},{4,20},{5,21},{6,22},{7,23},{8,0},{9,1},... | collective-permute-start | bytes 3145736 | tf_op jit(solution)/shard_map/ppermute | solution.py:529
  344.8 26.4 %collective-permute-start.24 = (bf16[2,128,4096]{2,1,0:T(8,128)(2,1)}, bf16[2,128,4096]{2,1,0:T(8,128)(2,1)}, u32[]{:S(2)}, u32[]{:S(2)}) collective-permute-start(bf16[2,128,4096]{2,1,0:T(8,128)(2,1)} %shard_map.250.m0_ref), channel_id=1, source_target_pairs={{0,8},{1,9},{2,10},{3,11},{4,20},{5,21},{6,22},{7,23},{8,0},{9,1},... | collective-permute-start | bytes 6291464 | tf_op jit(solution)/shard_map/ppermute | solution.py:529
  348.1 34.5 %all-to-all-start.2 = ((bf16[4,144,768]{2,1,0:T(8,128)(2,1)}), bf16[4,144,768]{2,1,0:T(8,128)(2,1)}, u32[]{:S(2)}, u32[]{:S(2)}) async-start(bf16[4,144,768]{2,1,0:T(8,128)(2,1)} %pad_maximum_fusion.5), calls=%async_computation.4 | async-start | bytes 1769472 | tf_op jit(solution)/shard_map/all_to_all | solution.py:582
  353.1 77.6 %reduce-scatter.3.cloned.1.call-start = ((), (), s32[]{:S(2)}) async-start(), calls=%async_computation.5 | async-start | bytes 2621440 | tf_op jit(solution)/shard_map/reduce_scatter | solution.py:794
  353.1 33.8 %collective-permute-start.27 = (bf16[2,256,2048]{2,1,0:T(8,128)(2,1)S(1)}, bf16[2,256,2048]{2,1,0:T(8,128)(2,1)}, u32[]{:S(2)}, u32[]{:S(2)}) collective-permute-start(bf16[2,256,2048]{2,1,0:T(8,128)(2,1)S(1)} %shard_map.245.refs_0_), channel_id=1, source_target_pairs={{0,4},{1,5},{2,6},{3,7},{4,0},{5,1},{6,2},{7,3},{8,12},{9,13},{10,... | collective-permute-start | bytes 6291464 | tf_op jit(solution)/shard_map/ppermute | solution.py:529
  353.1 33.8 %collective-permute-start.28 = (bf16[2,256,2048]{2,1,0:T(8,128)(2,1)}, bf16[2,256,2048]{2,1,0:T(8,128)(2,1)}, u32[]{:S(2)}, u32[]{:S(2)}) collective-permute-start(bf16[2,256,2048]{2,1,0:T(8,128)(2,1)} %collective-permute-done.19.refs_1_), channel_id=1, source_target_pairs={{0,4},{1,5},{2,6},{3,7},{4,0},{5,1},{6,2},{7,3},{8,12},{9,13},{10,... | collective-permute-start | bytes 6291464 | tf_op jit(solution)/shard_map/ppermute | solution.py:529
  354.1 55.6 %collective-permute-start.30 = (bf16[2,128,4096]{2,1,0:T(8,128)(2,1)}, bf16[2,128,4096]{2,1,0:T(8,128)(2,1)}, u32[]{:S(2)}, u32[]{:S(2)}) collective-permute-start(bf16[2,128,4096]{2,1,0:T(8,128)(2,1)} %shard_map.250.m0_ref), channel_id=1, source_target_pairs={{0,4},{1,5},{2,6},{3,7},{4,0},{5,1},{6,2},{7,3},{8,12},{9,13},{10,... | collective-permute-start | bytes 6291464 | tf_op jit(solution)/shard_map/ppermute | solution.py:529
  400.4 26.5 %collective-permute-start.29 = (bf16[2,128,4096]{2,1,0:T(8,128)(2,1)S(1)}, bf16[2,128,4096]{2,1,0:T(8,128)(2,1)}, u32[]{:S(2)}, u32[]{:S(2)}) collective-permute-start(bf16[2,128,4096]{2,1,0:T(8,128)(2,1)S(1)} %shard_map.252.m0_ref), channel_id=1, source_target_pairs={{0,8},{1,9},{2,10},{3,11},{4,20},{5,21},{6,22},{7,23},{8,0},{9,1},... | collective-permute-start | bytes 6291464 | tf_op jit(solution)/shard_map/ppermute | solution.py:529
  408.1 27.7 %collective-permute-start.34 = (bf16[2,128,4096]{2,1,0:T(8,128)(2,1)S(1)}, bf16[2,128,4096]{2,1,0:T(8,128)(2,1)}, u32[]{:S(2)}, u32[]{:S(2)}) collective-permute-start(bf16[2,128,4096]{2,1,0:T(8,128)(2,1)S(1)} %shard_map.252.m0_ref), channel_id=1, source_target_pairs={{0,4},{1,5},{2,6},{3,7},{4,0},{5,1},{6,2},{7,3},{8,12},{9,13},{10,... | collective-permute-start | bytes 6291464 | tf_op jit(solution)/shard_map/ppermute | solution.py:529
  (72 other events, 889.9 us)
Sparse Core Ops, SparseCore 0:
  315.8 47.1 reduce-scatter.4
  365.9 47.1 reduce-scatter.2
where the time goes:
time: 467 us; the launch traced here: 460 us
  waiting for transfers between devices  166 us (36%)
  Pallas kernels  112 us (24%)
  starting transfers between devices  44.5 us (10%)
  matrix products  42.5 us (9%)
  local copies, waits for them, and re-layouts  37.6 us (8%)
  other arithmetic  37.2 us (8%)
  between operations  21.2 us (5%)
    ppermute x36, waiting for transfers between devices, move(): return lax.ppermute(x, AXES, pairs)  123 us
    all_to_all x3, waiting for transfers between devices, swap(): return lax.all_to_all(tie(x, *after), 'shard', 0, 0, tiled=True)  42.5 us
    ppermute x36, starting transfers between devices, move(): return lax.ppermute(x, AXES, pairs)  30.7 us
    unnamed x119, local copies, waits for them, and re-layouts  20.4 us
    pallas_call x1, Pallas kernels, place_mixed(): call(kernel, (J, planes), [pl.BlockSpec((None, part, columns), lambda i,...  15.4 us
    dot_general x4, matrix products, local(): jnp.einsum('td,te->de', x, y, preferred_element_type=f32).astype(bf16)  14.9 us
    pallas_call x1, Pallas kernels, place_columns(): call(kernel, (J, 2), [pl.BlockSpec((None, high, columns), lambda i, h, sp...  14.2 us
    all_to_all x3, starting transfers between devices, swap(): return lax.all_to_all(tie(x, *after), 'shard', 0, 0, tiled=True)  13.7 us
  transfers between devices with their start and end apart: 41, of which 18 were waited for; matrix products, arithmetic and copies ran while one was open for 17% of the time, Pallas kernels for 19%

commit v1 on v0

--- a/solution.py
+++ b/solution.py
@@ -151,7 +151,7 @@
 
 
 def assemble(w_fc1, w_qkv, arrays, order, spots, own, piece, blocks, before=None):
-    others, rows, cols = arrays[0].shape
+    _, others, rows, cols = arrays[0].shape
     planes = others + 1
     height = w_fc1.shape[0]
     third = w_qkv.shape[1] // 3 // piece
@@ -162,14 +162,15 @@
         fc1_out[here] = fc1_ref[...]
         for i, ref in enumerate((q_ref, k_ref, v_ref)):
             qkv_out[here, :, i * piece : (i + 1) * piece] = ref[...]
-        for n in range(len(arrays)):
+        places = [(ref, m) for ref in refs[: len(arrays)] for m in range(ref.shape[0])]
+        for n, (ref, m) in enumerate(places):
 
             @pl.when(pl.program_id(0) == n)
-            def _(ref=refs[n]):
+            def _(ref=ref, m=m):
                 for k in range(1, planes):
                     there = spots_ref[k]
-                    fc1_out[there] = ref[k - 1, :, :own]
-                    qkv_out[there] = ref[k - 1, :, own:]
+                    fc1_out[there] = ref[m, k - 1, :, :own]
+                    qkv_out[there] = ref[m, k - 1, :, own:]
 
     cut = lambda i: pl.BlockSpec(
         (None, rows, piece), lambda n, order, spots: (order[n], 0, i * third + spots[planes])
@@ -183,14 +184,14 @@
         more["input_output_aliases"] = {first: 0, first + 1: 1}
     return call(
         kernel,
-        (len(arrays),),
+        (sum(x.shape[0] for x in arrays),),
         [
             pl.BlockSpec((None, rows, own), lambda n, order, spots: (order[n], 0, spots[planes])),
             cut(0),
             cut(1),
             cut(2),
         ]
-        + [pl.BlockSpec(x.shape, lambda n, order, spots: (0, 0, 0)) for x in arrays]
+        + [pl.BlockSpec(x.shape, lambda n, order, spots: (0, 0, 0, 0)) for x in arrays]
         + [pl.BlockSpec(memory_space=pl.ANY)] * (0 if before is None else 2),
         [result(own), result(3 * piece)],
         [
@@ -306,7 +307,6 @@
         pl.BlockSpec((None, rows, width), lambda i, order: (order[i], 0, 0)),
         jax.ShapeDtypeStruct((count, rows, width), bf16),
         scalars=1,
-        us=5,
     )(order, mine, came)
 
 
@@ -410,39 +410,35 @@
         pl.BlockSpec((high, 2 * columns), lambda i, h, spots: (spots[i] * 2 + h, 0)),
         jax.ShapeDtypeStruct((J * rows, 2 * columns), f32),
         scalars=1,
-        us=11,
     )(spots, *mine, *other)
 
 
-def place_mixed(net, mine, other, factor):
+def place_mixed(net, mine, other, start, factor, before=None):
     J, planes = net.J, net.S
-    _, part, columns = mine[0].shape
+    count, part, columns = mine.shape
     piece = columns // planes // 4
     width = planes * CORES * piece
-    spots = jnp.concatenate([net.order(), jnp.stack([net.c, 1 - net.c])]).astype(jnp.int32)
-
-    def kernel(spots_ref, m0_ref, m1_ref, o0_ref, o1_ref, qkv_ref, out_ref):
-        here = pl.program_id(0)
-        for e, (place, refs) in enumerate(
-            ((net.mine, (m0_ref, m1_ref)), (net.theirs, (o0_ref, o1_ref)))
-        ):
-            last, _ = place(here)
-            core = spots_ref[J + e]
-            for ref, chosen in zip(refs, (jnp.logical_not(last), last)):
-                for k in range(planes):
-
-                    @pl.when(chosen & (pl.program_id(1) == k))
-                    def _(k=k, core=core, ref=ref):
-                        for i in range(3):
-                            start = (4 * k + i) * piece
-                            column = ((i * planes + k) * CORES + core) * piece
-                            qkv_ref[:, pl.ds(pl.multiple_of(column, LANES), piece)] = (
-                                ref[:, start : start + piece].astype(f32) * factor
-                            )
-                        block = ref[:, (4 * k + 3) * piece : (4 * k + 4) * piece].astype(f32)
-                        out_ref[pl.ds(pl.multiple_of(core * piece, LANES), piece), :] = (
-                            block * factor
-                        ).T
+    chips = net.order()[start : start + count]
+    spots = jnp.concatenate([chips, jnp.stack([net.c, 1 - net.c])]).astype(jnp.int32)
+
+    def kernel(spots_ref, mine_ref, other_ref, *refs):
+        qkv_ref, out_ref = refs[-2:]
+        for e, ref in enumerate((mine_ref, other_ref)):
+            core = spots_ref[count + e]
+            for k in range(planes):
+
+                @pl.when(pl.program_id(1) == k)
+                def _(k=k, core=core, ref=ref):
+                    for i in range(3):
+                        start = (4 * k + i) * piece
+                        column = ((i * planes + k) * CORES + core) * piece
+                        qkv_ref[:, pl.ds(pl.multiple_of(column, LANES), piece)] = (
+                            ref[:, start : start + piece].astype(f32) * factor
+                        )
+                    block = ref[:, (4 * k + 3) * piece : (4 * k + 4) * piece].astype(f32)
+                    out_ref[pl.ds(pl.multiple_of(core * piece, LANES), piece), :] = (
+                        block * factor
+                    ).T
 
     if part % LANES == 0:
         out_shape = (CORES * piece, planes * J * part)
@@ -452,24 +448,23 @@
         out_spec = pl.BlockSpec(
             (None, None, CORES * piece, part), lambda i, k, spots: (k, spots[i], 0, 0)
         )
+    before = before or ()
     return call(
         kernel,
-        (J, planes),
+        (count, planes),
         [
-            pl.BlockSpec(
-                (None, part, columns), lambda i, k, spots, place=place, n=n: (place(i)[1][n], 0, 0)
-            )
-            for place in (net.mine, net.theirs)
-            for n in range(2)
-        ],
+            pl.BlockSpec((None, part, columns), lambda i, k, spots: (i, 0, 0)),
+            pl.BlockSpec((None, part, columns), lambda i, k, spots: (i, 0, 0)),
+        ]
+        + [pl.BlockSpec(memory_space=pl.ANY)] * len(before),
         [pl.BlockSpec((part, 3 * width), lambda i, k, spots: (spots[i], 0)), out_spec],
         [
             jax.ShapeDtypeStruct((width // planes, 3 * width), f32),
             jax.ShapeDtypeStruct(out_shape, f32),
         ],
         scalars=1,
-        us=16,
-    )(spots, *mine, *other)
+        input_output_aliases={3 + i: i for i in range(len(before))},
+    )(spots, mine, other, *before)
 
 
 def place_rows(net, mine, other, factor):
@@ -499,7 +494,6 @@
         pl.BlockSpec((rows, columns), lambda i, spots: (spots[i], 0)),
         jax.ShapeDtypeStruct((2 * J * rows, columns), f32),
         scalars=1,
-        us=12,
     )(spots.astype(jnp.int32), *arrays)
 
 
@@ -681,15 +675,13 @@
     early = [x for pair in zip(hops[: S - 1], others[: S - 1]) for x in pair]
     early = tie(early, blocks)
     normed_rows = norm(early, places[:-CORES], gain_full, shift_full, S * CORES)
-    last = tie(hops[-1], normed_rows)
-    others.append(net.move(last, dc=1))
     blocks = tie(blocks, normed_rows)
     spots_w = jnp.concatenate([back_planes, (s * CORES + c)[None]]).astype(jnp.int32)
     chips = net.order()
     weights = lambda x, order, *before: assemble(
         w_fc1,
         w_qkv,
-        [y.reshape(S - 1, part, -1) for y in x],
+        [x.reshape(-1, S - 1, part, x.shape[-1])],
         order.astype(jnp.int32),
         spots_w,
         ff_own,
@@ -698,13 +690,15 @@
         *before,
     )
     weight_cols = weights(blocks, chips[: blocks.shape[0]])
-    last, other = tie((last, others[-1]), weight_cols)
+    last = tie(hops[-1], weight_cols)
+    other = net.move(last, dc=1)
+    if net.square:
+        weight_cols, came = tie((weight_cols, came), last)
+        weight_cols = weights(came, chips[2:], weight_cols)
+    last, other = tie((last, other), weight_cols)
     hidden_in, tok_rows, cot_rows, mean, inverse = norm(
         [last, other], places[-CORES:], gain_full, shift_full, S * CORES, normed_rows
     )
-    if net.square:
-        weight_cols, came = tie((weight_cols, came), hidden_in)
-        weight_cols = weights(came, chips[2:], weight_cols)
     fc1_cols = weight_cols[0].reshape(width, ff_own)
     qkv_cols = weight_cols[1].reshape(width, 3 * mix_own)
 
@@ -812,6 +806,11 @@
     fc1_part = tie(jnp.swapaxes(fc1_part, 0, 1).reshape(part, S * ff_own))
     step(None, fc1_part)
     fc1_came = net.gather(fc1_part)
+    if net.square:
+        fc2_last = net.move(step(fc2_came), dc=1)
+        fc2_mine, fc2_other = (fc2_part, fc2_came), (fc2_other, fc2_last)
+    else:
+        fc2_mine, fc2_other = (fc2_part, fc2_part), (fc2_other, fc2_other)
     branch_acts = add_in_order(*step((branch, branch_came)), back_planes.astype(jnp.int32))
     back_acts = add_in_order(*step((back, back_came)), back_planes.astype(jnp.int32))
     mark += [branch_acts, back_acts]
@@ -822,9 +821,10 @@
     mixed_part = tie(jnp.concatenate([mixed_part[:, :, : 3 * mix_own], riders], axis=1))
     step(None, mixed_part)
     mixed_part = swap(mixed_part)
+    fc2_own = place_rows(net, *step((fc2_mine, fc2_other)), factor)
+    step(None, fc2_own)
     fc1_other = net.move(step(fc1_part), dc=1)
     if net.square:
-        fc2_last = net.move(step(fc2_came), dc=1)
         fc1_came = step(fc1_came)
         mark += [fc1_came]
     mixed_part = step(mixed_part)
@@ -832,12 +832,13 @@
     mixed_part = jnp.concatenate([mixed_part[:, :part], out_part], axis=2)
     mixed_part = tie(jnp.swapaxes(mixed_part, 0, 1).reshape(part, S * 4 * mix_own))
     step(None, mixed_part)
-    mixed_came = net.gather(mixed_part)
+    mixed_first, mixed_second = net.gather(mixed_part), net.gather_more(mixed_part)
+    mixed_other = net.move(mixed_part, dc=1)
     if net.square:
         fc1_last = net.move(step(fc1_came), dc=1)
-        fc2_mine, fc2_other = (fc2_part, fc2_came), (fc2_other, fc2_last)
+        fc1_mine, fc1_other = (fc1_part, fc1_came), (fc1_other, fc1_last)
     else:
-        fc2_mine, fc2_other = (fc2_part, fc2_part), (fc2_other, fc2_other)
+        fc1_mine, fc1_other = (fc1_part, fc1_part), (fc1_other, fc1_other)
     count = riders.shape[1] // 2
     riders = step(riders)
     riders = (riders[:, :count] + riders[:, count:]).reshape(S, -1)[:, :riding]
@@ -852,25 +853,36 @@
     sums = tie(sums)
     step(None, sums)
     sums = net.plane_sum(sums, 0)
-    fc2_own = place_rows(net, *step((fc2_mine, fc2_other)), factor)
-    step(None, fc2_own)
-    mixed_part, mixed_came = second_gather(mixed_part, mixed_came)
-    mixed_other = net.move(mixed_part, dc=1)
     if net.square:
-        fc1_mine, fc1_other = (fc1_part, fc1_came), (fc1_other, fc1_last)
+        fc1_own = place_columns(net, *step((fc1_mine, fc1_other)), factor)
+        step(None, fc1_own)
+        own, other = step((mixed_part[None], mixed_other[None]))
+        placed = tie(place_mixed(net, own, other, 0, factor))
+        step(None, placed)
+        mixed_first, sums = tie(step((mixed_first, sums)))
+        step(None, mixed_first)
+        mixed_last = net.gather_more(mixed_first)
+        mixed_second = tie(step(mixed_second))
+        step(None, mixed_second)
+        first_other, second_other = net.move(mixed_first, dc=1), net.move(mixed_second, dc=1)
+        own, other = step((mixed_first[None], second_other[None]))
+        placed = tie(place_mixed(net, own, other, 1, factor, placed))
+        step(None, placed)
+        own, other = step((mixed_second[None], first_other[None]))
+        placed = tie(place_mixed(net, own, other, 2, factor, placed))
+        step(None, placed)
+        sums = net.plane_sum(tie(step(sums)), 1)
+        mixed_last = tie(step(mixed_last))
+        sums_came = net.move(tie(sums, mixed_last), dc=1)
+        last_other = net.move(mixed_last, dc=1)
+        placed = place_mixed(net, mixed_last[None], last_other[None], 3, factor, placed)
     else:
-        fc1_mine, fc1_other = (fc1_part, fc1_part), (fc1_other, fc1_other)
-    fc1_own = place_columns(net, *step((fc1_mine, fc1_other)), factor)
-    step(None, fc1_own)
-    if net.square:
-        mixed_came = tie(step(mixed_came))
-        mixed_last = net.move(mixed_came, dc=1)
-        mixed_mine, mixed_other = (mixed_part, mixed_came), (mixed_other, mixed_last)
-    else:
-        mixed_mine, mixed_other = (mixed_part, mixed_part), (mixed_other, mixed_other)
-    sums = net.plane_sum(tie(sums, mixed_mine), 1)
-    sums_came = net.move(sums, dc=1)
-    qkv_own, out_own = place_mixed(net, mixed_mine, mixed_other, factor)
+        mixed_near = lax.all_gather(mixed_part, "dp", axis_index_groups=net.groups())
+        fc1_own = place_columns(net, *step((fc1_mine, fc1_other)), factor)
+        sums = net.plane_sum(sums, 1)
+        sums_came = net.move(sums, dc=1)
+        placed = place_mixed(net, mixed_near, net.move(mixed_near, dc=1), 0, factor)
+    qkv_own, out_own = placed
     if out_own.ndim == 4:
         out_own = jnp.transpose(out_own, (2, 0, 1, 3)).reshape(height, width)
 

time: 467 us -> 459 us (0.983)
  waiting for transfers between devices: 166 us -> 152 us
    ppermute x36 -> x39, waiting for transfers between devices: 123 us -> 107 us  [move(): return lax.ppermute(x, AXES, pairs)]
    pallas_call x3 -> x6, Pallas kernels: 21.5 us -> 24.3 us  [the longest x4 17.2 us: place_mixed(): call(kernel, (count, planes), [pl.BlockSpec((None, part, columns), lambda...]
    ppermute x36 -> x39, starting transfers between devices: 30.7 us -> 33.1 us  [move(): return lax.ppermute(x, AXES, pairs)]
  transfers between devices with their start and end apart: 41 -> 44, of which waited for: 18 -> 19; matrix products, arithmetic and copies ran while one was open for 17% -> 17% of each run, Pallas kernels for 19% -> 22%
where the time goes in v1:
time: 459 us; the launch traced here: 452 us
  waiting for transfers between devices  152 us (33%)
  Pallas kernels  114 us (25%)
  starting transfers between devices  46.8 us (10%)
  matrix products  41.4 us (9%)
  local copies, waits for them, and re-layouts  40.1 us (9%)
  other arithmetic  37.3 us (8%)
  between operations  21.1 us (5%)
    ppermute x39, waiting for transfers between devices, move(): return lax.ppermute(x, AXES, pairs)  107 us
    all_to_all x3, waiting for transfers between devices, swap(): return lax.all_to_all(tie(x, *after), 'shard', 0, 0, tiled=True)  43.4 us
    ppermute x39, starting transfers between devices, move(): return lax.ppermute(x, AXES, pairs)  33.1 us
    unnamed x119, local copies, waits for them, and re-layouts  25 us
    pallas_call x4, Pallas kernels, place_mixed(): call(kernel, (count, planes), [pl.BlockSpec((None, part, columns), lambda...  17.2 us
    dot_general x4, matrix products, local(): jnp.einsum('td,te->de', x, y, preferred_element_type=f32).astype(bf16)  15 us
    pallas_call x1, Pallas kernels, place_columns(): call(kernel, (J, 2), [pl.BlockSpec((None, high, columns), lambda i, h, sp...  14.2 us
    all_to_all x3, starting transfers between devices, swap(): return lax.all_to_all(tie(x, *after), 'shard', 0, 0, tiled=True)  13.7 us
  transfers between devices with their start and end apart: 44, of which 19 were waited for; matrix products, arithmetic and copies ran while one was open for 17% of the time, Pallas kernels for 22%

profile of v1, /device:TPU:0, one launch (start us, length us, event | category | flops | bytes accessed | tf_op | source)
XLA Modules:
  0.0 452.0 jit_solution(10772219175571251948)
XLA Ops:
  13.2 5.1 %collective-permute-start.3 = (bf16[5760]{0:T(1024)(128)(2,1)S(1)}, bf16[5760]{0:T(1024)(128)(2,1)S(1)}, u32[]{:S(2)}, u32[]{:S(2)}) collective-permute-start(bf16[5760]{0:T(1024)(128)(2,1)S(1)} %dynamic-update-slice.6), channel_id=1, source_target_pairs={{0,3},{1,0},{2,1},{3,2},{4,7},{5,4},{6,5},{7,6},{8,11},{9,8},{10,9... | collective-permute-start | bytes 34568 | tf_op jit(solution)/shard_map/ppermute | solution.py:523
  54.8 31.1 %all-to-all-done = bf16[4,128,1792]{2,1,0:T(8,128)(2,1)} async-done(((bf16[4,128,1792]{2,1,0:T(8,128)(2,1)}), bf16[4,128,1792]{2,1,0:T(8,128)(2,1)}, u32[]{:S(2)}, u32[]{:S(2)}) %all-to-all-start) | async-done | bytes 1835040 | tf_op jit(solution)/shard_map/all_to_all | solution.py:576
  89.0 16.8 %collective-permute-done.8.refs_1_ = bf16[1,384,1792]{2,1,0:T(8,128)(2,1)S(1)} collective-permute-done((bf16[1,384,1792]{2,1,0:T(8,128)(2,1)S(1)}, bf16[1,384,1792]{2,1,0:T(8,128)(2,1)S(1)}, u32[]{:S(2)}, u32[]{:S(2)}) %collective-permute-start.8) | collective-permute-done | bytes 1376288 | tf_op jit(solution)/shard_map/ppermute | solution.py:523
  107.5 8.2 %collective-permute-done.7.refs_4_ = bf16[256,2048]{1,0:T(8,128)(2,1)S(1)} collective-permute-done((bf16[256,2048]{1,0:T(8,128)(2,1)}, bf16[256,2048]{1,0:T(8,128)(2,1)S(1)}, u32[]{:S(2)}, u32[]{:S(2)}) %collective-permute-start.7) | collective-permute-done | bytes 1048608 | tf_op jit(solution)/shard_map/ppermute | solution.py:523
  119.5 7.8 %shard_map.240 = (bf16[1024,2048]{1,0:T(8,128)(2,1)}, bf16[1024,2048]{1,0:T(8,128)(2,1)}, bf16[1024,2048]{1,0:T(8,128)(2,1)}, f32[1024,128]{1,0:T(8,128)S(1)}, f32[1024,128]{1,0:T(8,128)S(1)}) custom-call(s32[6]{0:T(128)S(1)} %copy-done.32, f32[1,2048]{1,0:T(1,128)S(1)} %bitcast.180, f32[1,2048]{1,0:T(1,128)S(1)} %bitcast.184, ...), custom_call_target="tpu_custom_call" | custom-call | tf_op jit(solution)/shard_map/pallas_call | solution.py:238
  132.8 10.6 %collective-permute-done.9.refs_0_ = bf16[256,2048]{1,0:T(8,128)(2,1)} collective-permute-done((bf16[256,2048]{1,0:T(8,128)(2,1)S(1)}, bf16[256,2048]{1,0:T(8,128)(2,1)}, u32[]{:S(2)}, u32[]{:S(2)}) %collective-permute-start.9) | collective-permute-done | bytes 1048608 | tf_op jit(solution)/shard_map/ppermute | solution.py:523
  155.4 11.0 %multiply_convert_fusion = (bf16[1024,1024]{1,0:T(8,128)(2,1)S(1)}, f32[1024,1024]{1,0:T(8,128)}) fusion(f32[1024]{0:T(1024)S(1)} %dynamic_slice.74, bf16[1024,2048]{1,0:T(8,128)(2,1)} %get-tuple-element.200, bf16[2048,1024]{1,0:T(8,128)(2,1)} %bitcast.201), kind=kOutput, calls=%fused_computation.12 | convolution fusion | flops 4305453056 | bytes 14684160 | tf_op jit(solution)/shard_map/dot_general | solution.py:705
  173.6 9.1 %fusion.6.hidden_ref = bf16[1024,1024]{1,0:T(8,128)(2,1)S(1)} fusion(f32[1024,1024]{1,0:T(8,128)} %get-tuple-element.311, f32[1024]{0:T(1024)S(1)} %dynamic_slice.74, bf16[1024,2048]{1,0:T(8,128)(2,1)S(1)} %copy-done.40, bf16[1024,2048]{1,0:T(8,128)(2,1)S(1)} %copy-done.43), kind=kOutput, calls=%fused_computation.9 | convolution fusion | flops 4316987392 | bytes 14684160 | tf_op jit(solution)/shard_map/td,fd->tf/dot_general | solution.py:751
  191.8 6.1 %collective-permute-done.13 = bf16[2,1,256,2048]{3,2,1,0:T(8,128)(2,1)S(1)} collective-permute-done((bf16[2,1,256,2048]{3,2,1,0:T(8,128)(2,1)S(1)}, bf16[2,1,256,2048]{3,2,1,0:T(8,128)(2,1)S(1)}, u32[]{:S(2)}, u32[]{:S(2)}) %collective-permute-start.13) | collective-permute-done | bytes 2097184 | tf_op jit(solution)/shard_map/ppermute | solution.py:523
  199.2 5.1 %broadcast_add_fusion.mixed_ref = f32[1024,768]{1,0:T(8,128)} fusion(f32[768]{0:T(1024)S(1)} %reshape.342, bf16[1024,2048]{1,0:T(8,128)(2,1)S(1)} %copy-done.45, bf16[2048,768]{1,0:T(8,128)(2,1)S(1)} %bitcast.173), kind=kOutput, calls=%fused_computation.34 | convolution fusion | flops 3222011904 | bytes 10488832 | tf_op jit(solution)/shard_map/dot_general | solution.py:757
  205.8 12.2 %shard_map.244 = (bf16[1024,256]{1,0:T(8,128)(2,1)S(1)}, bf16[1024,768]{1,0:T(8,128)(2,1)S(1)}) custom-call(s32[1024,128]{1,0:T(8,128)S(1)} %copy-done.30, f32[1024,128]{1,0:T(8,128)S(1)} %copy-done.29, f32[1024,128]{1,0:T(8,128)S(1)} %copy-done.28, f32[1024,128]{1,0:T(8,128)S(1)} %copy-done.27, f32[1024,768]{1,0:T(8,128)} %broadcast_add_fusion.mixed_ref, ...), custom_call_target="tpu_custom_call" | custom-call | flops 4000000000 | tf_op jit(solution)/shard_map/pallas_call | solution.py:94
  218.1 13.5 %collective-permute-done.15 = bf16[2,4,128,1024]{3,2,1,0:T(8,128)(2,1)S(1)} collective-permute-done((bf16[2,4,128,1024]{3,2,1,0:T(8,128)(2,1)}, bf16[2,4,128,1024]{3,2,1,0:T(8,128)(2,1)S(1)}, u32[]{:S(2)}, u32[]{:S(2)}) %collective-permute-start.15) | collective-permute-done | bytes 2097184 | tf_op jit(solution)/shard_map/ppermute | solution.py:523
  245.8 14.3 %collective-permute-done.17 = bf16[4,128,1024]{2,1,0:T(8,128)(2,1)S(1)} collective-permute-done((bf16[4,128,1024]{2,1,0:T(8,128)(2,1)S(1)}, bf16[4,128,1024]{2,1,0:T(8,128)(2,1)S(1)}, u32[]{:S(2)}, u32[]{:S(2)}) %collective-permute-start.17) | collective-permute-done | bytes 1048608 | tf_op jit(solution)/shard_map/ppermute | solution.py:523
  271.8 9.5 %shard_map.246 = (f32[512,2048]{1,0:T(8,128)}, bf16[512,2048]{1,0:T(8,128)(2,1)S(1)}) custom-call(bf16[1024,256]{1,0:T(8,128)(2,1)S(1)} %copy-done.37, bf16[256,2048]{1,0:T(8,128)(2,1)S(1)} %copy-done.16, bf16[1024,1024]{1,0:T(8,128)(2,1)S(1)} %copy-done.35, bf16[1024,2048]{1,0:T(8,128)(2,1)} %constant_dynamic-slice_fusion.6.fc2_ref), custom_call_target="tpu_custom_call" | custom-call | flops 3333333248 | tf_op jit(solution)/shard_map/pallas_call | solution.py:325
  282.8 13.3 %shard_map.247 = (f32[512,2048]{1,0:T(8,128)}, bf16[512,2048]{1,0:T(8,128)(2,1)}, f32[8,2048]{1,0:T(8,128)S(1)}) custom-call(bf16[1024,1024]{1,0:T(8,128)(2,1)} %copy-done.48, bf16[2048,1024]{1,0:T(8,128)(2,1)} %bitcast.202, bf16[1024,768]{1,0:T(8,128)(2,1)S(1)} %copy-done.10, bf16[2048,768]{1,0:T(8,128)(2,1)} %bitcast.172, ...), custom_call_target="tpu_custom_call" | custom-call | flops 4666666496 | tf_op jit(solution)/shard_map/pallas_call | solution.py:355
  308.1 5.2 %shard_map.249 = bf16[4,128,2048]{2,1,0:T(8,128)(2,1)} custom-call(s32[4]{0:T(128)S(1)} %and_select_fusion.2.order_ref, f32[512,2048]{1,0:T(8,128)} %get-tuple-element.233.mine_ref, bf16[512,2048]{1,0:T(8,128)(2,1)} %collective-permute-done.21.came_ref), custom_call_target="tpu_custom_call" | custom-call | tf_op jit(solution)/shard_map/pallas_call | solution.py:303
  318.3 4.9 %shard_map.248 = bf16[4,128,2048]{2,1,0:T(8,128)(2,1)} custom-call(s32[4]{0:T(128)S(1)} %and_select_fusion.2.order_ref, f32[512,2048]{1,0:T(8,128)} %get-tuple-element.231.mine_ref, bf16[512,2048]{1,0:T(8,128)(2,1)S(1)} %collective-permute-done.18.came_ref), custom_call_target="tpu_custom_call" | custom-call | tf_op jit(solution)/shard_map/pallas_call | solution.py:303
  323.2 16.8 %collective-permute-done.23 = bf16[128,4096]{1,0:T(8,128)(2,1)} collective-permute-done((bf16[128,4096]{1,0:T(8,128)(2,1)S(1)}, bf16[128,4096]{1,0:T(8,128)(2,1)}, u32[]{:S(2)}, u32[]{:S(2)}) %collective-permute-start.23) | collective-permute-done | bytes 1048608 | tf_op jit(solution)/shard_map/ppermute | solution.py:523
  346.0 5.0 %all-to-all-start.2 = ((bf16[4,144,768]{2,1,0:T(8,128)(2,1)}), bf16[4,144,768]{2,1,0:T(8,128)(2,1)}, u32[]{:S(2)}, u32[]{:S(2)}) async-start(bf16[4,144,768]{2,1,0:T(8,128)(2,1)} %pad_maximum_fusion.5), calls=%async_computation.4 | async-start | bytes 1769472 | tf_op jit(solution)/shard_map/all_to_all | solution.py:576
  352.0 11.9 %shard_map.251 = f32[2048,2048]{1,0:T(8,128)} custom-call(s32[8]{0:T(128)S(1)} %pad_add_fusion.4.spots_ref, bf16[2,256,2048]{2,1,0:T(8,128)(2,1)S(1)} %shard_map.245.refs_0_, bf16[2,256,2048]{2,1,0:T(8,128)(2,1)} %collective-permute-done.19.refs_1_, bf16[2,256,2048]{2,1,0:T(8,128)(2,1)} %collective-permute-done.24.refs_2_, ...), custom_call_target="tpu_custom_call" | custom-call | tf_op jit(solution)/shard_map/pallas_call | solution.py:490
  363.9 5.0 %collective-permute-done.26.m1_ref = bf16[2,128,4096]{2,1,0:T(8,128)(2,1)} collective-permute-done((bf16[2,128,4096]{2,1,0:T(8,128)(2,1)}, bf16[2,128,4096]{2,1,0:T(8,128)(2,1)}, u32[]{:S(2)}, u32[]{:S(2)}) %collective-permute-start.26) | collective-permute-done | bytes 2097184 | tf_op jit(solution)/shard_map/ppermute | solution.py:523
  368.9 12.3 %all-to-all-done.2 = bf16[4,144,768]{2,1,0:T(8,128)(2,1)} async-done(((bf16[4,144,768]{2,1,0:T(8,128)(2,1)}), bf16[4,144,768]{2,1,0:T(8,128)(2,1)}, u32[]{:S(2)}, u32[]{:S(2)}) %all-to-all-start.2) | async-done | bytes 884768 | tf_op jit(solution)/shard_map/all_to_all | solution.py:576
  390.4 14.2 %shard_map.252 = f32[512,8192]{1,0:T(8,128)} custom-call(s32[6]{0:T(128)S(1)} %concatenate.75.spots_ref, bf16[2,128,4096]{2,1,0:T(8,128)(2,1)} %shard_map.250.m0_ref, bf16[2,128,4096]{2,1,0:T(8,128)(2,1)} %collective-permute-done.26.m1_ref, bf16[2,128,4096]{2,1,0:T(8,128)(2,1)} %collective-permute-done.30.o0_ref, ...), custom_call_target="tpu_custom_call" | custom-call | tf_op jit(solution)/shard_map/pallas_call | solution.py:400
  419.0 4.9 %shard_map.254 = (f32[512,6144]{1,0:T(8,128)}, f32[512,2048]{1,0:T(8,128)}) custom-call(s32[3]{0:T(128)S(1)} %add_add_fusion.4.spots_ref, bf16[1,128,4096]{2,1,0:T(8,128)(2,1)} %bitcast.67.mine_ref, bf16[1,128,4096]{2,1,0:T(8,128)(2,1)S(1)} %bitcast.178, f32[512,6144]{1,0:T(8,128)} %get-tuple-element.256.refs_0_, ...), custom_call_target="tpu_custom_call", output_to_operand_aliasing={{0}: (3, {}), {1}: (4, {})} | custom-call | tf_op jit(solution)/shard_map/pallas_call | solution.py:452
  (319 shorter events, 176.9 us)
Async XLA Ops:
  13.2 31.0 %collective-permute-start.3 = (bf16[5760]{0:T(1024)(128)(2,1)S(1)}, bf16[5760]{0:T(1024)(128)(2,1)S(1)}, u32[]{:S(2)}, u32[]{:S(2)}) collective-permute-start(bf16[5760]{0:T(1024)(128)(2,1)S(1)} %dynamic-update-slice.6), channel_id=1, source_target_pairs={{0,3},{1,0},{2,1},{3,2},{4,7},{5,4},{6,5},{7,6},{8,11},{9,8},{10,9... | collective-permute-start | bytes 34568 | tf_op jit(solution)/shard_map/ppermute | solution.py:523
  18.2 25.9 %collective-permute-start.2 = (bf16[5760]{0:T(1024)(128)(2,1)S(1)}, bf16[5760]{0:T(1024)(128)(2,1)S(1)}, u32[]{:S(2)}, u32[]{:S(2)}) collective-permute-start(bf16[5760]{0:T(1024)(128)(2,1)S(1)} %dynamic-update-slice.6), channel_id=1, source_target_pairs={{0,2},{1,3},{2,0},{3,1},{4,6},{5,7},{6,4},{7,5},{8,10},{9,11},{10,... | collective-permute-start | bytes 34568 | tf_op jit(solution)/shard_map/ppermute | solution.py:523
  18.2 25.9 %collective-permute-start.1 = (bf16[5760]{0:T(1024)(128)(2,1)S(1)}, bf16[5760]{0:T(1024)(128)(2,1)S(1)}, u32[]{:S(2)}, u32[]{:S(2)}) collective-permute-start(bf16[5760]{0:T(1024)(128)(2,1)S(1)} %dynamic-update-slice.6), channel_id=1, source_target_pairs={{0,1},{1,2},{2,3},{3,0},{4,5},{5,6},{6,7},{7,4},{8,9},{9,10},{10,1... | collective-permute-start | bytes 34568 | tf_op jit(solution)/shard_map/ppermute | solution.py:523
  20.5 28.2 %collective-permute-start = (bf16[256,2048]{1,0:T(8,128)(2,1)S(1)}, bf16[256,2048]{1,0:T(8,128)(2,1)}, u32[]{:S(2)}, u32[]{:S(2)}) collective-permute-start(bf16[256,2048]{1,0:T(8,128)(2,1)S(1)} %pad_maximum_fusion.4.refs_0_), channel_id=1, source_target_pairs={{0,1},{1,2},{2,3},{3,0},{4,5},{5,6},{6,7},{7,4},{8,9},{9,10},{10,1... | collective-permute-start | bytes 3145736 | tf_op jit(solution)/shard_map/ppermute | solution.py:523
  27.3 58.6 %all-to-all-start = ((bf16[4,128,1792]{2,1,0:T(8,128)(2,1)}), bf16[4,128,1792]{2,1,0:T(8,128)(2,1)}, u32[]{:S(2)}, u32[]{:S(2)}) async-start(bf16[4,128,1792]{2,1,0:T(8,128)(2,1)} %copy-done.2), calls=%async_computation | async-start | bytes 3670016 | tf_op jit(solution)/shard_map/all_to_all | solution.py:576
  89.0 26.8 %collective-permute-start.7 = (bf16[256,2048]{1,0:T(8,128)(2,1)}, bf16[256,2048]{1,0:T(8,128)(2,1)S(1)}, u32[]{:S(2)}, u32[]{:S(2)}) collective-permute-start(bf16[256,2048]{1,0:T(8,128)(2,1)} %collective-permute-done.refs_2_), channel_id=1, source_target_pairs={{0,1},{1,2},{2,3},{3,0},{4,5},{5,6},{6,7},{7,4},{8,9},{9,10},{10,1... | collective-permute-start | bytes 3145736 | tf_op jit(solution)/shard_map/ppermute | solution.py:523
  106.0 37.5 %collective-permute-start.12 = (bf16[2,384,1792]{2,1,0:T(8,128)(2,1)S(1)}, bf16[2,384,1792]{2,1,0:T(8,128)(2,1)}, u32[]{:S(2)}, u32[]{:S(2)}) collective-permute-start(bf16[2,384,1792]{2,1,0:T(8,128)(2,1)S(1)} %shard_map.239), channel_id=1, source_target_pairs={{0,8},{1,9},{2,10},{3,11},{4,20},{5,21},{6,22},{7,23},{8,0},{9,1},... | collective-permute-start | bytes 8257544 | tf_op jit(solution)/shard_map/ppermute | solution.py:523
  115.8 27.7 %collective-permute-start.9 = (bf16[256,2048]{1,0:T(8,128)(2,1)S(1)}, bf16[256,2048]{1,0:T(8,128)(2,1)}, u32[]{:S(2)}, u32[]{:S(2)}) collective-permute-start(bf16[256,2048]{1,0:T(8,128)(2,1)S(1)} %collective-permute-done.7.refs_4_), channel_id=1, source_target_pairs={{0,1},{1,2},{2,3},{3,0},{4,5},{5,6},{6,7},{7,4},{8,9},{9,10},{10,1... | collective-permute-start | bytes 3145736 | tf_op jit(solution)/shard_map/ppermute | solution.py:523
  171.8 26.1 %collective-permute-start.13 = (bf16[2,1,256,2048]{3,2,1,0:T(8,128)(2,1)S(1)}, bf16[2,1,256,2048]{3,2,1,0:T(8,128)(2,1)S(1)}, u32[]{:S(2)}, u32[]{:S(2)}) collective-permute-start(bf16[2,1,256,2048]{3,2,1,0:T(8,128)(2,1)S(1)} %pad_maximum_fusion.1), channel_id=1, source_target_pairs={{0,16},{1,17},{2,18},{3,19},{4,12},{5,13},{6,14},{7,15},{8,24},{9,... | collective-permute-start | bytes 6291464 | tf_op jit(solution)/shard_map/ppermute | solution.py:523
  190.3 41.3 %collective-permute-start.15 = (bf16[2,4,128,1024]{3,2,1,0:T(8,128)(2,1)}, bf16[2,4,128,1024]{3,2,1,0:T(8,128)(2,1)S(1)}, u32[]{:S(2)}, u32[]{:S(2)}) collective-permute-start(bf16[2,4,128,1024]{3,2,1,0:T(8,128)(2,1)} %pad_maximum_fusion.2), channel_id=1, source_target_pairs={{0,16},{1,17},{2,18},{3,19},{4,12},{5,13},{6,14},{7,15},{8,24},{9,... | collective-permute-start | bytes 6291464 | tf_op jit(solution)/shard_map/ppermute | solution.py:523
  198.6 36.3 %collective-permute-start.14 = (bf16[1,256,2048]{2,1,0:T(8,128)(2,1)S(1)}, bf16[1,256,2048]{2,1,0:T(8,128)(2,1)S(1)}, u32[]{:S(2)}, u32[]{:S(2)}) collective-permute-start(bf16[1,256,2048]{2,1,0:T(8,128)(2,1)S(1)} %get-tuple-element.189), channel_id=1, source_target_pairs={{0,8},{1,9},{2,10},{3,11},{4,20},{5,21},{6,22},{7,23},{8,0},{9,1},... | collective-permute-start | bytes 3145736 | tf_op jit(solution)/shard_map/ppermute | solution.py:523
  235.3 30.5 %collective-permute-start.16 = (bf16[256,2048]{1,0:T(8,128)(2,1)S(1)}, bf16[256,2048]{1,0:T(8,128)(2,1)S(1)}, u32[]{:S(2)}, u32[]{:S(2)}) collective-permute-start(bf16[256,2048]{1,0:T(8,128)(2,1)S(1)} %bitcast.169), channel_id=1, source_target_pairs={{0,16},{1,17},{2,18},{3,19},{4,12},{5,13},{6,14},{7,15},{8,24},{9,... | collective-permute-start | bytes 3145736 | tf_op jit(solution)/shard_map/ppermute | solution.py:523
  245.3 57.6 %collective-permute-start.20 = (bf16[2,4,128,1024]{3,2,1,0:T(8,128)(2,1)}, bf16[2,4,128,1024]{3,2,1,0:T(8,128)(2,1)}, u32[]{:S(2)}, u32[]{:S(2)}) collective-permute-start(bf16[2,4,128,1024]{3,2,1,0:T(8,128)(2,1)} %pad_maximum_fusion.3), channel_id=1, source_target_pairs={{0,16},{1,17},{2,18},{3,19},{4,12},{5,13},{6,14},{7,15},{8,24},{9,... | collective-permute-start | bytes 6291464 | tf_op jit(solution)/shard_map/ppermute | solution.py:523
  261.5 45.3 %all-to-all-start.1 = ((bf16[4,128,1024]{2,1,0:T(8,128)(2,1)}), bf16[4,128,1024]{2,1,0:T(8,128)(2,1)}, u32[]{:S(2)}, u32[]{:S(2)}) async-start(bf16[4,128,1024]{2,1,0:T(8,128)(2,1)} %add_convert_fusion.1), calls=%async_computation.1 | async-start | bytes 2097152 | tf_op jit(solution)/shard_map/all_to_all | solution.py:576
  265.7 151.7 %reduce-scatter.5.cloned.1.call-start = ((), (), s32[]{:S(2)}) async-start(), calls=%async_computation.6 | async-start | bytes 2621440 | tf_op jit(solution)/shard_map/reduce_scatter | solution.py:788
  268.3 38.5 %collective-permute-start.19 = (bf16[2,256,2048]{2,1,0:T(8,128)(2,1)S(1)}, bf16[2,256,2048]{2,1,0:T(8,128)(2,1)}, u32[]{:S(2)}, u32[]{:S(2)}) collective-permute-start(bf16[2,256,2048]{2,1,0:T(8,128)(2,1)S(1)} %shard_map.245.refs_0_), channel_id=1, source_target_pairs={{0,8},{1,9},{2,10},{3,11},{4,20},{5,21},{6,22},{7,23},{8,0},{9,1},... | collective-permute-start | bytes 6291464 | tf_op jit(solution)/shard_map/ppermute | solution.py:523
  313.9 26.1 %collective-permute-start.23 = (bf16[128,4096]{1,0:T(8,128)(2,1)S(1)}, bf16[128,4096]{1,0:T(8,128)(2,1)}, u32[]{:S(2)}, u32[]{:S(2)}) collective-permute-start(bf16[128,4096]{1,0:T(8,128)(2,1)S(1)} %bitcast.170), channel_id=1, source_target_pairs={{0,16},{1,17},{2,18},{3,19},{4,12},{5,13},{6,14},{7,15},{8,24},{9,... | collective-permute-start | bytes 3145736 | tf_op jit(solution)/shard_map/ppermute | solution.py:523
  315.7 27.6 %collective-permute-start.22 = (bf16[4,128,1024]{2,1,0:T(8,128)(2,1)}, bf16[4,128,1024]{2,1,0:T(8,128)(2,1)}, u32[]{:S(2)}, u32[]{:S(2)}) collective-permute-start(bf16[4,128,1024]{2,1,0:T(8,128)(2,1)} %get-tuple-element.229), channel_id=1, source_target_pairs={{0,8},{1,9},{2,10},{3,11},{4,20},{5,21},{6,22},{7,23},{8,0},{9,1},... | collective-permute-start | bytes 3145736 | tf_op jit(solution)/shard_map/ppermute | solution.py:523
  316.5 35.4 %collective-permute-start.24 = (bf16[2,256,2048]{2,1,0:T(8,128)(2,1)S(1)}, bf16[2,256,2048]{2,1,0:T(8,128)(2,1)}, u32[]{:S(2)}, u32[]{:S(2)}) collective-permute-start(bf16[2,256,2048]{2,1,0:T(8,128)(2,1)S(1)} %shard_map.245.refs_0_), channel_id=1, source_target_pairs={{0,4},{1,5},{2,6},{3,7},{4,0},{5,1},{6,2},{7,3},{8,12},{9,13},{10,... | collective-permute-start | bytes 6291464 | tf_op jit(solution)/shard_map/ppermute | solution.py:523
  317.9 34.1 %collective-permute-start.25 = (bf16[2,256,2048]{2,1,0:T(8,128)(2,1)}, bf16[2,256,2048]{2,1,0:T(8,128)(2,1)}, u32[]{:S(2)}, u32[]{:S(2)}) collective-permute-start(bf16[2,256,2048]{2,1,0:T(8,128)(2,1)} %collective-permute-done.19.refs_1_), channel_id=1, source_target_pairs={{0,4},{1,5},{2,6},{3,7},{4,0},{5,1},{6,2},{7,3},{8,12},{9,13},{10,... | collective-permute-start | bytes 6291464 | tf_op jit(solution)/shard_map/ppermute | solution.py:523
  342.6 26.4 %collective-permute-start.26 = (bf16[2,128,4096]{2,1,0:T(8,128)(2,1)}, bf16[2,128,4096]{2,1,0:T(8,128)(2,1)}, u32[]{:S(2)}, u32[]{:S(2)}) collective-permute-start(bf16[2,128,4096]{2,1,0:T(8,128)(2,1)} %shard_map.250.m0_ref), channel_id=1, source_target_pairs={{0,8},{1,9},{2,10},{3,11},{4,20},{5,21},{6,22},{7,23},{8,0},{9,1},... | collective-permute-start | bytes 6291464 | tf_op jit(solution)/shard_map/ppermute | solution.py:523
  346.0 35.2 %all-to-all-start.2 = ((bf16[4,144,768]{2,1,0:T(8,128)(2,1)}), bf16[4,144,768]{2,1,0:T(8,128)(2,1)}, u32[]{:S(2)}, u32[]{:S(2)}) async-start(bf16[4,144,768]{2,1,0:T(8,128)(2,1)} %pad_maximum_fusion.5), calls=%async_computation.4 | async-start | bytes 1769472 | tf_op jit(solution)/shard_map/all_to_all | solution.py:576
  351.0 81.7 %reduce-scatter.3.cloned.1.call-start = ((), (), s32[]{:S(2)}) async-start(), calls=%async_computation.5 | async-start | bytes 2621440 | tf_op jit(solution)/shard_map/reduce_scatter | solution.py:788
  363.9 26.4 %collective-permute-start.30 = (bf16[2,128,4096]{2,1,0:T(8,128)(2,1)}, bf16[2,128,4096]{2,1,0:T(8,128)(2,1)}, u32[]{:S(2)}, u32[]{:S(2)}) collective-permute-start(bf16[2,128,4096]{2,1,0:T(8,128)(2,1)} %shard_map.250.m0_ref), channel_id=1, source_target_pairs={{0,4},{1,5},{2,6},{3,7},{4,0},{5,1},{6,2},{7,3},{8,12},{9,13},{10,... | collective-permute-start | bytes 6291464 | tf_op jit(solution)/shard_map/ppermute | solution.py:523
  (73 other events, 681.4 us)
Sparse Core Ops, SparseCore 0:
  313.5 47.4 reduce-scatter.4
  363.4 47.6 reduce-scatter.2

commit v2 on v1

--- a/solution.py
+++ b/solution.py
@@ -100,7 +100,7 @@
             jax.ShapeDtypeStruct((rows, width), bf16),
             jax.ShapeDtypeStruct((rows, 3 * width), bf16),
         ],
-        cost_estimate=pl.CostEstimate(flops=4 * 10**9, bytes_accessed=0, transcendentals=0),
+        cost_estimate=pl.CostEstimate(flops=2 * 10**9, bytes_accessed=0, transcendentals=0),
         compiler_params=pltpu.CompilerParams(vmem_limit_bytes=VMEM),
     )(*tables, mixed, outer)
 
@@ -112,7 +112,7 @@
             num_scalar_prefetch=scalars, grid=grid, in_specs=in_specs, out_specs=out_specs
         ),
         out_shape=out_shape,
-        cost_estimate=pl.CostEstimate(flops=us * 10**9 // 3, bytes_accessed=0, transcendentals=0),
+        cost_estimate=pl.CostEstimate(flops=us * 10**9 // 6, bytes_accessed=0, transcendentals=0),
         compiler_params=pltpu.CompilerParams(vmem_limit_bytes=VMEM),
         **more,
     )
@@ -812,7 +812,9 @@
     else:
         fc2_mine, fc2_other = (fc2_part, fc2_part), (fc2_other, fc2_other)
     branch_acts = add_in_order(*step((branch, branch_came)), back_planes.astype(jnp.int32))
-    back_acts = add_in_order(*step((back, back_came)), back_planes.astype(jnp.int32))
+    back_acts = add_in_order(
+        *step(tie((back, back_came), branch_acts)), back_planes.astype(jnp.int32)
+    )
     mark += [branch_acts, back_acts]
     fc1_part, fc1_came = second_gather(fc1_part, fc1_came)
     branch_sum, back_sum = scatter(branch_acts), scatter(back_acts)

time: 459 us -> 452 us (0.985)
  local copies, waits for them, and re-layouts: 40.1 us -> 33.6 us
  matrix products: 41.4 us -> 36.3 us
    unnamed x119, local copies, waits for them, and re-layouts: 25 us -> 18.7 us
  transfers between devices with their start and end apart: 44 -> 44, of which waited for: 19 -> 19; matrix products, arithmetic and copies ran while one was open for 17% -> 17% of each run, Pallas kernels for 22% -> 23%
where the time goes in v2:
time: 452 us; the launch traced here: 446 us
  waiting for transfers between devices  151 us (33%)
  Pallas kernels  117 us (26%)
  starting transfers between devices  44.3 us (10%)
  other arithmetic  41.5 us (9%)
  matrix products  36.3 us (8%)
  local copies, waits for them, and re-layouts  33.6 us (7%)
  between operations  21.2 us (5%)
    ppermute x39, waiting for transfers between devices, move(): return lax.ppermute(x, AXES, pairs)  110 us
    all_to_all x3, waiting for transfers between devices, swap(): return lax.all_to_all(tie(x, *after), 'shard', 0, 0, tiled=True)  40.5 us
    ppermute x39, starting transfers between devices, move(): return lax.ppermute(x, AXES, pairs)  31.3 us
    unnamed x119, local copies, waits for them, and re-layouts  18.7 us
    pallas_call x4, Pallas kernels, place_mixed(): call(kernel, (count, planes), [pl.BlockSpec((None, part, columns), lambda...  17.2 us
    dot_general x4, matrix products, local(): jnp.einsum('td,te->de', x, y, preferred_element_type=f32).astype(bf16)  14.8 us
    pallas_call x1, Pallas kernels, place_columns(): call(kernel, (J, 2), [pl.BlockSpec((None, high, columns), lambda i, h, sp...  14.3 us
    pallas_call x2, Pallas kernels, norm(): call(kernel, (len(arrays),), [line, line] + [pl.BlockSpec(x.shape, lambda...  13.4 us
  transfers between devices with their start and end apart: 44, of which 19 were waited for; matrix products, arithmetic and copies ran while one was open for 17% of the time, Pallas kernels for 23%

profile of v2, /device:TPU:0, one launch (start us, length us, event | category | flops | bytes accessed | tf_op | source)
XLA Modules:
  0.0 445.5 jit_solution(16329136664600901712)
XLA Ops:
  13.2 5.1 %collective-permute-start.3 = (bf16[5760]{0:T(1024)(128)(2,1)S(1)}, bf16[5760]{0:T(1024)(128)(2,1)S(1)}, u32[]{:S(2)}, u32[]{:S(2)}) collective-permute-start(bf16[5760]{0:T(1024)(128)(2,1)S(1)} %dynamic-update-slice.6), channel_id=1, source_target_pairs={{0,3},{1,0},{2,1},{3,2},{4,7},{5,4},{6,5},{7,6},{8,11},{9,8},{10,9... | collective-permute-start | bytes 34568 | tf_op jit(solution)/shard_map/ppermute | solution.py:523
  54.5 31.3 %all-to-all-done = bf16[4,128,1792]{2,1,0:T(8,128)(2,1)} async-done(((bf16[4,128,1792]{2,1,0:T(8,128)(2,1)}), bf16[4,128,1792]{2,1,0:T(8,128)(2,1)}, u32[]{:S(2)}, u32[]{:S(2)}) %all-to-all-start) | async-done | bytes 1835040 | tf_op jit(solution)/shard_map/all_to_all | solution.py:576
  88.9 16.8 %collective-permute-done.8.refs_1_ = bf16[1,384,1792]{2,1,0:T(8,128)(2,1)S(1)} collective-permute-done((bf16[1,384,1792]{2,1,0:T(8,128)(2,1)S(1)}, bf16[1,384,1792]{2,1,0:T(8,128)(2,1)S(1)}, u32[]{:S(2)}, u32[]{:S(2)}) %collective-permute-start.8) | collective-permute-done | bytes 1376288 | tf_op jit(solution)/shard_map/ppermute | solution.py:523
  108.9 6.9 %collective-permute-done.7.refs_4_ = bf16[256,2048]{1,0:T(8,128)(2,1)S(1)} collective-permute-done((bf16[256,2048]{1,0:T(8,128)(2,1)}, bf16[256,2048]{1,0:T(8,128)(2,1)S(1)}, u32[]{:S(2)}, u32[]{:S(2)}) %collective-permute-start.7) | collective-permute-done | bytes 1048608 | tf_op jit(solution)/shard_map/ppermute | solution.py:523
  119.4 7.8 %shard_map.240 = (bf16[1024,2048]{1,0:T(8,128)(2,1)}, bf16[1024,2048]{1,0:T(8,128)(2,1)}, bf16[1024,2048]{1,0:T(8,128)(2,1)}, f32[1024,128]{1,0:T(8,128)S(1)}, f32[1024,128]{1,0:T(8,128)S(1)}) custom-call(s32[6]{0:T(128)S(1)} %copy-done.31, f32[1,2048]{1,0:T(1,128)S(1)} %bitcast.180, f32[1,2048]{1,0:T(1,128)S(1)} %bitcast.184, ...), custom_call_target="tpu_custom_call" | custom-call | tf_op jit(solution)/shard_map/pallas_call | solution.py:238
  132.0 11.4 %collective-permute-done.9.refs_0_ = bf16[256,2048]{1,0:T(8,128)(2,1)} collective-permute-done((bf16[256,2048]{1,0:T(8,128)(2,1)S(1)}, bf16[256,2048]{1,0:T(8,128)(2,1)}, u32[]{:S(2)}, u32[]{:S(2)}) %collective-permute-start.9) | collective-permute-done | bytes 1048608 | tf_op jit(solution)/shard_map/ppermute | solution.py:523
  147.6 5.7 %shard_map.243 = (bf16[1024,2048]{1,0:T(8,128)(2,1)}, bf16[1024,2048]{1,0:T(8,128)(2,1)}, bf16[1024,2048]{1,0:T(8,128)(2,1)}, f32[1024,128]{1,0:T(8,128)S(1)}, f32[1024,128]{1,0:T(8,128)S(1)}) custom-call(s32[2]{0:T(128)S(1)} %copy-done.30, f32[1,2048]{1,0:T(1,128)S(1)} %bitcast.181, ...), custom_call_target="tpu_custom_call", output_to_operand_aliasing={{0}: (5, {}), {1}: (6, {}), {2}: (7, {}), {3}: (8, {}), {4}... | custom-call | tf_op jit(solution)/shard_map/pallas_call | solution.py:238
  153.3 7.7 %multiply_convert_fusion = (bf16[1024,1024]{1,0:T(8,128)(2,1)S(1)}, f32[1024,1024]{1,0:T(8,128)S(1)}) fusion(f32[1024]{0:T(1024)S(1)} %dynamic_slice.74, bf16[1024,2048]{1,0:T(8,128)(2,1)} %get-tuple-element.202, bf16[2048,1024]{1,0:T(8,128)(2,1)S(1)} %bitcast.197), kind=kOutput, calls=%fused_computation.12 | convolution fusion | flops 4305453056 | bytes 14684160 | tf_op jit(solution)/shard_map/dot_general | solution.py:705
  170.6 7.3 %fusion.6.hidden_ref = bf16[1024,1024]{1,0:T(8,128)(2,1)S(1)} fusion(f32[1024,1024]{1,0:T(8,128)S(1)} %get-tuple-element.315, f32[1024]{0:T(1024)S(1)} %dynamic_slice.74, bf16[1024,2048]{1,0:T(8,128)(2,1)S(1)} %copy-done.35, bf16[1024,2048]{1,0:T(8,128)(2,1)S(1)} %copy-done.34), kind=kOutput, calls=%fused_computation.9 | convolution fusion | flops 4316987392 | bytes 14684160 | tf_op jit(solution)/shard_map/td,fd->tf/dot_general | solution.py:751
  186.9 8.5 %collective-permute-done.13 = bf16[2,1,256,2048]{3,2,1,0:T(8,128)(2,1)} collective-permute-done((bf16[2,1,256,2048]{3,2,1,0:T(8,128)(2,1)}, bf16[2,1,256,2048]{3,2,1,0:T(8,128)(2,1)}, u32[]{:S(2)}, u32[]{:S(2)}) %collective-permute-start.13) | collective-permute-done | bytes 2097184 | tf_op jit(solution)/shard_map/ppermute | solution.py:523
  200.4 5.1 %broadcast_add_fusion.mixed_ref = f32[1024,768]{1,0:T(8,128)} fusion(f32[768]{0:T(1024)S(1)} %reshape.342, bf16[1024,2048]{1,0:T(8,128)(2,1)S(1)} %copy-done.47, bf16[2048,768]{1,0:T(8,128)(2,1)S(1)} %bitcast.164), kind=kOutput, calls=%fused_computation.34 | convolution fusion | flops 3222011904 | bytes 10488832 | tf_op jit(solution)/shard_map/dot_general | solution.py:757
  207.0 12.3 %shard_map.244 = (bf16[1024,256]{1,0:T(8,128)(2,1)S(1)}, bf16[1024,768]{1,0:T(8,128)(2,1)S(1)}) custom-call(s32[1024,128]{1,0:T(8,128)S(1)} %copy-done.27, f32[1024,128]{1,0:T(8,128)S(1)} %copy-done.26, f32[1024,128]{1,0:T(8,128)S(1)} %copy-done.25, f32[1024,128]{1,0:T(8,128)S(1)} %copy-done.24, f32[1024,768]{1,0:T(8,128)} %broadcast_add_fusion.mixed_ref, ...), custom_call_target="tpu_custom_call" | custom-call | flops 2000000000 | tf_op jit(solution)/shard_map/pallas_call | solution.py:94
  219.4 9.8 %collective-permute-done.15 = bf16[2,4,128,1024]{3,2,1,0:T(8,128)(2,1)} collective-permute-done((bf16[2,4,128,1024]{3,2,1,0:T(8,128)(2,1)}, bf16[2,4,128,1024]{3,2,1,0:T(8,128)(2,1)}, u32[]{:S(2)}, u32[]{:S(2)}) %collective-permute-start.15) | collective-permute-done | bytes 2097184 | tf_op jit(solution)/shard_map/ppermute | solution.py:523
  244.7 11.6 %collective-permute-done.17 = bf16[4,128,1024]{2,1,0:T(8,128)(2,1)S(1)} collective-permute-done((bf16[4,128,1024]{2,1,0:T(8,128)(2,1)S(1)}, bf16[4,128,1024]{2,1,0:T(8,128)(2,1)S(1)}, u32[]{:S(2)}, u32[]{:S(2)}) %collective-permute-start.17) | collective-permute-done | bytes 1048608 | tf_op jit(solution)/shard_map/ppermute | solution.py:523
  267.1 9.9 %shard_map.246 = (f32[512,2048]{1,0:T(8,128)}, bf16[512,2048]{1,0:T(8,128)(2,1)}) custom-call(bf16[1024,256]{1,0:T(8,128)(2,1)S(1)} %copy-done.29, bf16[256,2048]{1,0:T(8,128)(2,1)S(1)} %copy-done.7, bf16[1024,1024]{1,0:T(8,128)(2,1)S(1)} %copy-done.19, bf16[1024,2048]{1,0:T(8,128)(2,1)} %constant_dynamic-slice_fusion.6.fc2_ref), custom_call_target="tpu_custom_call" | custom-call | flops 1666666624 | tf_op jit(solution)/shard_map/pallas_call | solution.py:325
  277.0 13.3 %shard_map.247 = (f32[512,2048]{1,0:T(8,128)}, bf16[512,2048]{1,0:T(8,128)(2,1)}, f32[8,2048]{1,0:T(8,128)S(1)}) custom-call(bf16[1024,1024]{1,0:T(8,128)(2,1)} %copy-done.38, bf16[2048,1024]{1,0:T(8,128)(2,1)} %bitcast.196, bf16[1024,768]{1,0:T(8,128)(2,1)S(1)} %copy-done.5, bf16[2048,768]{1,0:T(8,128)(2,1)} %bitcast.165, ...), custom_call_target="tpu_custom_call" | custom-call | flops 2333333248 | tf_op jit(solution)/shard_map/pallas_call | solution.py:355
  304.4 5.2 %shard_map.248 = bf16[4,128,2048]{2,1,0:T(8,128)(2,1)} custom-call(s32[4]{0:T(128)S(1)} %and_select_fusion.2.order_ref, f32[512,2048]{1,0:T(8,128)} %get-tuple-element.233.mine_ref, bf16[512,2048]{1,0:T(8,128)(2,1)} %collective-permute-done.18.came_ref), custom_call_target="tpu_custom_call" | custom-call | tf_op jit(solution)/shard_map/pallas_call | solution.py:303
  309.6 5.2 %shard_map.249 = bf16[4,128,2048]{2,1,0:T(8,128)(2,1)} custom-call(s32[4]{0:T(128)S(1)} %and_select_fusion.2.order_ref, f32[512,2048]{1,0:T(8,128)} %get-tuple-element.237.mine_ref, bf16[512,2048]{1,0:T(8,128)(2,1)} %collective-permute-done.21.came_ref), custom_call_target="tpu_custom_call" | custom-call | tf_op jit(solution)/shard_map/pallas_call | solution.py:303
  317.4 22.6 %collective-permute-done.23 = bf16[128,4096]{1,0:T(8,128)(2,1)S(1)} collective-permute-done((bf16[128,4096]{1,0:T(8,128)(2,1)S(1)}, bf16[128,4096]{1,0:T(8,128)(2,1)S(1)}, u32[]{:S(2)}, u32[]{:S(2)}) %collective-permute-start.23) | collective-permute-done | bytes 1048608 | tf_op jit(solution)/shard_map/ppermute | solution.py:523
  349.4 11.9 %shard_map.251 = f32[2048,2048]{1,0:T(8,128)} custom-call(s32[8]{0:T(128)S(1)} %pad_add_fusion.4.spots_ref, bf16[2,256,2048]{2,1,0:T(8,128)(2,1)S(1)} %shard_map.245.refs_0_, bf16[2,256,2048]{2,1,0:T(8,128)(2,1)} %collective-permute-done.19.refs_1_, bf16[2,256,2048]{2,1,0:T(8,128)(2,1)} %collective-permute-done.24.refs_2_, ...), custom_call_target="tpu_custom_call" | custom-call | tf_op jit(solution)/shard_map/pallas_call | solution.py:490
  361.4 6.4 %collective-permute-done.26.m1_ref = bf16[2,128,4096]{2,1,0:T(8,128)(2,1)} collective-permute-done((bf16[2,128,4096]{2,1,0:T(8,128)(2,1)}, bf16[2,128,4096]{2,1,0:T(8,128)(2,1)}, u32[]{:S(2)}, u32[]{:S(2)}) %collective-permute-start.26) | collective-permute-done | bytes 2097184 | tf_op jit(solution)/shard_map/ppermute | solution.py:523
  367.8 9.2 %all-to-all-done.2 = bf16[4,144,768]{2,1,0:T(8,128)(2,1)} async-done(((bf16[4,144,768]{2,1,0:T(8,128)(2,1)}), bf16[4,144,768]{2,1,0:T(8,128)(2,1)}, u32[]{:S(2)}, u32[]{:S(2)}) %all-to-all-start.2) | async-done | bytes 884768 | tf_op jit(solution)/shard_map/all_to_all | solution.py:576
  385.1 14.3 %shard_map.252 = f32[512,8192]{1,0:T(8,128)} custom-call(s32[6]{0:T(128)S(1)} %concatenate.75.spots_ref, bf16[2,128,4096]{2,1,0:T(8,128)(2,1)} %shard_map.250.m0_ref, bf16[2,128,4096]{2,1,0:T(8,128)(2,1)} %collective-permute-done.26.m1_ref, bf16[2,128,4096]{2,1,0:T(8,128)(2,1)} %collective-permute-done.30.o0_ref, ...), custom_call_target="tpu_custom_call" | custom-call | tf_op jit(solution)/shard_map/pallas_call | solution.py:400
  412.6 4.9 %shard_map.254 = (f32[512,6144]{1,0:T(8,128)}, f32[512,2048]{1,0:T(8,128)}) custom-call(s32[3]{0:T(128)S(1)} %add_add_fusion.4.spots_ref, bf16[1,128,4096]{2,1,0:T(8,128)(2,1)} %bitcast.67.mine_ref, bf16[1,128,4096]{2,1,0:T(8,128)(2,1)S(1)} %bitcast.178, f32[512,6144]{1,0:T(8,128)} %get-tuple-element.260.refs_0_, ...), custom_call_target="tpu_custom_call", output_to_operand_aliasing={{0}: (3, {}), {1}: (4, {})} | custom-call | tf_op jit(solution)/shard_map/pallas_call | solution.py:452
  (320 shorter events, 174.1 us)
Async XLA Ops:
  13.2 30.9 %collective-permute-start.3 = (bf16[5760]{0:T(1024)(128)(2,1)S(1)}, bf16[5760]{0:T(1024)(128)(2,1)S(1)}, u32[]{:S(2)}, u32[]{:S(2)}) collective-permute-start(bf16[5760]{0:T(1024)(128)(2,1)S(1)} %dynamic-update-slice.6), channel_id=1, source_target_pairs={{0,3},{1,0},{2,1},{3,2},{4,7},{5,4},{6,5},{7,6},{8,11},{9,8},{10,9... | collective-permute-start | bytes 34568 | tf_op jit(solution)/shard_map/ppermute | solution.py:523
  18.2 25.9 %collective-permute-start.2 = (bf16[5760]{0:T(1024)(128)(2,1)S(1)}, bf16[5760]{0:T(1024)(128)(2,1)S(1)}, u32[]{:S(2)}, u32[]{:S(2)}) collective-permute-start(bf16[5760]{0:T(1024)(128)(2,1)S(1)} %dynamic-update-slice.6), channel_id=1, source_target_pairs={{0,2},{1,3},{2,0},{3,1},{4,6},{5,7},{6,4},{7,5},{8,10},{9,11},{10,... | collective-permute-start | bytes 34568 | tf_op jit(solution)/shard_map/ppermute | solution.py:523
  18.2 25.8 %collective-permute-start.1 = (bf16[5760]{0:T(1024)(128)(2,1)S(1)}, bf16[5760]{0:T(1024)(128)(2,1)S(1)}, u32[]{:S(2)}, u32[]{:S(2)}) collective-permute-start(bf16[5760]{0:T(1024)(128)(2,1)S(1)} %dynamic-update-slice.6), channel_id=1, source_target_pairs={{0,1},{1,2},{2,3},{3,0},{4,5},{5,6},{6,7},{7,4},{8,9},{9,10},{10,1... | collective-permute-start | bytes 34568 | tf_op jit(solution)/shard_map/ppermute | solution.py:523
  20.5 28.2 %collective-permute-start = (bf16[256,2048]{1,0:T(8,128)(2,1)S(1)}, bf16[256,2048]{1,0:T(8,128)(2,1)}, u32[]{:S(2)}, u32[]{:S(2)}) collective-permute-start(bf16[256,2048]{1,0:T(8,128)(2,1)S(1)} %pad_maximum_fusion.4.refs_0_), channel_id=1, source_target_pairs={{0,1},{1,2},{2,3},{3,0},{4,5},{5,6},{6,7},{7,4},{8,9},{9,10},{10,1... | collective-permute-start | bytes 3145736 | tf_op jit(solution)/shard_map/ppermute | solution.py:523
  27.2 58.6 %all-to-all-start = ((bf16[4,128,1792]{2,1,0:T(8,128)(2,1)}), bf16[4,128,1792]{2,1,0:T(8,128)(2,1)}, u32[]{:S(2)}, u32[]{:S(2)}) async-start(bf16[4,128,1792]{2,1,0:T(8,128)(2,1)} %copy-done.3), calls=%async_computation | async-start | bytes 3670016 | tf_op jit(solution)/shard_map/all_to_all | solution.py:576
  88.9 26.8 %collective-permute-start.7 = (bf16[256,2048]{1,0:T(8,128)(2,1)}, bf16[256,2048]{1,0:T(8,128)(2,1)S(1)}, u32[]{:S(2)}, u32[]{:S(2)}) collective-permute-start(bf16[256,2048]{1,0:T(8,128)(2,1)} %collective-permute-done.refs_2_), channel_id=1, source_target_pairs={{0,1},{1,2},{2,3},{3,0},{4,5},{5,6},{6,7},{7,4},{8,9},{9,10},{10,1... | collective-permute-start | bytes 3145736 | tf_op jit(solution)/shard_map/ppermute | solution.py:523
  107.4 36.1 %collective-permute-start.12 = (bf16[2,384,1792]{2,1,0:T(8,128)(2,1)}, bf16[2,384,1792]{2,1,0:T(8,128)(2,1)}, u32[]{:S(2)}, u32[]{:S(2)}) collective-permute-start(bf16[2,384,1792]{2,1,0:T(8,128)(2,1)} %shard_map.239), channel_id=1, source_target_pairs={{0,8},{1,9},{2,10},{3,11},{4,20},{5,21},{6,22},{7,23},{8,0},{9,1},... | collective-permute-start | bytes 8257544 | tf_op jit(solution)/shard_map/ppermute | solution.py:523
  115.7 27.7 %collective-permute-start.9 = (bf16[256,2048]{1,0:T(8,128)(2,1)S(1)}, bf16[256,2048]{1,0:T(8,128)(2,1)}, u32[]{:S(2)}, u32[]{:S(2)}) collective-permute-start(bf16[256,2048]{1,0:T(8,128)(2,1)S(1)} %collective-permute-done.7.refs_4_), channel_id=1, source_target_pairs={{0,1},{1,2},{2,3},{3,0},{4,5},{5,6},{6,7},{7,4},{8,9},{9,10},{10,1... | collective-permute-start | bytes 3145736 | tf_op jit(solution)/shard_map/ppermute | solution.py:523
  169.1 26.4 %collective-permute-start.13 = (bf16[2,1,256,2048]{3,2,1,0:T(8,128)(2,1)}, bf16[2,1,256,2048]{3,2,1,0:T(8,128)(2,1)}, u32[]{:S(2)}, u32[]{:S(2)}) collective-permute-start(bf16[2,1,256,2048]{3,2,1,0:T(8,128)(2,1)} %pad_maximum_fusion.1), channel_id=1, source_target_pairs={{0,16},{1,17},{2,18},{3,19},{4,12},{5,13},{6,14},{7,15},{8,24},{9,... | collective-permute-start | bytes 6291464 | tf_op jit(solution)/shard_map/ppermute | solution.py:523
  185.7 43.5 %collective-permute-start.15 = (bf16[2,4,128,1024]{3,2,1,0:T(8,128)(2,1)}, bf16[2,4,128,1024]{3,2,1,0:T(8,128)(2,1)}, u32[]{:S(2)}, u32[]{:S(2)}) collective-permute-start(bf16[2,4,128,1024]{3,2,1,0:T(8,128)(2,1)} %pad_maximum_fusion.2), channel_id=1, source_target_pairs={{0,16},{1,17},{2,18},{3,19},{4,12},{5,13},{6,14},{7,15},{8,24},{9,... | collective-permute-start | bytes 6291464 | tf_op jit(solution)/shard_map/ppermute | solution.py:523
  199.8 32.7 %collective-permute-start.14 = (bf16[1,256,2048]{2,1,0:T(8,128)(2,1)}, bf16[1,256,2048]{2,1,0:T(8,128)(2,1)}, u32[]{:S(2)}, u32[]{:S(2)}) collective-permute-start(bf16[1,256,2048]{2,1,0:T(8,128)(2,1)} %get-tuple-element.191), channel_id=1, source_target_pairs={{0,8},{1,9},{2,10},{3,11},{4,20},{5,21},{6,22},{7,23},{8,0},{9,1},... | collective-permute-start | bytes 3145736 | tf_op jit(solution)/shard_map/ppermute | solution.py:523
  234.1 27.8 %collective-permute-start.16 = (bf16[256,2048]{1,0:T(8,128)(2,1)S(1)}, bf16[256,2048]{1,0:T(8,128)(2,1)S(1)}, u32[]{:S(2)}, u32[]{:S(2)}) collective-permute-start(bf16[256,2048]{1,0:T(8,128)(2,1)S(1)} %bitcast.170), channel_id=1, source_target_pairs={{0,16},{1,17},{2,18},{3,19},{4,12},{5,13},{6,14},{7,15},{8,24},{9,... | collective-permute-start | bytes 3145736 | tf_op jit(solution)/shard_map/ppermute | solution.py:523
  244.2 53.4 %collective-permute-start.20 = (bf16[2,4,128,1024]{3,2,1,0:T(8,128)(2,1)}, bf16[2,4,128,1024]{3,2,1,0:T(8,128)(2,1)}, u32[]{:S(2)}, u32[]{:S(2)}) collective-permute-start(bf16[2,4,128,1024]{3,2,1,0:T(8,128)(2,1)} %pad_maximum_fusion.3), channel_id=1, source_target_pairs={{0,16},{1,17},{2,18},{3,19},{4,12},{5,13},{6,14},{7,15},{8,24},{9,... | collective-permute-start | bytes 6291464 | tf_op jit(solution)/shard_map/ppermute | solution.py:523
  257.7 43.8 %all-to-all-start.1 = ((bf16[4,128,1024]{2,1,0:T(8,128)(2,1)}), bf16[4,128,1024]{2,1,0:T(8,128)(2,1)}, u32[]{:S(2)}, u32[]{:S(2)}) async-start(bf16[4,128,1024]{2,1,0:T(8,128)(2,1)} %add_convert_fusion.1), calls=%async_computation.1 | async-start | bytes 2097152 | tf_op jit(solution)/shard_map/all_to_all | solution.py:576
  261.9 149.1 %reduce-scatter.5.cloned.1.call-start = ((), (), s32[]{:S(2)}) async-start(), calls=%async_computation.6 | async-start | bytes 2621440 | tf_op jit(solution)/shard_map/reduce_scatter | solution.py:788
  265.8 37.3 %collective-permute-start.19 = (bf16[2,256,2048]{2,1,0:T(8,128)(2,1)S(1)}, bf16[2,256,2048]{2,1,0:T(8,128)(2,1)}, u32[]{:S(2)}, u32[]{:S(2)}) collective-permute-start(bf16[2,256,2048]{2,1,0:T(8,128)(2,1)S(1)} %shard_map.245.refs_0_), channel_id=1, source_target_pairs={{0,8},{1,9},{2,10},{3,11},{4,20},{5,21},{6,22},{7,23},{8,0},{9,1},... | collective-permute-start | bytes 6291464 | tf_op jit(solution)/shard_map/ppermute | solution.py:523
  276.9 27.4 %collective-permute-start.18 = (bf16[512,2048]{1,0:T(8,128)(2,1)}, bf16[512,2048]{1,0:T(8,128)(2,1)}, u32[]{:S(2)}, u32[]{:S(2)}) collective-permute-start(bf16[512,2048]{1,0:T(8,128)(2,1)} %get-tuple-element.213), channel_id=1, source_target_pairs={{0,4},{1,5},{2,6},{3,7},{4,0},{5,1},{6,2},{7,3},{8,12},{9,13},{10,... | collective-permute-start | bytes 6291464 | tf_op jit(solution)/shard_map/ppermute | solution.py:523
  314.8 25.3 %collective-permute-start.23 = (bf16[128,4096]{1,0:T(8,128)(2,1)S(1)}, bf16[128,4096]{1,0:T(8,128)(2,1)S(1)}, u32[]{:S(2)}, u32[]{:S(2)}) collective-permute-start(bf16[128,4096]{1,0:T(8,128)(2,1)S(1)} %bitcast.171), channel_id=1, source_target_pairs={{0,16},{1,17},{2,18},{3,19},{4,12},{5,13},{6,14},{7,15},{8,24},{9,... | collective-permute-start | bytes 3145736 | tf_op jit(solution)/shard_map/ppermute | solution.py:523
  316.4 26.3 %collective-permute-start.22 = (bf16[4,128,1024]{2,1,0:T(8,128)(2,1)}, bf16[4,128,1024]{2,1,0:T(8,128)(2,1)S(1)}, u32[]{:S(2)}, u32[]{:S(2)}) collective-permute-start(bf16[4,128,1024]{2,1,0:T(8,128)(2,1)} %get-tuple-element.231), channel_id=1, source_target_pairs={{0,8},{1,9},{2,10},{3,11},{4,20},{5,21},{6,22},{7,23},{8,0},{9,1},... | collective-permute-start | bytes 3145736 | tf_op jit(solution)/shard_map/ppermute | solution.py:523
  316.9 32.5 %collective-permute-start.24 = (bf16[2,256,2048]{2,1,0:T(8,128)(2,1)S(1)}, bf16[2,256,2048]{2,1,0:T(8,128)(2,1)}, u32[]{:S(2)}, u32[]{:S(2)}) collective-permute-start(bf16[2,256,2048]{2,1,0:T(8,128)(2,1)S(1)} %shard_map.245.refs_0_), channel_id=1, source_target_pairs={{0,4},{1,5},{2,6},{3,7},{4,0},{5,1},{6,2},{7,3},{8,12},{9,13},{10,... | collective-permute-start | bytes 6291464 | tf_op jit(solution)/shard_map/ppermute | solution.py:523
  316.9 32.5 %collective-permute-start.25 = (bf16[2,256,2048]{2,1,0:T(8,128)(2,1)}, bf16[2,256,2048]{2,1,0:T(8,128)(2,1)}, u32[]{:S(2)}, u32[]{:S(2)}) collective-permute-start(bf16[2,256,2048]{2,1,0:T(8,128)(2,1)} %collective-permute-done.19.refs_1_), channel_id=1, source_target_pairs={{0,4},{1,5},{2,6},{3,7},{4,0},{5,1},{6,2},{7,3},{8,12},{9,13},{10,... | collective-permute-start | bytes 6291464 | tf_op jit(solution)/shard_map/ppermute | solution.py:523
  341.5 26.4 %collective-permute-start.26 = (bf16[2,128,4096]{2,1,0:T(8,128)(2,1)}, bf16[2,128,4096]{2,1,0:T(8,128)(2,1)}, u32[]{:S(2)}, u32[]{:S(2)}) collective-permute-start(bf16[2,128,4096]{2,1,0:T(8,128)(2,1)} %shard_map.250.m0_ref), channel_id=1, source_target_pairs={{0,8},{1,9},{2,10},{3,11},{4,20},{5,21},{6,22},{7,23},{8,0},{9,1},... | collective-permute-start | bytes 6291464 | tf_op jit(solution)/shard_map/ppermute | solution.py:523
  344.2 32.7 %all-to-all-start.2 = ((bf16[4,144,768]{2,1,0:T(8,128)(2,1)}), bf16[4,144,768]{2,1,0:T(8,128)(2,1)}, u32[]{:S(2)}, u32[]{:S(2)}) async-start(bf16[4,144,768]{2,1,0:T(8,128)(2,1)} %pad_maximum_fusion.5), calls=%async_computation.4 | async-start | bytes 1769472 | tf_op jit(solution)/shard_map/all_to_all | solution.py:576
  348.5 77.8 %reduce-scatter.3.cloned.1.call-start = ((), (), s32[]{:S(2)}) async-start(), calls=%async_computation.5 | async-start | bytes 2621440 | tf_op jit(solution)/shard_map/reduce_scatter | solution.py:788
  (74 other events, 695.4 us)
Sparse Core Ops, SparseCore 0:
  314.9 50.1 reduce-scatter.4
  367.5 44.3 reduce-scatter.2

commit v3 on v2

--- a/solution.py
+++ b/solution.py
@@ -841,23 +841,23 @@
         fc1_mine, fc1_other = (fc1_part, fc1_came), (fc1_other, fc1_last)
     else:
         fc1_mine, fc1_other = (fc1_part, fc1_part), (fc1_other, fc1_other)
-    count = riders.shape[1] // 2
-    riders = step(riders)
-    riders = (riders[:, :count] + riders[:, count:]).reshape(S, -1)[:, :riding]
-    sums = jnp.concatenate(
-        [
-            jnp.sum(riders[:, : 2 * height], axis=0),
-            column_sums[:ff_own],
-            riders[:, 2 * height :].reshape(-1),
-            column_sums[ff_own:],
-        ]
-    )
-    sums = tie(sums)
-    step(None, sums)
-    sums = net.plane_sum(sums, 0)
     if net.square:
         fc1_own = place_columns(net, *step((fc1_mine, fc1_other)), factor)
         step(None, fc1_own)
+        count = riders.shape[1] // 2
+        riders = step(riders)
+        riders = (riders[:, :count] + riders[:, count:]).reshape(S, -1)[:, :riding]
+        sums = jnp.concatenate(
+            [
+                jnp.sum(riders[:, : 2 * height], axis=0),
+                column_sums[:ff_own],
+                riders[:, 2 * height :].reshape(-1),
+                column_sums[ff_own:],
+            ]
+        )
+        sums = tie(sums)
+        step(None, sums)
+        sums = net.plane_sum(sums, 0)
         own, other = step((mixed_part[None], mixed_other[None]))
         placed = tie(place_mixed(net, own, other, 0, factor))
         step(None, placed)
@@ -880,6 +880,20 @@
         placed = place_mixed(net, mixed_last[None], last_other[None], 3, factor, placed)
     else:
         mixed_near = lax.all_gather(mixed_part, "dp", axis_index_groups=net.groups())
+        count = riders.shape[1] // 2
+        riders = step(riders)
+        riders = (riders[:, :count] + riders[:, count:]).reshape(S, -1)[:, :riding]
+        sums = jnp.concatenate(
+            [
+                jnp.sum(riders[:, : 2 * height], axis=0),
+                column_sums[:ff_own],
+                riders[:, 2 * height :].reshape(-1),
+                column_sums[ff_own:],
+            ]
+        )
+        sums = tie(sums)
+        step(None, sums)
+        sums = net.plane_sum(sums, 0)
         fc1_own = place_columns(net, *step((fc1_mine, fc1_other)), factor)
         sums = net.plane_sum(sums, 1)
         sums_came = net.move(sums, dc=1)

time: 452 us -> 449 us (level)
    unnamed x119 -> x117, local copies, waits for them, and re-layouts: 18.7 us -> 17.7 us
  transfers between devices with their start and end apart: 44 -> 44, of which waited for: 19 -> 18; matrix products, arithmetic and copies ran while one was open for 17% -> 17% of each run, Pallas kernels for 23% -> 23%
where the time goes in v3:
time: 449 us; the launch traced here: 443 us
  waiting for transfers between devices  149 us (33%)
  Pallas kernels  117 us (26%)
  starting transfers between devices  44.4 us (10%)
  other arithmetic  41.9 us (9%)
  matrix products  36.3 us (8%)
  local copies, waits for them, and re-layouts  32.6 us (7%)
  between operations  21.2 us (5%)
    ppermute x39, waiting for transfers between devices, move(): return lax.ppermute(x, AXES, pairs)  108 us
    all_to_all x3, waiting for transfers between devices, swap(): return lax.all_to_all(tie(x, *after), 'shard', 0, 0, tiled=True)  40.4 us
    ppermute x39, starting transfers between devices, move(): return lax.ppermute(x, AXES, pairs)  31.5 us
    unnamed x117, local copies, waits for them, and re-layouts  17.7 us
    pallas_call x4, Pallas kernels, place_mixed(): call(kernel, (count, planes), [pl.BlockSpec((None, part, columns), lambda...  17.2 us
    dot_general x4, matrix products, local(): jnp.einsum('td,te->de', x, y, preferred_element_type=f32).astype(bf16)  14.8 us
    pallas_call x1, Pallas kernels, place_columns(): call(kernel, (J, 2), [pl.BlockSpec((None, high, columns), lambda i, h, sp...  14.2 us
    pallas_call x2, Pallas kernels, norm(): call(kernel, (len(arrays),), [line, line] + [pl.BlockSpec(x.shape, lambda...  13.4 us
  transfers between devices with their start and end apart: 44, of which 18 were waited for; matrix products, arithmetic and copies ran while one was open for 17% of the time, Pallas kernels for 23%

profile of v3, /device:TPU:0, one launch (start us, length us, event | category | flops | bytes accessed | tf_op | source)
XLA Modules:
  0.0 442.8 jit_solution(11379965683085793866)
XLA Ops:
  13.2 5.1 %collective-permute-start.3 = (bf16[5760]{0:T(1024)(128)(2,1)S(1)}, bf16[5760]{0:T(1024)(128)(2,1)S(1)}, u32[]{:S(2)}, u32[]{:S(2)}) collective-permute-start(bf16[5760]{0:T(1024)(128)(2,1)S(1)} %dynamic-update-slice.6), channel_id=1, source_target_pairs={{0,3},{1,0},{2,1},{3,2},{4,7},{5,4},{6,5},{7,6},{8,11},{9,8},{10,9... | collective-permute-start | bytes 34568 | tf_op jit(solution)/shard_map/ppermute | solution.py:523
  54.6 31.3 %all-to-all-done = bf16[4,128,1792]{2,1,0:T(8,128)(2,1)} async-done(((bf16[4,128,1792]{2,1,0:T(8,128)(2,1)}), bf16[4,128,1792]{2,1,0:T(8,128)(2,1)}, u32[]{:S(2)}, u32[]{:S(2)}) %all-to-all-start) | async-done | bytes 1835040 | tf_op jit(solution)/shard_map/all_to_all | solution.py:576
  88.9 16.8 %collective-permute-done.8.refs_1_ = bf16[1,384,1792]{2,1,0:T(8,128)(2,1)S(1)} collective-permute-done((bf16[1,384,1792]{2,1,0:T(8,128)(2,1)S(1)}, bf16[1,384,1792]{2,1,0:T(8,128)(2,1)S(1)}, u32[]{:S(2)}, u32[]{:S(2)}) %collective-permute-start.8) | collective-permute-done | bytes 1376288 | tf_op jit(solution)/shard_map/ppermute | solution.py:523
  108.9 6.9 %collective-permute-done.7.refs_4_ = bf16[256,2048]{1,0:T(8,128)(2,1)S(1)} collective-permute-done((bf16[256,2048]{1,0:T(8,128)(2,1)}, bf16[256,2048]{1,0:T(8,128)(2,1)S(1)}, u32[]{:S(2)}, u32[]{:S(2)}) %collective-permute-start.7) | collective-permute-done | bytes 1048608 | tf_op jit(solution)/shard_map/ppermute | solution.py:523
  119.4 7.8 %shard_map.240 = (bf16[1024,2048]{1,0:T(8,128)(2,1)}, bf16[1024,2048]{1,0:T(8,128)(2,1)}, bf16[1024,2048]{1,0:T(8,128)(2,1)}, f32[1024,128]{1,0:T(8,128)S(1)}, f32[1024,128]{1,0:T(8,128)S(1)}) custom-call(s32[6]{0:T(128)S(1)} %copy-done.31, f32[1,2048]{1,0:T(1,128)S(1)} %bitcast.180, f32[1,2048]{1,0:T(1,128)S(1)} %bitcast.184, ...), custom_call_target="tpu_custom_call" | custom-call | tf_op jit(solution)/shard_map/pallas_call | solution.py:238
  132.0 11.4 %collective-permute-done.9.refs_0_ = bf16[256,2048]{1,0:T(8,128)(2,1)} collective-permute-done((bf16[256,2048]{1,0:T(8,128)(2,1)S(1)}, bf16[256,2048]{1,0:T(8,128)(2,1)}, u32[]{:S(2)}, u32[]{:S(2)}) %collective-permute-start.9) | collective-permute-done | bytes 1048608 | tf_op jit(solution)/shard_map/ppermute | solution.py:523
  147.6 5.7 %shard_map.243 = (bf16[1024,2048]{1,0:T(8,128)(2,1)}, bf16[1024,2048]{1,0:T(8,128)(2,1)}, bf16[1024,2048]{1,0:T(8,128)(2,1)}, f32[1024,128]{1,0:T(8,128)S(1)}, f32[1024,128]{1,0:T(8,128)S(1)}) custom-call(s32[2]{0:T(128)S(1)} %copy-done.30, f32[1,2048]{1,0:T(1,128)S(1)} %bitcast.181, ...), custom_call_target="tpu_custom_call", output_to_operand_aliasing={{0}: (5, {}), {1}: (6, {}), {2}: (7, {}), {3}: (8, {}), {4}... | custom-call | tf_op jit(solution)/shard_map/pallas_call | solution.py:238
  153.3 7.7 %multiply_convert_fusion = (bf16[1024,1024]{1,0:T(8,128)(2,1)S(1)}, f32[1024,1024]{1,0:T(8,128)S(1)}) fusion(f32[1024]{0:T(1024)S(1)} %dynamic_slice.74, bf16[1024,2048]{1,0:T(8,128)(2,1)} %get-tuple-element.202, bf16[2048,1024]{1,0:T(8,128)(2,1)S(1)} %bitcast.197), kind=kOutput, calls=%fused_computation.12 | convolution fusion | flops 4305453056 | bytes 14684160 | tf_op jit(solution)/shard_map/dot_general | solution.py:705
  170.6 7.3 %fusion.6.hidden_ref = bf16[1024,1024]{1,0:T(8,128)(2,1)S(1)} fusion(f32[1024,1024]{1,0:T(8,128)S(1)} %get-tuple-element.315, f32[1024]{0:T(1024)S(1)} %dynamic_slice.74, bf16[1024,2048]{1,0:T(8,128)(2,1)S(1)} %copy-done.35, bf16[1024,2048]{1,0:T(8,128)(2,1)S(1)} %copy-done.34), kind=kOutput, calls=%fused_computation.9 | convolution fusion | flops 4316987392 | bytes 14684160 | tf_op jit(solution)/shard_map/td,fd->tf/dot_general | solution.py:751
  187.0 8.5 %collective-permute-done.13 = bf16[2,1,256,2048]{3,2,1,0:T(8,128)(2,1)} collective-permute-done((bf16[2,1,256,2048]{3,2,1,0:T(8,128)(2,1)}, bf16[2,1,256,2048]{3,2,1,0:T(8,128)(2,1)}, u32[]{:S(2)}, u32[]{:S(2)}) %collective-permute-start.13) | collective-permute-done | bytes 2097184 | tf_op jit(solution)/shard_map/ppermute | solution.py:523
  200.4 5.1 %broadcast_add_fusion.mixed_ref = f32[1024,768]{1,0:T(8,128)} fusion(f32[768]{0:T(1024)S(1)} %reshape.342, bf16[1024,2048]{1,0:T(8,128)(2,1)S(1)} %copy-done.46, bf16[2048,768]{1,0:T(8,128)(2,1)S(1)} %bitcast.164), kind=kOutput, calls=%fused_computation.34 | convolution fusion | flops 3222011904 | bytes 10488832 | tf_op jit(solution)/shard_map/dot_general | solution.py:757
  207.0 12.4 %shard_map.244 = (bf16[1024,256]{1,0:T(8,128)(2,1)S(1)}, bf16[1024,768]{1,0:T(8,128)(2,1)S(1)}) custom-call(s32[1024,128]{1,0:T(8,128)S(1)} %copy-done.27, f32[1024,128]{1,0:T(8,128)S(1)} %copy-done.26, f32[1024,128]{1,0:T(8,128)S(1)} %copy-done.25, f32[1024,128]{1,0:T(8,128)S(1)} %copy-done.24, f32[1024,768]{1,0:T(8,128)} %broadcast_add_fusion.mixed_ref, ...), custom_call_target="tpu_custom_call" | custom-call | flops 2000000000 | tf_op jit(solution)/shard_map/pallas_call | solution.py:94
  219.4 9.7 %collective-permute-done.15 = bf16[2,4,128,1024]{3,2,1,0:T(8,128)(2,1)} collective-permute-done((bf16[2,4,128,1024]{3,2,1,0:T(8,128)(2,1)}, bf16[2,4,128,1024]{3,2,1,0:T(8,128)(2,1)}, u32[]{:S(2)}, u32[]{:S(2)}) %collective-permute-start.15) | collective-permute-done | bytes 2097184 | tf_op jit(solution)/shard_map/ppermute | solution.py:523
  244.7 11.6 %collective-permute-done.17 = bf16[4,128,1024]{2,1,0:T(8,128)(2,1)S(1)} collective-permute-done((bf16[4,128,1024]{2,1,0:T(8,128)(2,1)S(1)}, bf16[4,128,1024]{2,1,0:T(8,128)(2,1)S(1)}, u32[]{:S(2)}, u32[]{:S(2)}) %collective-permute-start.17) | collective-permute-done | bytes 1048608 | tf_op jit(solution)/shard_map/ppermute | solution.py:523
  267.1 9.9 %shard_map.246 = (f32[512,2048]{1,0:T(8,128)}, bf16[512,2048]{1,0:T(8,128)(2,1)}) custom-call(bf16[1024,256]{1,0:T(8,128)(2,1)S(1)} %copy-done.29, bf16[256,2048]{1,0:T(8,128)(2,1)S(1)} %copy-done.7, bf16[1024,1024]{1,0:T(8,128)(2,1)S(1)} %copy-done.19, bf16[1024,2048]{1,0:T(8,128)(2,1)} %constant_dynamic-slice_fusion.6.fc2_ref), custom_call_target="tpu_custom_call" | custom-call | flops 1666666624 | tf_op jit(solution)/shard_map/pallas_call | solution.py:325
  277.0 13.3 %shard_map.247 = (f32[512,2048]{1,0:T(8,128)}, bf16[512,2048]{1,0:T(8,128)(2,1)}, f32[8,2048]{1,0:T(8,128)S(1)}) custom-call(bf16[1024,1024]{1,0:T(8,128)(2,1)} %copy-done.38, bf16[2048,1024]{1,0:T(8,128)(2,1)} %bitcast.196, bf16[1024,768]{1,0:T(8,128)(2,1)S(1)} %copy-done.5, bf16[2048,768]{1,0:T(8,128)(2,1)} %bitcast.165, ...), custom_call_target="tpu_custom_call" | custom-call | flops 2333333248 | tf_op jit(solution)/shard_map/pallas_call | solution.py:355
  304.4 5.2 %shard_map.248 = bf16[4,128,2048]{2,1,0:T(8,128)(2,1)} custom-call(s32[4]{0:T(128)S(1)} %and_select_fusion.2.order_ref, f32[512,2048]{1,0:T(8,128)} %get-tuple-element.233.mine_ref, bf16[512,2048]{1,0:T(8,128)(2,1)} %collective-permute-done.18.came_ref), custom_call_target="tpu_custom_call" | custom-call | tf_op jit(solution)/shard_map/pallas_call | solution.py:303
  309.6 5.2 %shard_map.249 = bf16[4,128,2048]{2,1,0:T(8,128)(2,1)} custom-call(s32[4]{0:T(128)S(1)} %and_select_fusion.2.order_ref, f32[512,2048]{1,0:T(8,128)} %get-tuple-element.237.mine_ref, bf16[512,2048]{1,0:T(8,128)(2,1)} %collective-permute-done.21.came_ref), custom_call_target="tpu_custom_call" | custom-call | tf_op jit(solution)/shard_map/pallas_call | solution.py:303
  317.4 22.7 %collective-permute-done.23 = bf16[128,4096]{1,0:T(8,128)(2,1)S(1)} collective-permute-done((bf16[128,4096]{1,0:T(8,128)(2,1)S(1)}, bf16[128,4096]{1,0:T(8,128)(2,1)S(1)}, u32[]{:S(2)}, u32[]{:S(2)}) %collective-permute-start.23) | collective-permute-done | bytes 1048608 | tf_op jit(solution)/shard_map/ppermute | solution.py:523
  349.4 11.9 %shard_map.251 = f32[2048,2048]{1,0:T(8,128)} custom-call(s32[8]{0:T(128)S(1)} %pad_add_fusion.4.spots_ref, bf16[2,256,2048]{2,1,0:T(8,128)(2,1)S(1)} %shard_map.245.refs_0_, bf16[2,256,2048]{2,1,0:T(8,128)(2,1)} %collective-permute-done.19.refs_1_, bf16[2,256,2048]{2,1,0:T(8,128)(2,1)} %collective-permute-done.24.refs_2_, ...), custom_call_target="tpu_custom_call" | custom-call | tf_op jit(solution)/shard_map/pallas_call | solution.py:490
  361.4 6.5 %collective-permute-done.26.m1_ref = bf16[2,128,4096]{2,1,0:T(8,128)(2,1)} collective-permute-done((bf16[2,128,4096]{2,1,0:T(8,128)(2,1)}, bf16[2,128,4096]{2,1,0:T(8,128)(2,1)}, u32[]{:S(2)}, u32[]{:S(2)}) %collective-permute-start.26) | collective-permute-done | bytes 2097184 | tf_op jit(solution)/shard_map/ppermute | solution.py:523
  367.9 9.1 %all-to-all-done.2 = bf16[4,144,768]{2,1,0:T(8,128)(2,1)} async-done(((bf16[4,144,768]{2,1,0:T(8,128)(2,1)}), bf16[4,144,768]{2,1,0:T(8,128)(2,1)}, u32[]{:S(2)}, u32[]{:S(2)}) %all-to-all-start.2) | async-done | bytes 884768 | tf_op jit(solution)/shard_map/all_to_all | solution.py:576
  384.5 14.2 %shard_map.252 = f32[512,8192]{1,0:T(8,128)} custom-call(s32[6]{0:T(128)S(1)} %concatenate.73.spots_ref, bf16[2,128,4096]{2,1,0:T(8,128)(2,1)} %shard_map.250.m0_ref, bf16[2,128,4096]{2,1,0:T(8,128)(2,1)} %collective-permute-done.26.m1_ref, bf16[2,128,4096]{2,1,0:T(8,128)(2,1)} %collective-permute-done.28.o0_ref, ...), custom_call_target="tpu_custom_call" | custom-call | tf_op jit(solution)/shard_map/pallas_call | solution.py:400
  410.5 4.9 %shard_map.254 = (f32[512,6144]{1,0:T(8,128)}, f32[512,2048]{1,0:T(8,128)}) custom-call(s32[3]{0:T(128)S(1)} %add_add_fusion.4.spots_ref, bf16[1,128,4096]{2,1,0:T(8,128)(2,1)S(1)} %bitcast.176, bf16[1,128,4096]{2,1,0:T(8,128)(2,1)} %bitcast.68.other_ref, f32[512,6144]{1,0:T(8,128)} %get-tuple-element.260.refs_0_, ...), custom_call_target="tpu_custom_call", output_to_operand_aliasing={{0}: (3, {}), {1}: (4, {})} | custom-call | tf_op jit(solution)/shard_map/pallas_call | solution.py:452
  (320 shorter events, 171.4 us)
Async XLA Ops:
  13.2 30.9 %collective-permute-start.3 = (bf16[5760]{0:T(1024)(128)(2,1)S(1)}, bf16[5760]{0:T(1024)(128)(2,1)S(1)}, u32[]{:S(2)}, u32[]{:S(2)}) collective-permute-start(bf16[5760]{0:T(1024)(128)(2,1)S(1)} %dynamic-update-slice.6), channel_id=1, source_target_pairs={{0,3},{1,0},{2,1},{3,2},{4,7},{5,4},{6,5},{7,6},{8,11},{9,8},{10,9... | collective-permute-start | bytes 34568 | tf_op jit(solution)/shard_map/ppermute | solution.py:523
  18.2 25.8 %collective-permute-start.2 = (bf16[5760]{0:T(1024)(128)(2,1)S(1)}, bf16[5760]{0:T(1024)(128)(2,1)S(1)}, u32[]{:S(2)}, u32[]{:S(2)}) collective-permute-start(bf16[5760]{0:T(1024)(128)(2,1)S(1)} %dynamic-update-slice.6), channel_id=1, source_target_pairs={{0,2},{1,3},{2,0},{3,1},{4,6},{5,7},{6,4},{7,5},{8,10},{9,11},{10,... | collective-permute-start | bytes 34568 | tf_op jit(solution)/shard_map/ppermute | solution.py:523
  18.2 25.8 %collective-permute-start.1 = (bf16[5760]{0:T(1024)(128)(2,1)S(1)}, bf16[5760]{0:T(1024)(128)(2,1)S(1)}, u32[]{:S(2)}, u32[]{:S(2)}) collective-permute-start(bf16[5760]{0:T(1024)(128)(2,1)S(1)} %dynamic-update-slice.6), channel_id=1, source_target_pairs={{0,1},{1,2},{2,3},{3,0},{4,5},{5,6},{6,7},{7,4},{8,9},{9,10},{10,1... | collective-permute-start | bytes 34568 | tf_op jit(solution)/shard_map/ppermute | solution.py:523
  20.5 28.2 %collective-permute-start = (bf16[256,2048]{1,0:T(8,128)(2,1)S(1)}, bf16[256,2048]{1,0:T(8,128)(2,1)}, u32[]{:S(2)}, u32[]{:S(2)}) collective-permute-start(bf16[256,2048]{1,0:T(8,128)(2,1)S(1)} %pad_maximum_fusion.4.refs_0_), channel_id=1, source_target_pairs={{0,1},{1,2},{2,3},{3,0},{4,5},{5,6},{6,7},{7,4},{8,9},{9,10},{10,1... | collective-permute-start | bytes 3145736 | tf_op jit(solution)/shard_map/ppermute | solution.py:523
  27.2 58.6 %all-to-all-start = ((bf16[4,128,1792]{2,1,0:T(8,128)(2,1)}), bf16[4,128,1792]{2,1,0:T(8,128)(2,1)}, u32[]{:S(2)}, u32[]{:S(2)}) async-start(bf16[4,128,1792]{2,1,0:T(8,128)(2,1)} %copy-done.3), calls=%async_computation | async-start | bytes 3670016 | tf_op jit(solution)/shard_map/all_to_all | solution.py:576
  88.9 26.8 %collective-permute-start.7 = (bf16[256,2048]{1,0:T(8,128)(2,1)}, bf16[256,2048]{1,0:T(8,128)(2,1)S(1)}, u32[]{:S(2)}, u32[]{:S(2)}) collective-permute-start(bf16[256,2048]{1,0:T(8,128)(2,1)} %collective-permute-done.refs_2_), channel_id=1, source_target_pairs={{0,1},{1,2},{2,3},{3,0},{4,5},{5,6},{6,7},{7,4},{8,9},{9,10},{10,1... | collective-permute-start | bytes 3145736 | tf_op jit(solution)/shard_map/ppermute | solution.py:523
  107.4 36.1 %collective-permute-start.12 = (bf16[2,384,1792]{2,1,0:T(8,128)(2,1)}, bf16[2,384,1792]{2,1,0:T(8,128)(2,1)}, u32[]{:S(2)}, u32[]{:S(2)}) collective-permute-start(bf16[2,384,1792]{2,1,0:T(8,128)(2,1)} %shard_map.239), channel_id=1, source_target_pairs={{0,8},{1,9},{2,10},{3,11},{4,20},{5,21},{6,22},{7,23},{8,0},{9,1},... | collective-permute-start | bytes 8257544 | tf_op jit(solution)/shard_map/ppermute | solution.py:523
  115.7 27.7 %collective-permute-start.9 = (bf16[256,2048]{1,0:T(8,128)(2,1)S(1)}, bf16[256,2048]{1,0:T(8,128)(2,1)}, u32[]{:S(2)}, u32[]{:S(2)}) collective-permute-start(bf16[256,2048]{1,0:T(8,128)(2,1)S(1)} %collective-permute-done.7.refs_4_), channel_id=1, source_target_pairs={{0,1},{1,2},{2,3},{3,0},{4,5},{5,6},{6,7},{7,4},{8,9},{9,10},{10,1... | collective-permute-start | bytes 3145736 | tf_op jit(solution)/shard_map/ppermute | solution.py:523
  169.1 26.4 %collective-permute-start.13 = (bf16[2,1,256,2048]{3,2,1,0:T(8,128)(2,1)}, bf16[2,1,256,2048]{3,2,1,0:T(8,128)(2,1)}, u32[]{:S(2)}, u32[]{:S(2)}) collective-permute-start(bf16[2,1,256,2048]{3,2,1,0:T(8,128)(2,1)} %pad_maximum_fusion.1), channel_id=1, source_target_pairs={{0,16},{1,17},{2,18},{3,19},{4,12},{5,13},{6,14},{7,15},{8,24},{9,... | collective-permute-start | bytes 6291464 | tf_op jit(solution)/shard_map/ppermute | solution.py:523
  185.7 43.5 %collective-permute-start.15 = (bf16[2,4,128,1024]{3,2,1,0:T(8,128)(2,1)}, bf16[2,4,128,1024]{3,2,1,0:T(8,128)(2,1)}, u32[]{:S(2)}, u32[]{:S(2)}) collective-permute-start(bf16[2,4,128,1024]{3,2,1,0:T(8,128)(2,1)} %pad_maximum_fusion.2), channel_id=1, source_target_pairs={{0,16},{1,17},{2,18},{3,19},{4,12},{5,13},{6,14},{7,15},{8,24},{9,... | collective-permute-start | bytes 6291464 | tf_op jit(solution)/shard_map/ppermute | solution.py:523
  199.8 32.6 %collective-permute-start.14 = (bf16[1,256,2048]{2,1,0:T(8,128)(2,1)}, bf16[1,256,2048]{2,1,0:T(8,128)(2,1)}, u32[]{:S(2)}, u32[]{:S(2)}) collective-permute-start(bf16[1,256,2048]{2,1,0:T(8,128)(2,1)} %get-tuple-element.191), channel_id=1, source_target_pairs={{0,8},{1,9},{2,10},{3,11},{4,20},{5,21},{6,22},{7,23},{8,0},{9,1},... | collective-permute-start | bytes 3145736 | tf_op jit(solution)/shard_map/ppermute | solution.py:523
  234.1 27.9 %collective-permute-start.16 = (bf16[256,2048]{1,0:T(8,128)(2,1)S(1)}, bf16[256,2048]{1,0:T(8,128)(2,1)S(1)}, u32[]{:S(2)}, u32[]{:S(2)}) collective-permute-start(bf16[256,2048]{1,0:T(8,128)(2,1)S(1)} %bitcast.170), channel_id=1, source_target_pairs={{0,16},{1,17},{2,18},{3,19},{4,12},{5,13},{6,14},{7,15},{8,24},{9,... | collective-permute-start | bytes 3145736 | tf_op jit(solution)/shard_map/ppermute | solution.py:523
  244.2 53.5 %collective-permute-start.20 = (bf16[2,4,128,1024]{3,2,1,0:T(8,128)(2,1)}, bf16[2,4,128,1024]{3,2,1,0:T(8,128)(2,1)}, u32[]{:S(2)}, u32[]{:S(2)}) collective-permute-start(bf16[2,4,128,1024]{3,2,1,0:T(8,128)(2,1)} %pad_maximum_fusion.3), channel_id=1, source_target_pairs={{0,16},{1,17},{2,18},{3,19},{4,12},{5,13},{6,14},{7,15},{8,24},{9,... | collective-permute-start | bytes 6291464 | tf_op jit(solution)/shard_map/ppermute | solution.py:523
  257.7 43.8 %all-to-all-start.1 = ((bf16[4,128,1024]{2,1,0:T(8,128)(2,1)}), bf16[4,128,1024]{2,1,0:T(8,128)(2,1)}, u32[]{:S(2)}, u32[]{:S(2)}) async-start(bf16[4,128,1024]{2,1,0:T(8,128)(2,1)} %add_convert_fusion.1), calls=%async_computation.1 | async-start | bytes 2097152 | tf_op jit(solution)/shard_map/all_to_all | solution.py:576
  261.9 147.0 %reduce-scatter.5.cloned.1.call-start = ((), (), s32[]{:S(2)}) async-start(), calls=%async_computation.6 | async-start | bytes 2621440 | tf_op jit(solution)/shard_map/reduce_scatter | solution.py:788
  265.8 37.2 %collective-permute-start.19 = (bf16[2,256,2048]{2,1,0:T(8,128)(2,1)S(1)}, bf16[2,256,2048]{2,1,0:T(8,128)(2,1)}, u32[]{:S(2)}, u32[]{:S(2)}) collective-permute-start(bf16[2,256,2048]{2,1,0:T(8,128)(2,1)S(1)} %shard_map.245.refs_0_), channel_id=1, source_target_pairs={{0,8},{1,9},{2,10},{3,11},{4,20},{5,21},{6,22},{7,23},{8,0},{9,1},... | collective-permute-start | bytes 6291464 | tf_op jit(solution)/shard_map/ppermute | solution.py:523
  277.0 27.4 %collective-permute-start.18 = (bf16[512,2048]{1,0:T(8,128)(2,1)}, bf16[512,2048]{1,0:T(8,128)(2,1)}, u32[]{:S(2)}, u32[]{:S(2)}) collective-permute-start(bf16[512,2048]{1,0:T(8,128)(2,1)} %get-tuple-element.213), channel_id=1, source_target_pairs={{0,4},{1,5},{2,6},{3,7},{4,0},{5,1},{6,2},{7,3},{8,12},{9,13},{10,... | collective-permute-start | bytes 6291464 | tf_op jit(solution)/shard_map/ppermute | solution.py:523
  316.4 26.3 %collective-permute-start.22 = (bf16[4,128,1024]{2,1,0:T(8,128)(2,1)}, bf16[4,128,1024]{2,1,0:T(8,128)(2,1)S(1)}, u32[]{:S(2)}, u32[]{:S(2)}) collective-permute-start(bf16[4,128,1024]{2,1,0:T(8,128)(2,1)} %get-tuple-element.231), channel_id=1, source_target_pairs={{0,8},{1,9},{2,10},{3,11},{4,20},{5,21},{6,22},{7,23},{8,0},{9,1},... | collective-permute-start | bytes 3145736 | tf_op jit(solution)/shard_map/ppermute | solution.py:523
  316.9 32.5 %collective-permute-start.24 = (bf16[2,256,2048]{2,1,0:T(8,128)(2,1)S(1)}, bf16[2,256,2048]{2,1,0:T(8,128)(2,1)}, u32[]{:S(2)}, u32[]{:S(2)}) collective-permute-start(bf16[2,256,2048]{2,1,0:T(8,128)(2,1)S(1)} %shard_map.245.refs_0_), channel_id=1, source_target_pairs={{0,4},{1,5},{2,6},{3,7},{4,0},{5,1},{6,2},{7,3},{8,12},{9,13},{10,... | collective-permute-start | bytes 6291464 | tf_op jit(solution)/shard_map/ppermute | solution.py:523
  316.9 32.5 %collective-permute-start.25 = (bf16[2,256,2048]{2,1,0:T(8,128)(2,1)}, bf16[2,256,2048]{2,1,0:T(8,128)(2,1)}, u32[]{:S(2)}, u32[]{:S(2)}) collective-permute-start(bf16[2,256,2048]{2,1,0:T(8,128)(2,1)} %collective-permute-done.19.refs_1_), channel_id=1, source_target_pairs={{0,4},{1,5},{2,6},{3,7},{4,0},{5,1},{6,2},{7,3},{8,12},{9,13},{10,... | collective-permute-start | bytes 6291464 | tf_op jit(solution)/shard_map/ppermute | solution.py:523
  341.5 26.4 %collective-permute-start.26 = (bf16[2,128,4096]{2,1,0:T(8,128)(2,1)}, bf16[2,128,4096]{2,1,0:T(8,128)(2,1)}, u32[]{:S(2)}, u32[]{:S(2)}) collective-permute-start(bf16[2,128,4096]{2,1,0:T(8,128)(2,1)} %shard_map.250.m0_ref), channel_id=1, source_target_pairs={{0,8},{1,9},{2,10},{3,11},{4,20},{5,21},{6,22},{7,23},{8,0},{9,1},... | collective-permute-start | bytes 6291464 | tf_op jit(solution)/shard_map/ppermute | solution.py:523
  344.3 32.7 %all-to-all-start.2 = ((bf16[4,144,768]{2,1,0:T(8,128)(2,1)}), bf16[4,144,768]{2,1,0:T(8,128)(2,1)}, u32[]{:S(2)}, u32[]{:S(2)}) async-start(bf16[4,144,768]{2,1,0:T(8,128)(2,1)} %pad_maximum_fusion.5), calls=%async_computation.4 | async-start | bytes 1769472 | tf_op jit(solution)/shard_map/all_to_all | solution.py:576
  348.5 75.7 %reduce-scatter.3.cloned.1.call-start = ((), (), s32[]{:S(2)}) async-start(), calls=%async_computation.5 | async-start | bytes 2621440 | tf_op jit(solution)/shard_map/reduce_scatter | solution.py:788
  379.0 26.3 %collective-permute-start.27 = (bf16[128,4096]{1,0:T(8,128)(2,1)S(1)}, bf16[128,4096]{1,0:T(8,128)(2,1)S(1)}, u32[]{:S(2)}, u32[]{:S(2)}) collective-permute-start(bf16[128,4096]{1,0:T(8,128)(2,1)S(1)} %bitcast.167), channel_id=1, source_target_pairs={{0,16},{1,17},{2,18},{3,19},{4,12},{5,13},{6,14},{7,15},{8,24},{9,... | collective-permute-start | bytes 3145736 | tf_op jit(solution)/shard_map/ppermute | solution.py:523
  (75 other events, 802.7 us)
Sparse Core Ops, SparseCore 0:
  314.9 50.1 reduce-scatter.4
  367.5 44.3 reduce-scatter.2

commit v4 on v3

--- a/solution.py
+++ b/solution.py
@@ -870,10 +870,10 @@
         own, other = step((mixed_first[None], second_other[None]))
         placed = tie(place_mixed(net, own, other, 1, factor, placed))
         step(None, placed)
+        sums = net.plane_sum(tie(step(sums)), 1)
         own, other = step((mixed_second[None], first_other[None]))
         placed = tie(place_mixed(net, own, other, 2, factor, placed))
         step(None, placed)
-        sums = net.plane_sum(tie(step(sums)), 1)
         mixed_last = tie(step(mixed_last))
         sums_came = net.move(tie(sums, mixed_last), dc=1)
         last_other = net.move(mixed_last, dc=1)

time: 449 us -> 448 us (level)
  transfers between devices with their start and end apart: 44 -> 44, of which waited for: 18 -> 17; matrix products, arithmetic and copies ran while one was open for 17% -> 17% of each run, Pallas kernels for 23% -> 23%
where the time goes in v4:
time: 448 us; the launch traced here: 441 us
  waiting for transfers between devices  148 us (33%)
  Pallas kernels  117 us (26%)
  starting transfers between devices  43.4 us (10%)
  other arithmetic  42.2 us (9%)
  matrix products  36.3 us (8%)
  local copies, waits for them, and re-layouts  32.7 us (7%)
  between operations  21.2 us (5%)
    ppermute x39, waiting for transfers between devices, move(): return lax.ppermute(x, AXES, pairs)  109 us
    all_to_all x3, waiting for transfers between devices, swap(): return lax.all_to_all(tie(x, *after), 'shard', 0, 0, tiled=True)  38.9 us
    ppermute x39, starting transfers between devices, move(): return lax.ppermute(x, AXES, pairs)  30.4 us
    unnamed x117, local copies, waits for them, and re-layouts  17.8 us
    pallas_call x4, Pallas kernels, place_mixed(): call(kernel, (count, planes), [pl.BlockSpec((None, part, columns), lambda...  17.2 us
    dot_general x4, matrix products, local(): jnp.einsum('td,te->de', x, y, preferred_element_type=f32).astype(bf16)  14.8 us
    pallas_call x1, Pallas kernels, place_columns(): call(kernel, (J, 2), [pl.BlockSpec((None, high, columns), lambda i, h, sp...  14.2 us
    pallas_call x2, Pallas kernels, norm(): call(kernel, (len(arrays),), [line, line] + [pl.BlockSpec(x.shape, lambda...  13.4 us
  transfers between devices with their start and end apart: 44, of which 17 were waited for; matrix products, arithmetic and copies ran while one was open for 17% of the time, Pallas kernels for 23%

profile of v4, /device:TPU:0, one launch (start us, length us, event | category | flops | bytes accessed | tf_op | source)
XLA Modules:
  0.0 441.3 jit_solution(16177043281280932341)
XLA Ops:
  43.9 5.8 %collective-permute-done.refs_2_ = bf16[256,2048]{1,0:T(8,128)(2,1)} collective-permute-done((bf16[256,2048]{1,0:T(8,128)(2,1)S(1)}, bf16[256,2048]{1,0:T(8,128)(2,1)}, u32[]{:S(2)}, u32[]{:S(2)}) %collective-permute-start) | collective-permute-done | bytes 1048608 | tf_op jit(solution)/shard_map/ppermute | solution.py:523
  57.0 29.8 %all-to-all-done = bf16[4,128,1792]{2,1,0:T(8,128)(2,1)} async-done(((bf16[4,128,1792]{2,1,0:T(8,128)(2,1)}), bf16[4,128,1792]{2,1,0:T(8,128)(2,1)}, u32[]{:S(2)}, u32[]{:S(2)}) %all-to-all-start) | async-done | bytes 1835040 | tf_op jit(solution)/shard_map/all_to_all | solution.py:576
  89.8 16.8 %collective-permute-done.8.refs_1_ = bf16[1,384,1792]{2,1,0:T(8,128)(2,1)S(1)} collective-permute-done((bf16[1,384,1792]{2,1,0:T(8,128)(2,1)S(1)}, bf16[1,384,1792]{2,1,0:T(8,128)(2,1)S(1)}, u32[]{:S(2)}, u32[]{:S(2)}) %collective-permute-start.8) | collective-permute-done | bytes 1376288 | tf_op jit(solution)/shard_map/ppermute | solution.py:523
  109.8 6.9 %collective-permute-done.7.refs_4_ = bf16[256,2048]{1,0:T(8,128)(2,1)S(1)} collective-permute-done((bf16[256,2048]{1,0:T(8,128)(2,1)}, bf16[256,2048]{1,0:T(8,128)(2,1)S(1)}, u32[]{:S(2)}, u32[]{:S(2)}) %collective-permute-start.7) | collective-permute-done | bytes 1048608 | tf_op jit(solution)/shard_map/ppermute | solution.py:523
  120.3 7.8 %shard_map.240 = (bf16[1024,2048]{1,0:T(8,128)(2,1)}, bf16[1024,2048]{1,0:T(8,128)(2,1)}, bf16[1024,2048]{1,0:T(8,128)(2,1)}, f32[1024,128]{1,0:T(8,128)S(1)}, f32[1024,128]{1,0:T(8,128)S(1)}) custom-call(s32[6]{0:T(128)S(1)} %copy-done.31, f32[1,2048]{1,0:T(1,128)S(1)} %bitcast.180, f32[1,2048]{1,0:T(1,128)S(1)} %bitcast.184, ...), custom_call_target="tpu_custom_call" | custom-call | tf_op jit(solution)/shard_map/pallas_call | solution.py:238
  132.9 11.4 %collective-permute-done.9.refs_0_ = bf16[256,2048]{1,0:T(8,128)(2,1)} collective-permute-done((bf16[256,2048]{1,0:T(8,128)(2,1)S(1)}, bf16[256,2048]{1,0:T(8,128)(2,1)}, u32[]{:S(2)}, u32[]{:S(2)}) %collective-permute-start.9) | collective-permute-done | bytes 1048608 | tf_op jit(solution)/shard_map/ppermute | solution.py:523
  148.5 5.7 %shard_map.243 = (bf16[1024,2048]{1,0:T(8,128)(2,1)}, bf16[1024,2048]{1,0:T(8,128)(2,1)}, bf16[1024,2048]{1,0:T(8,128)(2,1)}, f32[1024,128]{1,0:T(8,128)S(1)}, f32[1024,128]{1,0:T(8,128)S(1)}) custom-call(s32[2]{0:T(128)S(1)} %copy-done.30, f32[1,2048]{1,0:T(1,128)S(1)} %bitcast.181, ...), custom_call_target="tpu_custom_call", output_to_operand_aliasing={{0}: (5, {}), {1}: (6, {}), {2}: (7, {}), {3}: (8, {}), {4}... | custom-call | tf_op jit(solution)/shard_map/pallas_call | solution.py:238
  154.2 7.7 %multiply_convert_fusion = (bf16[1024,1024]{1,0:T(8,128)(2,1)S(1)}, f32[1024,1024]{1,0:T(8,128)S(1)}) fusion(f32[1024]{0:T(1024)S(1)} %dynamic_slice.74, bf16[1024,2048]{1,0:T(8,128)(2,1)} %get-tuple-element.202, bf16[2048,1024]{1,0:T(8,128)(2,1)S(1)} %bitcast.197), kind=kOutput, calls=%fused_computation.12 | convolution fusion | flops 4305453056 | bytes 14684160 | tf_op jit(solution)/shard_map/dot_general | solution.py:705
  171.5 7.3 %fusion.6.hidden_ref = bf16[1024,1024]{1,0:T(8,128)(2,1)S(1)} fusion(f32[1024,1024]{1,0:T(8,128)S(1)} %get-tuple-element.315, f32[1024]{0:T(1024)S(1)} %dynamic_slice.74, bf16[1024,2048]{1,0:T(8,128)(2,1)S(1)} %copy-done.35, bf16[1024,2048]{1,0:T(8,128)(2,1)S(1)} %copy-done.34), kind=kOutput, calls=%fused_computation.9 | convolution fusion | flops 4316987392 | bytes 14684160 | tf_op jit(solution)/shard_map/td,fd->tf/dot_general | solution.py:751
  187.9 8.5 %collective-permute-done.13 = bf16[2,1,256,2048]{3,2,1,0:T(8,128)(2,1)} collective-permute-done((bf16[2,1,256,2048]{3,2,1,0:T(8,128)(2,1)}, bf16[2,1,256,2048]{3,2,1,0:T(8,128)(2,1)}, u32[]{:S(2)}, u32[]{:S(2)}) %collective-permute-start.13) | collective-permute-done | bytes 2097184 | tf_op jit(solution)/shard_map/ppermute | solution.py:523
  201.3 5.1 %broadcast_add_fusion.mixed_ref = f32[1024,768]{1,0:T(8,128)} fusion(f32[768]{0:T(1024)S(1)} %reshape.342, bf16[1024,2048]{1,0:T(8,128)(2,1)S(1)} %copy-done.46, bf16[2048,768]{1,0:T(8,128)(2,1)S(1)} %bitcast.164), kind=kOutput, calls=%fused_computation.34 | convolution fusion | flops 3222011904 | bytes 10488832 | tf_op jit(solution)/shard_map/dot_general | solution.py:757
  207.9 12.4 %shard_map.244 = (bf16[1024,256]{1,0:T(8,128)(2,1)S(1)}, bf16[1024,768]{1,0:T(8,128)(2,1)S(1)}) custom-call(s32[1024,128]{1,0:T(8,128)S(1)} %copy-done.27, f32[1024,128]{1,0:T(8,128)S(1)} %copy-done.26, f32[1024,128]{1,0:T(8,128)S(1)} %copy-done.25, f32[1024,128]{1,0:T(8,128)S(1)} %copy-done.24, f32[1024,768]{1,0:T(8,128)} %broadcast_add_fusion.mixed_ref, ...), custom_call_target="tpu_custom_call" | custom-call | flops 2000000000 | tf_op jit(solution)/shard_map/pallas_call | solution.py:94
  220.3 9.7 %collective-permute-done.15 = bf16[2,4,128,1024]{3,2,1,0:T(8,128)(2,1)} collective-permute-done((bf16[2,4,128,1024]{3,2,1,0:T(8,128)(2,1)}, bf16[2,4,128,1024]{3,2,1,0:T(8,128)(2,1)}, u32[]{:S(2)}, u32[]{:S(2)}) %collective-permute-start.15) | collective-permute-done | bytes 2097184 | tf_op jit(solution)/shard_map/ppermute | solution.py:523
  245.6 11.6 %collective-permute-done.17 = bf16[4,128,1024]{2,1,0:T(8,128)(2,1)S(1)} collective-permute-done((bf16[4,128,1024]{2,1,0:T(8,128)(2,1)S(1)}, bf16[4,128,1024]{2,1,0:T(8,128)(2,1)S(1)}, u32[]{:S(2)}, u32[]{:S(2)}) %collective-permute-start.17) | collective-permute-done | bytes 1048608 | tf_op jit(solution)/shard_map/ppermute | solution.py:523
  268.0 9.9 %shard_map.246 = (f32[512,2048]{1,0:T(8,128)}, bf16[512,2048]{1,0:T(8,128)(2,1)}) custom-call(bf16[1024,256]{1,0:T(8,128)(2,1)S(1)} %copy-done.29, bf16[256,2048]{1,0:T(8,128)(2,1)S(1)} %copy-done.7, bf16[1024,1024]{1,0:T(8,128)(2,1)S(1)} %copy-done.19, bf16[1024,2048]{1,0:T(8,128)(2,1)} %constant_dynamic-slice_fusion.6.fc2_ref), custom_call_target="tpu_custom_call" | custom-call | flops 1666666624 | tf_op jit(solution)/shard_map/pallas_call | solution.py:325
  277.9 13.3 %shard_map.247 = (f32[512,2048]{1,0:T(8,128)}, bf16[512,2048]{1,0:T(8,128)(2,1)}, f32[8,2048]{1,0:T(8,128)S(1)}) custom-call(bf16[1024,1024]{1,0:T(8,128)(2,1)} %copy-done.38, bf16[2048,1024]{1,0:T(8,128)(2,1)} %bitcast.196, bf16[1024,768]{1,0:T(8,128)(2,1)S(1)} %copy-done.5, bf16[2048,768]{1,0:T(8,128)(2,1)} %bitcast.165, ...), custom_call_target="tpu_custom_call" | custom-call | flops 2333333248 | tf_op jit(solution)/shard_map/pallas_call | solution.py:355
  305.3 5.2 %shard_map.248 = bf16[4,128,2048]{2,1,0:T(8,128)(2,1)} custom-call(s32[4]{0:T(128)S(1)} %and_select_fusion.2.order_ref, f32[512,2048]{1,0:T(8,128)} %get-tuple-element.233.mine_ref, bf16[512,2048]{1,0:T(8,128)(2,1)} %collective-permute-done.18.came_ref), custom_call_target="tpu_custom_call" | custom-call | tf_op jit(solution)/shard_map/pallas_call | solution.py:303
  310.5 5.2 %shard_map.249 = bf16[4,128,2048]{2,1,0:T(8,128)(2,1)} custom-call(s32[4]{0:T(128)S(1)} %and_select_fusion.2.order_ref, f32[512,2048]{1,0:T(8,128)} %get-tuple-element.237.mine_ref, bf16[512,2048]{1,0:T(8,128)(2,1)} %collective-permute-done.21.came_ref), custom_call_target="tpu_custom_call" | custom-call | tf_op jit(solution)/shard_map/pallas_call | solution.py:303
  318.3 22.7 %collective-permute-done.23 = bf16[128,4096]{1,0:T(8,128)(2,1)S(1)} collective-permute-done((bf16[128,4096]{1,0:T(8,128)(2,1)S(1)}, bf16[128,4096]{1,0:T(8,128)(2,1)S(1)}, u32[]{:S(2)}, u32[]{:S(2)}) %collective-permute-start.23) | collective-permute-done | bytes 1048608 | tf_op jit(solution)/shard_map/ppermute | solution.py:523
  350.3 11.9 %shard_map.251 = f32[2048,2048]{1,0:T(8,128)} custom-call(s32[8]{0:T(128)S(1)} %pad_add_fusion.4.spots_ref, bf16[2,256,2048]{2,1,0:T(8,128)(2,1)S(1)} %shard_map.245.refs_0_, bf16[2,256,2048]{2,1,0:T(8,128)(2,1)} %collective-permute-done.19.refs_1_, bf16[2,256,2048]{2,1,0:T(8,128)(2,1)} %collective-permute-done.24.refs_2_, ...), custom_call_target="tpu_custom_call" | custom-call | tf_op jit(solution)/shard_map/pallas_call | solution.py:490
  362.3 6.5 %collective-permute-done.26.m1_ref = bf16[2,128,4096]{2,1,0:T(8,128)(2,1)} collective-permute-done((bf16[2,128,4096]{2,1,0:T(8,128)(2,1)}, bf16[2,128,4096]{2,1,0:T(8,128)(2,1)}, u32[]{:S(2)}, u32[]{:S(2)}) %collective-permute-start.26) | collective-permute-done | bytes 2097184 | tf_op jit(solution)/shard_map/ppermute | solution.py:523
  368.8 9.1 %all-to-all-done.2 = bf16[4,144,768]{2,1,0:T(8,128)(2,1)} async-done(((bf16[4,144,768]{2,1,0:T(8,128)(2,1)}), bf16[4,144,768]{2,1,0:T(8,128)(2,1)}, u32[]{:S(2)}, u32[]{:S(2)}) %all-to-all-start.2) | async-done | bytes 884768 | tf_op jit(solution)/shard_map/all_to_all | solution.py:576
  385.4 14.2 %shard_map.252 = f32[512,8192]{1,0:T(8,128)} custom-call(s32[6]{0:T(128)S(1)} %concatenate.73.spots_ref, bf16[2,128,4096]{2,1,0:T(8,128)(2,1)} %shard_map.250.m0_ref, bf16[2,128,4096]{2,1,0:T(8,128)(2,1)} %collective-permute-done.26.m1_ref, bf16[2,128,4096]{2,1,0:T(8,128)(2,1)} %collective-permute-done.28.o0_ref, ...), custom_call_target="tpu_custom_call" | custom-call | tf_op jit(solution)/shard_map/pallas_call | solution.py:400
  411.7 4.9 %shard_map.254 = (f32[512,6144]{1,0:T(8,128)}, f32[512,2048]{1,0:T(8,128)}) custom-call(s32[3]{0:T(128)S(1)} %get-tuple-element.323.spots_ref, bf16[1,128,4096]{2,1,0:T(8,128)(2,1)S(1)} %bitcast.176, bf16[1,128,4096]{2,1,0:T(8,128)(2,1)} %bitcast.66.other_ref, f32[512,6144]{1,0:T(8,128)} %get-tuple-element.260.refs_0_, ...), custom_call_target="tpu_custom_call", output_to_operand_aliasing={{0}: (3, {}), {1}: (4, {})} | custom-call | tf_op jit(solution)/shard_map/pallas_call | solution.py:452
  (320 shorter events, 170.7 us)
Async XLA Ops:
  13.2 30.0 %collective-permute-start.1 = (bf16[5760]{0:T(1024)(128)(2,1)S(1)}, bf16[5760]{0:T(1024)(128)(2,1)S(1)}, u32[]{:S(2)}, u32[]{:S(2)}) collective-permute-start(bf16[5760]{0:T(1024)(128)(2,1)S(1)} %dynamic-update-slice.6), channel_id=1, source_target_pairs={{0,1},{1,2},{2,3},{3,0},{4,5},{5,6},{6,7},{7,4},{8,9},{9,10},{10,1... | collective-permute-start | bytes 34568 | tf_op jit(solution)/shard_map/ppermute | solution.py:523
  16.2 26.9 %collective-permute-start.2 = (bf16[5760]{0:T(1024)(128)(2,1)S(1)}, bf16[5760]{0:T(1024)(128)(2,1)S(1)}, u32[]{:S(2)}, u32[]{:S(2)}) collective-permute-start(bf16[5760]{0:T(1024)(128)(2,1)S(1)} %dynamic-update-slice.6), channel_id=1, source_target_pairs={{0,2},{1,3},{2,0},{3,1},{4,6},{5,7},{6,4},{7,5},{8,10},{9,11},{10,... | collective-permute-start | bytes 34568 | tf_op jit(solution)/shard_map/ppermute | solution.py:523
  21.4 28.2 %collective-permute-start = (bf16[256,2048]{1,0:T(8,128)(2,1)S(1)}, bf16[256,2048]{1,0:T(8,128)(2,1)}, u32[]{:S(2)}, u32[]{:S(2)}) collective-permute-start(bf16[256,2048]{1,0:T(8,128)(2,1)S(1)} %pad_maximum_fusion.4.refs_0_), channel_id=1, source_target_pairs={{0,1},{1,2},{2,3},{3,0},{4,5},{5,6},{6,7},{7,4},{8,9},{9,10},{10,1... | collective-permute-start | bytes 3145736 | tf_op jit(solution)/shard_map/ppermute | solution.py:523
  26.4 60.4 %all-to-all-start = ((bf16[4,128,1792]{2,1,0:T(8,128)(2,1)}), bf16[4,128,1792]{2,1,0:T(8,128)(2,1)}, u32[]{:S(2)}, u32[]{:S(2)}) async-start(bf16[4,128,1792]{2,1,0:T(8,128)(2,1)} %copy-done.3), calls=%async_computation | async-start | bytes 3670016 | tf_op jit(solution)/shard_map/all_to_all | solution.py:576
  89.8 26.8 %collective-permute-start.7 = (bf16[256,2048]{1,0:T(8,128)(2,1)}, bf16[256,2048]{1,0:T(8,128)(2,1)S(1)}, u32[]{:S(2)}, u32[]{:S(2)}) collective-permute-start(bf16[256,2048]{1,0:T(8,128)(2,1)} %collective-permute-done.refs_2_), channel_id=1, source_target_pairs={{0,1},{1,2},{2,3},{3,0},{4,5},{5,6},{6,7},{7,4},{8,9},{9,10},{10,1... | collective-permute-start | bytes 3145736 | tf_op jit(solution)/shard_map/ppermute | solution.py:523
  108.3 36.1 %collective-permute-start.12 = (bf16[2,384,1792]{2,1,0:T(8,128)(2,1)}, bf16[2,384,1792]{2,1,0:T(8,128)(2,1)}, u32[]{:S(2)}, u32[]{:S(2)}) collective-permute-start(bf16[2,384,1792]{2,1,0:T(8,128)(2,1)} %shard_map.239), channel_id=1, source_target_pairs={{0,8},{1,9},{2,10},{3,11},{4,20},{5,21},{6,22},{7,23},{8,0},{9,1},... | collective-permute-start | bytes 8257544 | tf_op jit(solution)/shard_map/ppermute | solution.py:523
  116.6 27.7 %collective-permute-start.9 = (bf16[256,2048]{1,0:T(8,128)(2,1)S(1)}, bf16[256,2048]{1,0:T(8,128)(2,1)}, u32[]{:S(2)}, u32[]{:S(2)}) collective-permute-start(bf16[256,2048]{1,0:T(8,128)(2,1)S(1)} %collective-permute-done.7.refs_4_), channel_id=1, source_target_pairs={{0,1},{1,2},{2,3},{3,0},{4,5},{5,6},{6,7},{7,4},{8,9},{9,10},{10,1... | collective-permute-start | bytes 3145736 | tf_op jit(solution)/shard_map/ppermute | solution.py:523
  170.0 26.4 %collective-permute-start.13 = (bf16[2,1,256,2048]{3,2,1,0:T(8,128)(2,1)}, bf16[2,1,256,2048]{3,2,1,0:T(8,128)(2,1)}, u32[]{:S(2)}, u32[]{:S(2)}) collective-permute-start(bf16[2,1,256,2048]{3,2,1,0:T(8,128)(2,1)} %pad_maximum_fusion.1), channel_id=1, source_target_pairs={{0,16},{1,17},{2,18},{3,19},{4,12},{5,13},{6,14},{7,15},{8,24},{9,... | collective-permute-start | bytes 6291464 | tf_op jit(solution)/shard_map/ppermute | solution.py:523
  186.6 43.5 %collective-permute-start.15 = (bf16[2,4,128,1024]{3,2,1,0:T(8,128)(2,1)}, bf16[2,4,128,1024]{3,2,1,0:T(8,128)(2,1)}, u32[]{:S(2)}, u32[]{:S(2)}) collective-permute-start(bf16[2,4,128,1024]{3,2,1,0:T(8,128)(2,1)} %pad_maximum_fusion.2), channel_id=1, source_target_pairs={{0,16},{1,17},{2,18},{3,19},{4,12},{5,13},{6,14},{7,15},{8,24},{9,... | collective-permute-start | bytes 6291464 | tf_op jit(solution)/shard_map/ppermute | solution.py:523
  200.7 32.6 %collective-permute-start.14 = (bf16[1,256,2048]{2,1,0:T(8,128)(2,1)}, bf16[1,256,2048]{2,1,0:T(8,128)(2,1)}, u32[]{:S(2)}, u32[]{:S(2)}) collective-permute-start(bf16[1,256,2048]{2,1,0:T(8,128)(2,1)} %get-tuple-element.191), channel_id=1, source_target_pairs={{0,8},{1,9},{2,10},{3,11},{4,20},{5,21},{6,22},{7,23},{8,0},{9,1},... | collective-permute-start | bytes 3145736 | tf_op jit(solution)/shard_map/ppermute | solution.py:523
  235.0 27.9 %collective-permute-start.16 = (bf16[256,2048]{1,0:T(8,128)(2,1)S(1)}, bf16[256,2048]{1,0:T(8,128)(2,1)S(1)}, u32[]{:S(2)}, u32[]{:S(2)}) collective-permute-start(bf16[256,2048]{1,0:T(8,128)(2,1)S(1)} %bitcast.170), channel_id=1, source_target_pairs={{0,16},{1,17},{2,18},{3,19},{4,12},{5,13},{6,14},{7,15},{8,24},{9,... | collective-permute-start | bytes 3145736 | tf_op jit(solution)/shard_map/ppermute | solution.py:523
  245.1 53.5 %collective-permute-start.20 = (bf16[2,4,128,1024]{3,2,1,0:T(8,128)(2,1)}, bf16[2,4,128,1024]{3,2,1,0:T(8,128)(2,1)}, u32[]{:S(2)}, u32[]{:S(2)}) collective-permute-start(bf16[2,4,128,1024]{3,2,1,0:T(8,128)(2,1)} %pad_maximum_fusion.3), channel_id=1, source_target_pairs={{0,16},{1,17},{2,18},{3,19},{4,12},{5,13},{6,14},{7,15},{8,24},{9,... | collective-permute-start | bytes 6291464 | tf_op jit(solution)/shard_map/ppermute | solution.py:523
  258.6 43.8 %all-to-all-start.1 = ((bf16[4,128,1024]{2,1,0:T(8,128)(2,1)}), bf16[4,128,1024]{2,1,0:T(8,128)(2,1)}, u32[]{:S(2)}, u32[]{:S(2)}) async-start(bf16[4,128,1024]{2,1,0:T(8,128)(2,1)} %add_convert_fusion.1), calls=%async_computation.1 | async-start | bytes 2097152 | tf_op jit(solution)/shard_map/all_to_all | solution.py:576
  262.8 147.3 %reduce-scatter.5.cloned.1.call-start = ((), (), s32[]{:S(2)}) async-start(), calls=%async_computation.6 | async-start | bytes 2621440 | tf_op jit(solution)/shard_map/reduce_scatter | solution.py:788
  266.7 37.2 %collective-permute-start.19 = (bf16[2,256,2048]{2,1,0:T(8,128)(2,1)S(1)}, bf16[2,256,2048]{2,1,0:T(8,128)(2,1)}, u32[]{:S(2)}, u32[]{:S(2)}) collective-permute-start(bf16[2,256,2048]{2,1,0:T(8,128)(2,1)S(1)} %shard_map.245.refs_0_), channel_id=1, source_target_pairs={{0,8},{1,9},{2,10},{3,11},{4,20},{5,21},{6,22},{7,23},{8,0},{9,1},... | collective-permute-start | bytes 6291464 | tf_op jit(solution)/shard_map/ppermute | solution.py:523
  277.9 27.4 %collective-permute-start.18 = (bf16[512,2048]{1,0:T(8,128)(2,1)}, bf16[512,2048]{1,0:T(8,128)(2,1)}, u32[]{:S(2)}, u32[]{:S(2)}) collective-permute-start(bf16[512,2048]{1,0:T(8,128)(2,1)} %get-tuple-element.213), channel_id=1, source_target_pairs={{0,4},{1,5},{2,6},{3,7},{4,0},{5,1},{6,2},{7,3},{8,12},{9,13},{10,... | collective-permute-start | bytes 6291464 | tf_op jit(solution)/shard_map/ppermute | solution.py:523
  315.7 25.3 %collective-permute-start.23 = (bf16[128,4096]{1,0:T(8,128)(2,1)S(1)}, bf16[128,4096]{1,0:T(8,128)(2,1)S(1)}, u32[]{:S(2)}, u32[]{:S(2)}) collective-permute-start(bf16[128,4096]{1,0:T(8,128)(2,1)S(1)} %bitcast.171), channel_id=1, source_target_pairs={{0,16},{1,17},{2,18},{3,19},{4,12},{5,13},{6,14},{7,15},{8,24},{9,... | collective-permute-start | bytes 3145736 | tf_op jit(solution)/shard_map/ppermute | solution.py:523
  317.3 26.3 %collective-permute-start.22 = (bf16[4,128,1024]{2,1,0:T(8,128)(2,1)}, bf16[4,128,1024]{2,1,0:T(8,128)(2,1)S(1)}, u32[]{:S(2)}, u32[]{:S(2)}) collective-permute-start(bf16[4,128,1024]{2,1,0:T(8,128)(2,1)} %get-tuple-element.231), channel_id=1, source_target_pairs={{0,8},{1,9},{2,10},{3,11},{4,20},{5,21},{6,22},{7,23},{8,0},{9,1},... | collective-permute-start | bytes 3145736 | tf_op jit(solution)/shard_map/ppermute | solution.py:523
  317.8 32.5 %collective-permute-start.24 = (bf16[2,256,2048]{2,1,0:T(8,128)(2,1)S(1)}, bf16[2,256,2048]{2,1,0:T(8,128)(2,1)}, u32[]{:S(2)}, u32[]{:S(2)}) collective-permute-start(bf16[2,256,2048]{2,1,0:T(8,128)(2,1)S(1)} %shard_map.245.refs_0_), channel_id=1, source_target_pairs={{0,4},{1,5},{2,6},{3,7},{4,0},{5,1},{6,2},{7,3},{8,12},{9,13},{10,... | collective-permute-start | bytes 6291464 | tf_op jit(solution)/shard_map/ppermute | solution.py:523
  317.8 32.5 %collective-permute-start.25 = (bf16[2,256,2048]{2,1,0:T(8,128)(2,1)}, bf16[2,256,2048]{2,1,0:T(8,128)(2,1)}, u32[]{:S(2)}, u32[]{:S(2)}) collective-permute-start(bf16[2,256,2048]{2,1,0:T(8,128)(2,1)} %collective-permute-done.19.refs_1_), channel_id=1, source_target_pairs={{0,4},{1,5},{2,6},{3,7},{4,0},{5,1},{6,2},{7,3},{8,12},{9,13},{10,... | collective-permute-start | bytes 6291464 | tf_op jit(solution)/shard_map/ppermute | solution.py:523
  342.4 26.4 %collective-permute-start.26 = (bf16[2,128,4096]{2,1,0:T(8,128)(2,1)}, bf16[2,128,4096]{2,1,0:T(8,128)(2,1)}, u32[]{:S(2)}, u32[]{:S(2)}) collective-permute-start(bf16[2,128,4096]{2,1,0:T(8,128)(2,1)} %shard_map.250.m0_ref), channel_id=1, source_target_pairs={{0,8},{1,9},{2,10},{3,11},{4,20},{5,21},{6,22},{7,23},{8,0},{9,1},... | collective-permute-start | bytes 6291464 | tf_op jit(solution)/shard_map/ppermute | solution.py:523
  345.2 32.7 %all-to-all-start.2 = ((bf16[4,144,768]{2,1,0:T(8,128)(2,1)}), bf16[4,144,768]{2,1,0:T(8,128)(2,1)}, u32[]{:S(2)}, u32[]{:S(2)}) async-start(bf16[4,144,768]{2,1,0:T(8,128)(2,1)} %pad_maximum_fusion.5), calls=%async_computation.4 | async-start | bytes 1769472 | tf_op jit(solution)/shard_map/all_to_all | solution.py:576
  349.4 73.2 %reduce-scatter.3.cloned.1.call-start = ((), (), s32[]{:S(2)}) async-start(), calls=%async_computation.5 | async-start | bytes 2621440 | tf_op jit(solution)/shard_map/reduce_scatter | solution.py:788
  379.9 26.3 %collective-permute-start.27 = (bf16[128,4096]{1,0:T(8,128)(2,1)S(1)}, bf16[128,4096]{1,0:T(8,128)(2,1)S(1)}, u32[]{:S(2)}, u32[]{:S(2)}) collective-permute-start(bf16[128,4096]{1,0:T(8,128)(2,1)S(1)} %bitcast.167), channel_id=1, source_target_pairs={{0,16},{1,17},{2,18},{3,19},{4,12},{5,13},{6,14},{7,15},{8,24},{9,... | collective-permute-start | bytes 3145736 | tf_op jit(solution)/shard_map/ppermute | solution.py:523
  (75 other events, 805.4 us)
Sparse Core Ops, SparseCore 0:
  315.8 50.1 reduce-scatter.4
  368.4 44.3 reduce-scatter.2
